TPU v7x, 32 devices: a whole 2x2x4 slice. The times are simulated.
32 devices in a mesh: group: 2 (over y), clip: 8 (over z, x), micro: 2 (over core).
Axes of the slice: x: 2, y: 2, z: 4, core: 2. Of those that a mesh axis runs over, the one named last changes fastest.
Arguments:
- inputs: bfloat16 [2, 4, 8, 1568, 384], P('group', 'micro', 'clip'), may hold values from -6 to 6
- offsets: int32 [2], P('group'), may hold values from 0 to 2, as said below
- cotangent: bfloat16 [2, 4, 8, 392, 768], P('group', 'micro', 'clip'), may hold values from -6 to 6
- gain_attn1: float32 [384], replicated, may hold values from 0.1 to 1.9
- w_qkv1: bfloat16 [384, 1152], replicated, may hold values from -0.625 to 0.625
- w_proj1: bfloat16 [384, 384], replicated, may hold values from -0.15625 to 0.15625
- gain_mlp1: float32 [384], replicated, may hold values from 0.1 to 1.9
- w_fc1: bfloat16 [384, 1536], replicated, may hold values from -0.3125 to 0.3125
- w_out1: bfloat16 [1536, 384], replicated, may hold values from -0.21875 to 0.21875
- gain_attn2: float32 [384], replicated, may hold values from 0.1 to 1.9
- w_qkv2: bfloat16 [384, 2304], replicated, may hold values from -0.625 to 0.625
- w_proj2: bfloat16 [768, 768], replicated, may hold values from -0.109375 to 0.109375
- w_skip: bfloat16 [384, 768], replicated, may hold values from -0.625 to 0.625
- gain_mlp2: float32 [768], replicated, may hold values from 0.1 to 1.9
- w_fc2: bfloat16 [768, 3072], replicated, may hold values from -0.21875 to 0.21875
- w_out2: bfloat16 [3072, 768], replicated, may hold values from -0.15625 to 0.15625
Outputs:
- output: bfloat16 [2, 4, 8, 392, 768], P('group', 'micro', 'clip')
- input_grad: bfloat16 [2, 4, 8, 1568, 384], P('group', 'micro', 'clip')
- grad_gain_attn1: float32 [384], replicated
- grad_gain_mlp1: float32 [384], replicated
- grad_gain_attn2: float32 [384], replicated
- grad_gain_mlp2: float32 [768], replicated
- grad_w_qkv1: float32 [442368], P(('clip', 'micro'))
- grad_w_proj1: float32 [147456], P(('clip', 'micro'))
- grad_w_fc1: float32 [589824], P(('clip', 'micro'))
- grad_w_out1: float32 [589824], P(('clip', 'micro'))
- grad_w_qkv2: float32 [884736], P(('clip', 'micro'))
- grad_w_proj2: float32 [589824], P(('clip', 'micro'))
- grad_w_skip: float32 [294912], P(('clip', 'micro'))
- grad_w_fc2: float32 [2359296], P(('clip', 'micro'))
- grad_w_out2: float32 [2359296], P(('clip', 'micro'))
Inputs may be any that keep to these rules, and one draw needn't show every extreme that they name: Memory frames of index below offsets[g] are not attended by any clip of stride group g; no two stride groups have the same offset.
All inputs are finite; a program needn't handle non-finite values.
Results may differ from a plain program's by a relative error of at most 0.023.
Values may be sent and summed in bfloat16 or wider, within the bound.
A program may use at most 448 MiB of HBM per device.

v0:
```python
from functools import partial

import jax
import jax.numpy as jnp
from jax import lax
from jax.sharding import PartitionSpec as P

H1 = 4
H2 = 8
D1 = 384
D2 = 768
FR = 8
HT = 14
WD = 14
QT = 1568
PT = 392
MT = 196


epsilon = 1e-06


def from_behind(value, axis, steps):
    count = lax.axis_size(axis)
    first, last = (max(0, -steps), min(count, count - steps))
    return lax.ppermute(value, axis, [(source, source + steps) for source in range(first, last)])


def norm_forward(values, gain):
    center = values - jnp.mean(values, axis=-1, keepdims=True)
    scale_inv = lax.rsqrt(jnp.mean(center * center, axis=-1, keepdims=True) + epsilon)
    unit = center * scale_inv
    return (unit * gain, unit, scale_inv)


def norm_backward(grad_out, unit, scale_inv, gain):
    grad_unit = grad_out * gain
    grad_gain = jnp.sum(grad_out * unit, axis=(0, 1))
    centered = jnp.mean(grad_unit, axis=-1, keepdims=True)
    aligned = jnp.mean(grad_unit * unit, axis=-1, keepdims=True)
    return (scale_inv * (grad_unit - centered - unit * aligned), grad_gain)


def pool_space(values):
    width = values.shape[-1]
    lead = values.shape[:-2]
    frames = values.shape[-2] // (HT * WD)
    shaped = values.reshape(lead + (frames, HT // 2, 2, WD // 2, 2, width))
    return jnp.mean(shaped, axis=(-4, -2)).reshape(lead + (-1, width))


def spread_space(grads):
    width = grads.shape[-1]
    lead = grads.shape[:-2]
    frames = grads.shape[-2] // (HT // 2 * (WD // 2))
    shaped = grads.reshape(lead + (frames, HT // 2, 1, WD // 2, 1, width))
    wide = jnp.broadcast_to(shaped, lead + (frames, HT // 2, 2, WD // 2, 2, width)) * 0.25
    return wide.reshape(lead + (-1, width))


def pool_time(values):
    width = values.shape[-1]
    lead = values.shape[:-2]
    shaped = values.reshape(lead + (FR // 2, 2, -1, width))
    return jnp.mean(shaped, axis=-3).reshape(lead + (-1, width))


def spread_time(grads):
    width = grads.shape[-1]
    lead = grads.shape[:-2]
    shaped = grads.reshape(lead + (FR // 2, 1, -1, width))
    wide = jnp.broadcast_to(shaped, lead + (FR // 2, 2, shaped.shape[-2], width)) * 0.5
    return wide.reshape(lead + (-1, width))


def key_mask(clip, offset):
    frame = jnp.arange(MT, dtype=jnp.int32) // (HT // 2 * (WD // 2))
    later = frame >= offset
    own = jnp.ones((PT,), jnp.bool_)
    return jnp.concatenate([own, later & (clip >= 1), later & (clip >= 2)])


def masked_scores(queries, keys, valid, heads):
    count = queries.shape[0]
    head_size = queries.shape[1] // heads
    split_query = queries.reshape(count, heads, head_size)
    split_keys = keys.reshape(-1, heads, head_size)
    scores = jnp.einsum(
        "nhd,khd->hnk", split_query, split_keys, preferred_element_type=jnp.float32
    ) * head_size ** (-0.5)
    return (jnp.where(valid[None, None, :], scores, -1e30), split_query, split_keys)


def attend_forward(packed, valid, heads):
    queries, keys, values = packed
    count = queries.shape[0]
    head_size = queries.shape[1] // heads
    scores, split_query, split_keys = masked_scores(queries, keys, valid, heads)
    top = jnp.max(scores, axis=-1, keepdims=True)
    expo = jnp.exp(scores - top)
    total = jnp.sum(expo, axis=-1, keepdims=True)
    probs = (expo / total).astype(jnp.bfloat16)
    mixed = jnp.einsum(
        "hnk,khd->nhd",
        probs,
        values.reshape(-1, heads, head_size),
        preferred_element_type=jnp.float32,
    )
    return (mixed.reshape(count, -1), top + jnp.log(total))


def attend_backward(packed, valid, heads):
    queries, keys, values, summary, grad_mixed = packed
    count = queries.shape[0]
    head_size = queries.shape[1] // heads
    scale = head_size ** (-0.5)
    scores, split_query, split_keys = masked_scores(queries, keys, valid, heads)
    probs = jnp.exp(scores - summary)
    split_grad = grad_mixed.reshape(count, heads, head_size)
    split_values = values.reshape(-1, heads, head_size)
    grad_probs = jnp.einsum(
        "nhd,khd->hnk", split_grad, split_values, preferred_element_type=jnp.float32
    )
    delta = jnp.sum(grad_probs * probs, axis=-1, keepdims=True)
    grad_scores = (probs * (grad_probs - delta)).astype(jnp.bfloat16)
    grad_queries = (
        jnp.einsum("hnk,khd->nhd", grad_scores, split_keys, preferred_element_type=jnp.float32)
        * scale
    )
    grad_keys = (
        jnp.einsum("hnk,nhd->khd", grad_scores, split_query, preferred_element_type=jnp.float32)
        * scale
    )
    grad_values = jnp.einsum(
        "hnk,nhd->khd", probs.astype(jnp.bfloat16), split_grad, preferred_element_type=jnp.float32
    )
    return (
        grad_queries.reshape(count, -1),
        grad_keys.reshape(-1, queries.shape[1]),
        grad_values.reshape(-1, queries.shape[1]),
    )


def pass_memory(memory):
    near = from_behind((memory[0], memory[1]), "clip", 1)
    far = from_behind((memory[0], memory[1]), "clip", 2)
    return (near, far)


def return_memory(grad_near, grad_far):
    back_one = (
        from_behind(grad_near[0].astype(jnp.bfloat16), "clip", -1).astype(jnp.float32),
        from_behind(grad_near[1].astype(jnp.bfloat16), "clip", -1).astype(jnp.float32),
    )
    back_two = (
        from_behind(grad_far[0].astype(jnp.bfloat16), "clip", -2).astype(jnp.float32),
        from_behind(grad_far[1].astype(jnp.bfloat16), "clip", -2).astype(jnp.float32),
    )
    return (back_one[0] + back_two[0], back_one[1] + back_two[1])


def gelu_back(inner, grad):
    unused, pullback = jax.vjp(partial(jax.nn.gelu, approximate=False), inner)
    return pullback(grad)[0]


def matmul(left, right):
    return jnp.einsum("bnc,cf->bnf", left, right, preferred_element_type=jnp.float32)


def matmul_back(grad, right):
    return jnp.einsum("bnf,cf->bnc", grad, right, preferred_element_type=jnp.float32)


def weight_grad(left, grad):
    return jnp.einsum("bnc,bnf->cf", left, grad, preferred_element_type=jnp.float32)


def attention_forward(queries, keys, values, valid, heads):
    near, far = pass_memory(
        (
            pool_time(keys.astype(jnp.float32)).astype(jnp.bfloat16),
            pool_time(values.astype(jnp.float32)).astype(jnp.bfloat16),
        )
    )
    all_keys = jnp.concatenate([keys, near[0], far[0]], axis=1)
    all_values = jnp.concatenate([values, near[1], far[1]], axis=1)
    mixed, summary = lax.map(
        partial(attend_forward, valid=valid, heads=heads), (queries, all_keys, all_values)
    )
    return (mixed, summary, all_keys, all_values)


def attention_backward(queries, all_keys, all_values, summary, grad_z, valid, heads):
    grad_q, grad_k, grad_v = lax.map(
        partial(attend_backward, valid=valid, heads=heads),
        (queries, all_keys, all_values, summary, grad_z),
    )
    near = (grad_k[:, PT : PT + MT], grad_v[:, PT : PT + MT])
    far = (grad_k[:, PT + MT :], grad_v[:, PT + MT :])
    back_keys, back_values = return_memory(near, far)
    key_total = (grad_k[:, :PT] + spread_time(back_keys)).astype(jnp.bfloat16)
    value_total = (grad_v[:, :PT] + spread_time(back_values)).astype(jnp.bfloat16)
    query_total = (grad_z.astype(jnp.float32) + grad_q).astype(jnp.bfloat16)
    return (query_total, key_total, value_total)


def body(
    inputs,
    offsets,
    cotangent,
    gain_attn1,
    w_qkv1,
    w_proj1,
    gain_mlp1,
    w_fc1,
    w_out1,
    gain_attn2,
    w_qkv2,
    w_proj2,
    w_skip,
    gain_mlp2,
    w_fc2,
    w_out2,
):
    batch = inputs.shape[1]
    valid = key_mask(lax.axis_index("clip"), offsets[0])
    source = inputs.reshape(batch, QT, D1).astype(jnp.float32)
    normed_a, unit_a, inv_a = norm_forward(source, gain_attn1)
    normed_a = normed_a.astype(jnp.bfloat16)
    joined_a = matmul(normed_a, w_qkv1)
    query_a = joined_a[..., :D1].astype(jnp.bfloat16)
    key_a = pool_space(joined_a[..., D1 : 2 * D1]).astype(jnp.bfloat16)
    value_a = pool_space(joined_a[..., 2 * D1 :]).astype(jnp.bfloat16)
    mixed_a, summary_a, keys_a, values_a = attention_forward(query_a, key_a, value_a, valid, H1)
    joint_a = (mixed_a + query_a.astype(jnp.float32)).astype(jnp.bfloat16)
    hidden_a = source + matmul(joint_a, w_proj1)
    normed_b, unit_b, inv_b = norm_forward(hidden_a, gain_mlp1)
    normed_b = normed_b.astype(jnp.bfloat16)
    inner_b = matmul(normed_b, w_fc1)
    active_b = jax.nn.gelu(inner_b, approximate=False).astype(jnp.bfloat16)
    middle = hidden_a + matmul(active_b, w_out1)
    normed_c, unit_c, inv_c = norm_forward(middle, gain_attn2)
    normed_c = normed_c.astype(jnp.bfloat16)
    joined_c = matmul(normed_c, w_qkv2)
    query_c = pool_space(joined_c[..., :D2]).astype(jnp.bfloat16)
    key_c = pool_space(joined_c[..., D2 : 2 * D2]).astype(jnp.bfloat16)
    value_c = pool_space(joined_c[..., 2 * D2 :]).astype(jnp.bfloat16)
    pooled_c = pool_space(normed_c.astype(jnp.float32)).astype(jnp.bfloat16)
    skipped = matmul(pooled_c, w_skip)
    mixed_c, summary_c, keys_c, values_c = attention_forward(query_c, key_c, value_c, valid, H2)
    joint_c = (mixed_c + query_c.astype(jnp.float32)).astype(jnp.bfloat16)
    hidden_c = skipped + matmul(joint_c, w_proj2)
    normed_d, unit_d, inv_d = norm_forward(hidden_c, gain_mlp2)
    normed_d = normed_d.astype(jnp.bfloat16)
    inner_d = matmul(normed_d, w_fc2)
    active_d = jax.nn.gelu(inner_d, approximate=False).astype(jnp.bfloat16)
    output = hidden_c + matmul(active_d, w_out2)
    grad_out = cotangent.reshape(batch, PT, D2).astype(jnp.float32)
    grad_mlp = grad_out.astype(jnp.bfloat16)
    grad_w_out2 = weight_grad(active_d, grad_mlp)
    grad_inner = gelu_back(inner_d, matmul_back(grad_mlp, w_out2)).astype(jnp.bfloat16)
    grad_w_fc2 = weight_grad(normed_d, grad_inner)
    grad_norm_d, grad_gain_mlp2 = norm_backward(
        matmul_back(grad_inner, w_fc2), unit_d, inv_d, gain_mlp2
    )
    grad_hidden = (grad_out + grad_norm_d).astype(jnp.bfloat16)
    grad_w_proj2 = weight_grad(joint_c, grad_hidden)
    grad_w_skip = weight_grad(pooled_c, grad_hidden)
    grad_z = matmul_back(grad_hidden, w_proj2).astype(jnp.bfloat16)
    grad_pooled = matmul_back(grad_hidden, w_skip)
    grad_query, grad_key, grad_value = attention_backward(
        query_c, keys_c, values_c, summary_c, grad_z, valid, H2
    )
    grad_joined = jnp.concatenate(
        [spread_space(grad_query), spread_space(grad_key), spread_space(grad_value)], axis=-1
    )
    grad_w_qkv2 = weight_grad(normed_c, grad_joined)
    grad_normed_c = matmul_back(grad_joined, w_qkv2) + spread_space(grad_pooled)
    grad_middle, grad_gain_attn2 = norm_backward(grad_normed_c, unit_c, inv_c, gain_attn2)
    grad_mlp_a = grad_middle.astype(jnp.bfloat16)
    grad_w_out1 = weight_grad(active_b, grad_mlp_a)
    grad_inner_b = gelu_back(inner_b, matmul_back(grad_mlp_a, w_out1)).astype(jnp.bfloat16)
    grad_w_fc1 = weight_grad(normed_b, grad_inner_b)
    grad_norm_b, grad_gain_mlp1 = norm_backward(
        matmul_back(grad_inner_b, w_fc1), unit_b, inv_b, gain_mlp1
    )
    grad_hidden_full = grad_middle + grad_norm_b
    grad_hidden_a = grad_hidden_full.astype(jnp.bfloat16)
    grad_w_proj1 = weight_grad(joint_a, grad_hidden_a)
    grad_z_a = matmul_back(grad_hidden_a, w_proj1).astype(jnp.bfloat16)
    grad_query_a, grad_key_a, grad_value_a = attention_backward(
        query_a, keys_a, values_a, summary_a, grad_z_a, valid, H1
    )
    grad_joined_a = jnp.concatenate(
        [grad_query_a, spread_space(grad_key_a), spread_space(grad_value_a)], axis=-1
    )
    grad_w_qkv1 = weight_grad(normed_a, grad_joined_a)
    grad_norm_a, grad_gain_attn1 = norm_backward(
        matmul_back(grad_joined_a, w_qkv1), unit_a, inv_a, gain_attn1
    )
    grad_source = (grad_hidden_full + grad_norm_a).astype(jnp.bfloat16)
    gains = lax.psum(
        (grad_gain_attn1, grad_gain_mlp1, grad_gain_attn2, grad_gain_mlp2),
        ("group", "clip", "micro"),
    )
    flats = (
        grad_w_qkv1.reshape(-1),
        grad_w_proj1.reshape(-1),
        grad_w_fc1.reshape(-1),
        grad_w_out1.reshape(-1),
        grad_w_qkv2.reshape(-1),
        grad_w_proj2.reshape(-1),
        grad_w_skip.reshape(-1),
        grad_w_fc2.reshape(-1),
        grad_w_out2.reshape(-1),
    )
    shares = (
        lax.psum_scatter(flats[0], ("clip", "micro"), scatter_dimension=0, tiled=True),
        lax.psum_scatter(flats[1], ("clip", "micro"), scatter_dimension=0, tiled=True),
        lax.psum_scatter(flats[2], ("clip", "micro"), scatter_dimension=0, tiled=True),
        lax.psum_scatter(flats[3], ("clip", "micro"), scatter_dimension=0, tiled=True),
        lax.psum_scatter(flats[4], ("clip", "micro"), scatter_dimension=0, tiled=True),
        lax.psum_scatter(flats[5], ("clip", "micro"), scatter_dimension=0, tiled=True),
        lax.psum_scatter(flats[6], ("clip", "micro"), scatter_dimension=0, tiled=True),
        lax.psum_scatter(flats[7], ("clip", "micro"), scatter_dimension=0, tiled=True),
        lax.psum_scatter(flats[8], ("clip", "micro"), scatter_dimension=0, tiled=True),
    )
    shares = (
        lax.psum(shares[0].astype(jnp.bfloat16), "group").astype(jnp.float32),
        lax.psum(shares[1].astype(jnp.bfloat16), "group").astype(jnp.float32),
        lax.psum(shares[2].astype(jnp.bfloat16), "group").astype(jnp.float32),
        lax.psum(shares[3].astype(jnp.bfloat16), "group").astype(jnp.float32),
        lax.psum(shares[4].astype(jnp.bfloat16), "group").astype(jnp.float32),
        lax.psum(shares[5].astype(jnp.bfloat16), "group").astype(jnp.float32),
        lax.psum(shares[6].astype(jnp.bfloat16), "group").astype(jnp.float32),
        lax.psum(shares[7].astype(jnp.bfloat16), "group").astype(jnp.float32),
        lax.psum(shares[8].astype(jnp.bfloat16), "group").astype(jnp.float32),
    )
    return (
        output.astype(jnp.bfloat16).reshape(cotangent.shape),
        grad_source.reshape(inputs.shape),
        gains[0],
        gains[1],
        gains[2],
        gains[3],
        shares[0],
        shares[1],
        shares[2],
        shares[3],
        shares[4],
        shares[5],
        shares[6],
        shares[7],
        shares[8],
    )


def solution(mesh):
    placed = (
        P("group", "micro", "clip", None, None),
        P("group"),
        P("group", "micro", "clip", None, None),
        P(),
        P(),
        P(),
        P(),
        P(),
        P(),
        P(),
        P(),
        P(),
        P(),
        P(),
        P(),
        P(),
    )
    return jax.shard_map(
        body,
        mesh=mesh,
        in_specs=placed,
        out_specs=(
            P("group", "micro", "clip", None, None),
            P("group", "micro", "clip", None, None),
            P(),
            P(),
            P(),
            P(),
            P(("clip", "micro")),
            P(("clip", "micro")),
            P(("clip", "micro")),
            P(("clip", "micro")),
            P(("clip", "micro")),
            P(("clip", "micro")),
            P(("clip", "micro")),
            P(("clip", "micro")),
            P(("clip", "micro")),
        ),
        check_vma=False,
    )
```

profile of v0, /device:TPU:0, one launch (start us, length us, event | category | flops | bytes accessed | tf_op | source)
XLA Modules:
  0.0 1966.0 jit_solution(11957651375857316101)
XLA Ops:
  25.4 7.4 reshape.446
  53.3 7.0 reshape.445
  115.8 54.6 %while.52 = (s32[]{:T(128)}, f32[2,1568,384]{2,1,0:T(8,128)}, f32[2,4,1568,1]{2,1,3,0:T(4,128)S(1)}, bf16[2,784,384]{1,2,0:T(8,128)(2,1)}, pred[784]{0:T(1024)(1...) while((s32[]{:T(128)}, f32[2,1568,384]{2,1,0:T(8,128)}, ...), condition=%wide.region_9.10_spmd, body=%wide.region_6.9_spmd.sunk | while | flops 1947223936 | bytes 78482824 | solution.py:188
  128.4 8.1 fusion.208
  155.5 8.1 fusion.208
  170.4 7.1 fusion.122
  180.9 19.4 fusion.50
  200.3 47.0 %multiply_convert_fusion.2 = (bf16[2,1568,1536]{2,1,0:T(8,128)(2,1)S(1)}, f32[2,1568,1536]{2,1,0:T(8,128)}) fusion(f32[2,1568,1536]{2,1,0:T(8,128)} %get-tuple-element.539, u8[1568,1536]{1,0:T(8,128)(4,1)} %get-tuple-element.399, u8[1568,1536]{1,0:T(8,128)(4,1)} %get-tuple-element.398), kind=kLoop, calls=%fused_computation.70 | loop fusion | flops 337182720 | bytes 52985856 | tf_op jit(solution)/shard_map/convert_element_type | solution.py:241
  257.9 12.8 fusion.68
  270.6 20.2 %fusion.116 = (f32[2,1568,768]{2,1,0:T(8,128)}, f32[2,1568,768]{2,1,0:T(8,128)}, f32[2,1568,768]{2,1,0:T(8,128)}) fusion(f32[2,1568,2304]{2,1,0:T(8,128)} %fusion.68), kind=kLoop, calls=%fused_computation.282 | loop fusion | bytes 57802752 | tf_op jit(solution)/shard_map/slice | solution.py:247
  290.8 12.1 reshape.451
  302.9 11.4 reduce_sum.320
  332.7 12.1 reshape.449
  344.8 11.3 reduce_sum.317
  377.2 6.7 reshape.477
  383.9 12.1 reshape.450
  396.0 11.2 reduce_sum.319
  414.0 7.1 reduce_sum.316
  424.0 11.1 pad_maximum_fusion.4
  435.0 8.6 copy.174
  443.6 10.2 pad_maximum_fusion.3
  453.8 8.6 copy.172
  463.9 31.6 %while.53 = (s32[]{:T(128)}, f32[2,392,768]{2,1,0:T(8,128)}, f32[2,8,392,1]{2,1,3,0:T(8,128)S(1)}, bf16[2,784,768]{1,2,0:T(8,128)(2,1)}, pred[784]{0:T(1024)(128...) while((s32[]{:T(128)}, f32[2,392,768]{2,1,0:T(8,128)}, ...), condition=%wide.region_23.24_spmd, body=%wide.region_20.23_spmd.sunk | while | flops 973611968 | bytes 44671120 | solution.py:188
  500.6 10.5 fusion.66
  511.1 24.3 %multiply_convert_fusion.3 = (bf16[2,392,3072]{2,1,0:T(8,128)(2,1)}, f32[2,392,3072]{2,1,0:T(8,128)}) fusion(f32[2,392,3072]{2,1,0:T(8,128)S(1)} %get-tuple-element.544, u8[392,3072]{1,0:T(8,128)(4,1)} %get-tuple-element.405, u8[392,3072]{1,0:T(8,128)(4,1)S(1)} %get-tuple-element.404), kind=kLoop, calls=%fused_computation.91 | loop fusion | flops 168591360 | bytes 26492928 | tf_op jit(solution)/shard_map/convert_element_type | solution.py:257
  535.4 11.8 add_convert_fusion.1
  547.2 10.3 convolution_bitcast_fusion.2
  557.5 7.4 multiply_reduce_fusion.11
  573.6 79.9 %while.54 = (s32[]{:T(128)}, f32[2,392,768]{2,1,0:T(8,128)}, f32[2,784,768]{1,2,0:T(8,128)}, f32[2,784,768]{1,2,0:T(8,128)}, bf16[2,784,768]{1,2,0:T(8,128)(2,1)...) while((s32[]{:T(128)}, f32[2,392,768]{2,1,0:T(8,128)}, ...), condition=%wide.region_30.31_spmd, body=%wide.region_28.30_spmd.sunk | while | flops 2398058496 | bytes 189283760 | solution.py:195
  588.1 8.6 multiply_reduce_fusion.17
  627.8 8.6 multiply_reduce_fusion.17
  653.4 9.5 copy.190
  668.9 9.5 copy.185
  687.5 9.7 convolution_bitcast_fusion
  728.4 11.0 reshape.454
  743.6 7.1 reshape.459
  756.0 10.7 reshape.473
  781.2 11.1 reshape.458
  801.9 11.0 reshape.456
  820.9 12.6 convolution_bitcast_fusion.1
  833.6 13.3 multiply_reduce_fusion.2
  849.0 10.9 convolution_bitcast_fusion.4
  859.9 22.6 %add_convert_fusion = bf16[2,1568,1536]{2,1,0:T(8,128)(2,1)} fusion(f32[2,1568,1536]{2,1,0:T(8,128)} %get-tuple-element.507, f32[2,1568,1536]{2,1,0:T(8,128)} %get-tuple-element.539, f32[2,1568,384]{2,1,0:T(8,128)} %copy-done.24, bf16[1536,384]{1,0:T(8,128)(2,1)S(1)} %copy-done.80), kind=kOutput, calls=%fused_computation.69 | convolution fusion | flops 3768016896 | bytes 54165504 | tf_op jit(solution)/shard_map/bnf,cf->bnc/dot_general | solution.py:172
  882.6 9.7 convolution_bitcast_fusion.5
  892.4 8.6 multiply_reduce_fusion.3
  911.0 148.7 %while.55 = (s32[]{:T(128)}, f32[2,1568,384]{2,1,0:T(8,128)}, f32[2,784,384]{1,2,0:T(8,128)}, f32[2,784,384]{1,2,0:T(8,128)}, bf16[2,784,384]{1,2,0:T(8,128)(2,1...) while((s32[]{:T(128)}, f32[2,1568,384]{2,1,0:T(8,128)}, ...), condition=%wide.region_37.38_spmd, body=%wide.region_35.37_spmd.sunk | while | flops 4765710336 | bytes 246936144 | solution.py:195
  914.5 9.6 subtract_exponential_fusion.5
  928.3 13.3 multiply_reduce_fusion.18
  941.7 13.8 multiply_convert_fusion.18
  959.4 10.3 fusion.237
  971.5 7.5 convolution_multiply_fusion.11
  988.6 9.6 subtract_exponential_fusion.5
  1002.4 13.3 multiply_reduce_fusion.18
  1015.8 13.8 multiply_convert_fusion.18
  1033.5 10.3 fusion.237
  1045.6 7.5 convolution_multiply_fusion.11
  1106.6 6.2 reshape.461
  1119.3 6.2 reshape.463
  1125.6 8.9 convolution_bitcast_fusion.3
  1134.6 7.6 fusion.47
  1145.0 686.1 %all-reduce.20 = (bf16[442368]{0:T(1024)(128)(2,1)}, bf16[147456]{0:T(1024)(128)(2,1)}, bf16[589824]{0:T(1024)(128)(2,1)}, bf16[589824]{0:T(1024)(128)(2,1)}, bf...) all-reduce(f32[442368]{0:T(1024)S(1)} %reshape.465, ...), channel_id=2, replica_groups=mesh['group'=2,'clip'=8,'micro'=2] {'clip','micro'}, use_global_device_ids=true, to_apply=%region_48.49.clone | all-reduce | flops 8257536 | bytes 49545216
  1845.5 65.0 %all-reduce.9 = (f32[384]{0:T(512)}, f32[384]{0:T(512)}, f32[384]{0:T(512)}, f32[768]{0:T(1024)}) all-reduce(f32[384]{0:T(512)} %get-tuple-element.406, f32[384]{0:T(512)} %get-tuple-element.402, f32[384]{0:T(512)} %get-tuple-element.400, ...), channel_id=1, replica_groups=mesh['group'=2,'clip'=8,'micro'=2] {'group','clip','micro'}, use_global_device_ids=true, to_apply=%region_41.42 | all-reduce | flops 1920 | bytes 15360 | tf_op jit(solution)/shard_map/psum | solution.py:303
  1910.5 7.2 fusion.59
  1921.9 27.1 %all-reduce.19.cloned.1.call-done = (bf16[36864]{0:T(1024)(128)(2,1)}, bf16[36864]{0:T(1024)(128)(2,1)}, bf16[55296]{0:T(1024)(128)(2,1)}, bf16[36864]{0:T(1024)...) async-done(((bf16[36864]{0:T(1024)(128)(2,1)}, bf16[36864]{0:T(1024)(128)(2,1)}, bf16[55296]{0:T(1024)(128)(2,1)}, bf16[36864]{0:T(1024)(128)(2,1)}, ...) | async-done | bytes 921616 | tf_op jit(solution)/shard_map/psum | solution.py:332
  (527 shorter events, 521.6 us)
Async XLA Ops:
  7.2 250.7 %copy-start = (bf16[384,2304]{1,0:T(8,128)(2,1)S(1)}, bf16[384,2304]{1,0:T(8,128)(2,1)}, u32[]{:S(2)}) copy-start(bf16[384,2304]{1,0:T(8,128)(2,1)} %param.34) | copy-start | bytes 5308420
  7.2 1910.5 %all-reduce.17.cloned.1.call-start = ((), (), s32[]{:S(2)}) async-start(), calls=%async_computation | async-start | bytes 221184 | tf_op jit(solution)/shard_map/psum | solution.py:330
  44.2 51.3 %collective-permute-start.2 = (bf16[2,196,384]{2,0,1:T(2,128)(2,1)}, bf16[2,196,384]{2,0,1:T(2,128)(2,1)}, u32[]{:S(2)}, u32[]{:S(2)}) collective-permute-start(bf16[2,196,384]{2,0,1:T(2,128)(2,1)} %bitcast.43), channel_id=1, source_target_pairs={{0,2},{2,4},{4,6},{6,8},{8,10},{10,12},{12,14},{1,3},{3,5},{5,7},{... | collective-permute-start | bytes 903176 | tf_op jit(solution)/shard_map/ppermute | solution.py:26
  49.8 45.7 %collective-permute-start.3 = (bf16[2,196,384]{2,0,1:T(2,128)(2,1)}, bf16[2,196,384]{2,0,1:T(2,128)(2,1)}, u32[]{:S(2)}, u32[]{:S(2)}) collective-permute-start(bf16[2,196,384]{2,0,1:T(2,128)(2,1)} %bitcast.43), channel_id=1, source_target_pairs={{0,4},{2,6},{4,8},{6,10},{8,12},{10,14},{1,5},{3,7},{5,9},{7,11},{... | collective-permute-start | bytes 903176 | tf_op jit(solution)/shard_map/ppermute | solution.py:26
  67.3 11.6 copy-start.37
  71.9 32.4 %collective-permute-start = (bf16[2,196,384]{2,0,1:T(2,128)(2,1)}, bf16[2,196,384]{2,0,1:T(2,128)(2,1)}, u32[]{:S(2)}, u32[]{:S(2)}) collective-permute-start(bf16[2,196,384]{2,0,1:T(2,128)(2,1)} %bitcast.39), channel_id=1, source_target_pairs={{0,2},{2,4},{4,6},{6,8},{8,10},{10,12},{12,14},{1,3},{3,5},{5,7},{... | collective-permute-start | bytes 903176 | tf_op jit(solution)/shard_map/ppermute | solution.py:26
  76.1 28.2 %collective-permute-start.1 = (bf16[2,196,384]{2,0,1:T(2,128)(2,1)}, bf16[2,196,384]{2,0,1:T(2,128)(2,1)}, u32[]{:S(2)}, u32[]{:S(2)}) collective-permute-start(bf16[2,196,384]{2,0,1:T(2,128)(2,1)} %bitcast.39), channel_id=1, source_target_pairs={{0,4},{2,6},{4,8},{6,10},{8,12},{10,14},{1,5},{3,7},{5,9},{7,11},{... | collective-permute-start | bytes 903176 | tf_op jit(solution)/shard_map/ppermute | solution.py:26
  177.6 22.7 %copy-start.57 = (f32[2,1568]{1,0:T(2,128)}, f32[2,1568]{1,0:T(2,128)S(1)}, u32[]{:S(2)}) copy-start(f32[2,1568]{1,0:T(2,128)S(1)} %broadcast_multiply_fusion.7) | copy-start | bytes 37636
  180.9 19.4 copy-start.59
  200.3 47.0 %copy-start.7 = (f32[2,1568,384]{2,1,0:T(8,128)S(1)}, f32[2,1568,384]{2,1,0:T(8,128)}, u32[]{:S(2)}) copy-start(f32[2,1568,384]{2,1,0:T(8,128)} %copy-done.6) | copy-start | bytes 14450692
  200.3 47.0 %copy-start.79 = (bf16[1536,384]{1,0:T(8,128)(2,1)S(1)}, bf16[1536,384]{1,0:T(8,128)(2,1)}, u32[]{:S(2)}) copy-start(bf16[1536,384]{1,0:T(8,128)(2,1)} %param.32) | copy-start | bytes 3538948
  326.3 97.7 %collective-permute-start.6 = (bf16[2,196,768]{2,0,1:T(2,128)(2,1)}, bf16[2,196,768]{2,0,1:T(2,128)(2,1)}, u32[]{:S(2)}, u32[]{:S(2)}) collective-permute-start(bf16[2,196,768]{2,0,1:T(2,128)(2,1)} %bitcast.56), channel_id=1, source_target_pairs={{0,2},{2,4},{4,6},{6,8},{8,10},{10,12},{12,14},{1,3},{3,5},{5,7},{... | collective-permute-start | bytes 1806344 | tf_op jit(solution)/shard_map/ppermute | solution.py:26
  330.5 93.4 %collective-permute-start.7 = (bf16[2,196,768]{2,0,1:T(2,128)(2,1)}, bf16[2,196,768]{2,0,1:T(2,128)(2,1)}, u32[]{:S(2)}, u32[]{:S(2)}) collective-permute-start(bf16[2,196,768]{2,0,1:T(2,128)(2,1)} %bitcast.56), channel_id=1, source_target_pairs={{0,4},{2,6},{4,8},{6,10},{8,12},{10,14},{1,5},{3,7},{5,9},{7,11},{... | collective-permute-start | bytes 1806344 | tf_op jit(solution)/shard_map/ppermute | solution.py:26
  371.0 72.5 %collective-permute-start.4 = (bf16[2,196,768]{2,0,1:T(2,128)(2,1)}, bf16[2,196,768]{2,0,1:T(2,128)(2,1)}, u32[]{:S(2)}, u32[]{:S(2)}) collective-permute-start(bf16[2,196,768]{2,0,1:T(2,128)(2,1)} %bitcast.52), channel_id=1, source_target_pairs={{0,2},{2,4},{4,6},{6,8},{8,10},{10,12},{12,14},{1,3},{3,5},{5,7},{... | collective-permute-start | bytes 1806344 | tf_op jit(solution)/shard_map/ppermute | solution.py:26
  373.1 70.4 %collective-permute-start.5 = (bf16[2,196,768]{2,0,1:T(2,128)(2,1)}, bf16[2,196,768]{2,0,1:T(2,128)(2,1)}, u32[]{:S(2)}, u32[]{:S(2)}) collective-permute-start(bf16[2,196,768]{2,0,1:T(2,128)(2,1)} %bitcast.52), channel_id=1, source_target_pairs={{0,4},{2,6},{4,8},{6,10},{8,12},{10,14},{1,5},{3,7},{5,9},{7,11},{... | collective-permute-start | bytes 1806344 | tf_op jit(solution)/shard_map/ppermute | solution.py:26
  410.6 12.0 copy-start.31
  424.0 19.6 copy-start.40
  453.8 10.2 copy-start.69
  500.1 64.8 %copy-start.18 = (f32[2,392,768]{2,1,0:T(8,128)}, f32[2,392,768]{2,1,0:T(8,128)S(1)}, u32[]{:S(2)}) copy-start(f32[2,392,768]{2,1,0:T(8,128)S(1)} %get-tuple-element.543) | copy-start | bytes 7225348
  511.1 24.4 %copy-start.52 = (bf16[1,2,1,392,768]{4,3,2,1,0:T(8,128)(2,1)S(1)}, bf16[1,2,1,392,768]{4,3,2,1,0:T(8,128)(2,1)}, u32[]{:S(2)}) copy-start(bf16[1,2,1,392,768]{4,3,2,1,0:T(8,128)(2,1)} %param.26) | copy-start | bytes 3612676
  547.2 10.3 copy-start.41
  653.4 15.5 copy-start.50
  684.4 12.8 slice-start.20
  684.4 12.8 slice-start.22
  687.5 9.7 copy-start.19
  687.5 9.7 slice-start.21
  687.5 9.7 slice-start.23
  687.5 14.7 slice-start.9
  687.5 14.7 slice-start.10
  708.0 15.1 copy-start.26
  711.4 11.7 copy-start.33
  714.6 57.0 %collective-permute-start.10 = (bf16[2,196,768]{2,0,1:T(2,128)(2,1)}, bf16[2,196,768]{2,0,1:T(2,128)(2,1)}, u32[]{:S(2)}, u32[]{:S(2)}) collective-permute-start(bf16[2,196,768]{2,0,1:T(2,128)(2,1)} %get-tuple-element.529), channel_id=1, source_target_pairs={{2,0},{4,2},{6,4},{8,6},{10,8},{12,10},{14,12},{3,1},{5,3},{7,5},{... | collective-permute-start | bytes 1806344 | tf_op jit(solution)/shard_map/ppermute | solution.py:26
  715.9 55.7 %collective-permute-start.11 = (bf16[2,196,768]{2,0,1:T(2,128)(2,1)}, bf16[2,196,768]{2,0,1:T(2,128)(2,1)}, u32[]{:S(2)}, u32[]{:S(2)}) collective-permute-start(bf16[2,196,768]{2,0,1:T(2,128)(2,1)} %get-tuple-element.530), channel_id=1, source_target_pairs={{4,0},{6,2},{8,4},{10,6},{12,8},{14,10},{5,1},{7,3},{9,5},{11,7},{... | collective-permute-start | bytes 1806344 | tf_op jit(solution)/shard_map/ppermute | solution.py:26
  720.3 72.0 %collective-permute-start.8 = (bf16[2,196,768]{2,0,1:T(2,128)(2,1)}, bf16[2,196,768]{2,0,1:T(2,128)(2,1)}, u32[]{:S(2)}, u32[]{:S(2)}) collective-permute-start(bf16[2,196,768]{2,0,1:T(2,128)(2,1)} %get-tuple-element.531), channel_id=1, source_target_pairs={{2,0},{4,2},{6,4},{8,6},{10,8},{12,10},{14,12},{3,1},{5,3},{7,5},{... | collective-permute-start | bytes 1806344 | tf_op jit(solution)/shard_map/ppermute | solution.py:26
  721.6 70.7 %collective-permute-start.9 = (bf16[2,196,768]{2,0,1:T(2,128)(2,1)}, bf16[2,196,768]{2,0,1:T(2,128)(2,1)}, u32[]{:S(2)}, u32[]{:S(2)}) collective-permute-start(bf16[2,196,768]{2,0,1:T(2,128)(2,1)} %get-tuple-element.532), channel_id=1, source_target_pairs={{4,0},{6,2},{8,4},{10,6},{12,8},{14,10},{5,1},{7,3},{9,5},{11,7},{... | collective-permute-start | bytes 1806344 | tf_op jit(solution)/shard_map/ppermute | solution.py:26
  728.4 11.0 copy-start.39
  801.9 16.1 slice-start.14
  818.1 15.4 slice-start.7
  818.1 15.4 slice-start.18
  820.9 12.6 slice-start.8
  820.9 12.6 slice-start.19
  820.9 12.7 copy-start.66
  820.9 12.7 copy-start.72
  820.9 12.7 copy-start.78
  849.0 10.9 copy-start.24
  849.0 10.9 copy-start.80
  849.0 33.6 %slice-start.5 = ((s8[4816896]{0:T(1024)(128)(4,1)}), s8[4194304]{0:T(1024)(128)(4,1)S(1)}, s32[]{:S(2)}) async-start(s8[4816896]{0:T(1024)(128)(4,1)} %bitcast.392), calls=%async_computation.7 | async-start | bytes 8388608
  859.9 22.7 %slice-start.6 = ((s8[4816896]{0:T(1024)(128)(4,1)}), s8[622592]{0:T(1024)(128)(4,1)S(1)}, s32[]{:S(2)}) async-start(s8[4816896]{0:T(1024)(128)(4,1)} %bitcast.392), calls=%async_computation.8 | async-start | bytes 1245184
  859.9 22.7 %copy-start.58 = (f32[2,1568]{1,0:T(2,128)S(1)}, f32[2,1568]{1,0:T(2,128)}, u32[]{:S(2)}) copy-start(f32[2,1568]{1,0:T(2,128)} %copy-done.57) | copy-start | bytes 37636
  859.9 22.7 %copy-start.60 = (f32[2,1568]{1,0:T(2,128)S(1)}, f32[2,1568]{1,0:T(2,128)}, u32[]{:S(2)}) copy-start(f32[2,1568]{1,0:T(2,128)} %copy-done.59) | copy-start | bytes 37636
  859.9 22.7 %copy-start.74 = (f32[384]{0:T(512)S(1)}, f32[384]{0:T(512)}, u32[]{:S(2)}) copy-start(f32[384]{0:T(512)} %param.30) | copy-start | bytes 4612
  882.6 9.8 copy-start.22
  882.6 9.8 copy-start.82
  882.6 18.4 slice-start.16
  912.8 11.3 copy-start.3
  941.7 13.8 copy-start.4
  986.9 11.3 copy-start.3
  1015.8 13.8 copy-start.4
  1059.7 13.1 slice-start.3
  1066.2 33.9 %collective-permute-start.12 = (bf16[2,196,384]{1,2,0:T(8,128)(2,1)}, bf16[2,196,384]{1,2,0:T(8,128)(2,1)S(1)}, u32[]{:S(2)}, u32[]{:S(2)}) collective-permute-start(bf16[2,196,384]{1,2,0:T(8,128)(2,1)} %get-tuple-element.533), channel_id=1, source_target_pairs={{2,0},{4,2},{6,4},{8,6},{10,8},{12,10},{14,12},{3,1},{5,3},{7,5},{... | collective-permute-start | bytes 903176 | tf_op jit(solution)/shard_map/ppermute | solution.py:26
  1067.7 32.4 %collective-permute-start.13 = (bf16[2,196,384]{1,2,0:T(8,128)(2,1)S(1)}, bf16[2,196,384]{1,2,0:T(8,128)(2,1)}, u32[]{:S(2)}, u32[]{:S(2)}) collective-permute-start(bf16[2,196,384]{1,2,0:T(8,128)(2,1)S(1)} %get-tuple-element.534), channel_id=1, source_target_pairs={{4,0},{6,2},{8,4},{10,6},{12,8},{14,10},{5,1},{7,3},{9,5},{11,7},{... | collective-permute-start | bytes 903176 | tf_op jit(solution)/shard_map/ppermute | solution.py:26
  1070.3 42.5 %collective-permute-start.14 = (bf16[2,196,384]{1,2,0:T(8,128)(2,1)}, bf16[2,196,384]{1,2,0:T(8,128)(2,1)}, u32[]{:S(2)}, u32[]{:S(2)}) collective-permute-start(bf16[2,196,384]{1,2,0:T(8,128)(2,1)} %get-tuple-element.535), channel_id=1, source_target_pairs={{2,0},{4,2},{6,4},{8,6},{10,8},{12,10},{14,12},{3,1},{5,3},{7,5},{... | collective-permute-start | bytes 903176 | tf_op jit(solution)/shard_map/ppermute | solution.py:26
  1071.6 41.2 %collective-permute-start.15 = (bf16[2,196,384]{1,2,0:T(8,128)(2,1)S(1)}, bf16[2,196,384]{1,2,0:T(8,128)(2,1)}, u32[]{:S(2)}, u32[]{:S(2)}) collective-permute-start(bf16[2,196,384]{1,2,0:T(8,128)(2,1)S(1)} %get-tuple-element.536), channel_id=1, source_target_pairs={{4,0},{6,2},{8,4},{10,6},{12,8},{14,10},{5,1},{7,3},{9,5},{11,7},{... | collective-permute-start | bytes 903176 | tf_op jit(solution)/shard_map/ppermute | solution.py:26
  1835.2 113.8 %all-reduce.19.cloned.1.call-start = ((), (), s32[]{:S(2)}) async-start(), calls=%async_computation.1 | async-start | bytes 1843200 | tf_op jit(solution)/shard_map/psum | solution.py:332
  (77 other events, 407.8 us)
Sparse Core Ops, SparseCore 0:
  1835.4 45.9 all-reduce.16
  1910.7 38.2 all-reduce.18
where the time goes:
time: 1980 us; the launch traced here: 1970 us
  blocking collectives  751 us (38%)
  local copies, waits for them, and re-layouts  440 us (22%)
  matrix products  392 us (20%)
  other arithmetic  295 us (15%)
  starting transfers between devices  37.4 us (2%)
  waiting for transfers between devices  27.1 us (1%)
  between operations  20.3 us (1%)
    unnamed x1, blocking collectives  686 us
    dot_general x9, matrix products, matmul_back(): jnp.einsum('bnf,cf->bnc', grad, right, preferred_element_type=jnp.float32)  79.6 us
    dot_general x9, matrix products, weight_grad(): jnp.einsum('bnc,bnf->cf', left, grad, preferred_element_type=jnp.float32)  71.9 us
    dot_general x9, matrix products, matmul(): jnp.einsum('bnc,cf->bnf', left, right, preferred_element_type=jnp.float32)  69 us
    psum x1, blocking collectives, body(): lax.psum((grad_gain_attn1, grad_gain_mlp1, grad_gain_attn2, grad_gain_mlp...  65 us
    reshape x6, local copies, waits for them, and re-layouts, pool_space(): shaped = values.reshape(lead + (frames, HT // 2, 2, WD // 2, 2, width))  57.4 us
    reduce_sum x6, other arithmetic, pool_space(): return jnp.mean(shaped, axis=(-4, -2)).reshape(lead + (-1, width))  52.9 us
    reshape x6, local copies, waits for them, and re-layouts, spread_space(): return wide.reshape(lead + (-1, width))  52.6 us
  transfers between devices with their start and end apart: 18, of which 1 were waited for; matrix products, arithmetic and copies ran while one was open for 14% of the time, Pallas kernels for 0%

commit v1 on v0

v1 whole, which is shorter than its diff:
```python
from functools import partial

import jax
import jax.numpy as jnp
from jax import lax
from jax.sharding import PartitionSpec as P

D1 = 384
D2 = 768
QT = 1568
PT = 392
MT = 196
HD = 96
FR = 8
HT = 14
WD = 14
H1 = 4
H2 = 8
epsilon = 1e-06
f32 = jnp.float32
bf16 = jnp.bfloat16


def shift(value, steps):
    count = lax.axis_size("clip")
    first, last = (max(0, -steps), min(count, count - steps))
    return lax.ppermute(value, "clip", [(s, s + steps) for s in range(first, last)])


def norm_stats(values):
    center = values - jnp.mean(values, axis=-1, keepdims=True)
    inv = lax.rsqrt(jnp.mean(center * center, axis=-1, keepdims=True) + epsilon)
    return (center * inv, inv)


def norm_back(grad, unit, inv, gain):
    du = grad * gain
    dg = jnp.sum(grad * unit, axis=tuple(range(grad.ndim - 1)))
    dx = inv * (
        du - jnp.mean(du, axis=-1, keepdims=True) - unit * jnp.mean(du * unit, axis=-1, keepdims=True)
    )
    return (dx, dg)


def dot(a, b):
    return jnp.einsum("...nc,cf->...nf", a, b, preferred_element_type=f32)


def dot_t(a, b):
    return jnp.einsum("...nf,cf->...nc", a, b, preferred_element_type=f32)


def wgrad(a, b):
    a = a.reshape(-1, a.shape[-1])
    b = b.reshape(-1, b.shape[-1])
    return jnp.einsum("nc,nf->cf", a, b, preferred_element_type=f32)


def split_heads(v, heads):
    return v.reshape(v.shape[:-1] + (heads, HD))


def attend(q, k, v, bias, heads):
    s = jnp.einsum(
        "bnhd,bkhd->bhnk", split_heads(q, heads), split_heads(k, heads), preferred_element_type=f32
    ) * HD ** (-0.5)
    s = s + bias
    top = jnp.max(s, axis=-1, keepdims=True)
    e = jnp.exp(s - top)
    total = jnp.sum(e, axis=-1, keepdims=True)
    o = jnp.einsum(
        "bhnk,bkhd->bnhd", (e / total).astype(bf16), split_heads(v, heads), preferred_element_type=f32
    )
    return (o.reshape(q.shape), top + jnp.log(total))


def attend_back(q, k, v, bias, lse, gz, heads):
    sq, sk, sv, sg = (split_heads(t, heads) for t in (q, k, v, gz))
    s = jnp.einsum("bnhd,bkhd->bhnk", sq, sk, preferred_element_type=f32) * HD ** (-0.5)
    p = jnp.exp(s + bias - lse)
    dp = jnp.einsum("bnhd,bkhd->bhnk", sg, sv, preferred_element_type=f32)
    delta = jnp.sum(dp * p, axis=-1, keepdims=True)
    ds = (p * (dp - delta)).astype(bf16)
    dq = jnp.einsum("bhnk,bkhd->bnhd", ds, sk, preferred_element_type=f32) * HD ** (-0.5)
    dk = jnp.einsum("bhnk,bnhd->bkhd", ds, sq, preferred_element_type=f32) * HD ** (-0.5)
    dv = jnp.einsum("bhnk,bnhd->bkhd", p.astype(bf16), sg, preferred_element_type=f32)
    return (dq.reshape(q.shape), dk.reshape(k.shape), dv.reshape(v.shape))


def gelu_both(x):
    phi = 0.5 * (1.0 + lax.erf(x * 0.7071067811865476))
    dens = jnp.exp(-0.5 * x * x) * 0.3989422804014327
    return ((x * phi).astype(bf16), phi + x * dens)


def tmean_matrix():
    rows = lax.broadcasted_iota(jnp.int32, (MT, PT), 0)
    cols = lax.broadcasted_iota(jnp.int32, (MT, PT), 1)
    cell = MT // (FR // 2)
    hit = (cols // (2 * cell) == rows // cell) & (cols % cell == rows % cell)
    return jnp.where(hit, 0.5, 0.0).astype(bf16)


def remember(pooled):
    mem = jnp.einsum("mp,bpc->bmc", tmean_matrix(), pooled, preferred_element_type=f32).astype(bf16)
    return jnp.concatenate([pooled, shift(mem, 1), shift(mem, 2)], axis=1)


def recall(grad_rows):
    near = shift(grad_rows[:, PT : PT + MT].astype(bf16), -1)
    far = shift(grad_rows[:, PT + MT :].astype(bf16), -2)
    total = (near.astype(f32) + far.astype(f32)).astype(bf16)
    back = jnp.einsum("mp,bmc->bpc", tmean_matrix(), total, preferred_element_type=f32)
    return grad_rows[:, :PT] + back


def halve(value, axis, bit, index):
    n = lax.axis_size(axis)
    mine = lax.dynamic_index_in_dim(value, index, 0, keepdims=False)
    theirs = lax.dynamic_index_in_dim(value, 1 - index, 0, keepdims=False).astype(bf16)
    got = lax.ppermute(theirs, axis, [(i, i ^ (1 << bit)) for i in range(n)])
    return mine.astype(f32) + got.astype(f32)


def reduce_share(grad):
    clips, micros = lax.axis_size("clip"), lax.axis_size("micro")
    shares = clips * micros
    rows, cols = grad.shape
    v = grad.reshape(clips, micros, rows // shares, cols)
    v = halve(jnp.moveaxis(v, 1, 0), "micro", 0, lax.axis_index("micro"))
    half = cols // 2
    v = jnp.stack([v[..., :half], v[..., half:]])
    g = lax.axis_index("group")
    v = halve(v, "group", 0, g)
    c = lax.axis_index("clip")
    bits = clips.bit_length() - 1
    for bit in range(bits):
        open_bits = bits - bit
        w = v.reshape((2 ** (open_bits - 1), 2) + v.shape[1:])
        v = halve(jnp.moveaxis(w, 1, 0), "clip", bit, (c >> bit) & 1)
    v = v.reshape(rows // shares, half).astype(bf16)
    other = lax.ppermute(v, "group", [(0, 1), (1, 0)])
    low = jnp.where(g == 0, v, other)
    high = jnp.where(g == 0, other, v)
    return jnp.concatenate([low, high], axis=-1).astype(f32).reshape(-1)


def body(inputs, offsets, cotangent, gain_attn1, w_qkv1, w_proj1, gain_mlp1, w_fc1, w_out1,
         gain_attn2, w_qkv2, w_proj2, w_skip, gain_mlp2, w_fc2, w_out2):
    B = inputs.shape[1]
    clip = lax.axis_index("clip")
    frame = jnp.arange(MT, dtype=jnp.int32) // (MT // (FR // 2))
    later = frame >= offsets[0]
    valid = jnp.concatenate([jnp.ones((PT,), jnp.bool_), later & (clip >= 1), later & (clip >= 2)])
    bias = jnp.where(valid, 0.0, -1e30).astype(f32)[None, None, None, :]
    x = inputs.reshape(B, FR, HT // 2, 2, WD // 2, 2, D1).transpose(0, 3, 5, 1, 2, 4, 6)
    x = x.reshape(B, 4, PT, D1).astype(f32)

    unit_a, inv_a = norm_stats(x)
    na = (unit_a * gain_attn1).astype(bf16)
    qa = dot(na, w_qkv1[:, :D1]).astype(bf16).reshape(B, QT, D1)
    kva = remember(jnp.mean(na.astype(f32), axis=1).astype(bf16))
    KVa = dot(kva, w_qkv1[:, D1:]).astype(bf16)
    Ka, Va = KVa[..., :D1], KVa[..., D1:]
    oa, lse_a = attend(qa, Ka, Va, bias, H1)
    za = (oa + qa.astype(f32)).astype(bf16)
    ha = x + dot(za, w_proj1).reshape(x.shape)
    unit_b, inv_b = norm_stats(ha)
    nb = (unit_b * gain_mlp1).astype(bf16)
    ub, gpb = gelu_both(dot(nb, w_fc1))
    middle = ha + dot(ub, w_out1)
    unit_c, inv_c = norm_stats(middle)
    nc = (unit_c * gain_attn2).astype(bf16)
    pc = jnp.mean(nc.astype(f32), axis=1).astype(bf16)
    kvc = remember(pc)
    qc = dot(pc, w_qkv2[:, :D2]).astype(bf16)
    skipped = dot(pc, w_skip)
    KVc = dot(kvc, w_qkv2[:, D2:]).astype(bf16)
    Kc, Vc = KVc[..., :D2], KVc[..., D2:]
    oc, lse_c = attend(qc, Kc, Vc, bias, H2)
    zc = (oc + qc.astype(f32)).astype(bf16)
    hc = skipped + dot(zc, w_proj2)
    unit_d, inv_d = norm_stats(hc)
    nd = (unit_d * gain_mlp2).astype(bf16)
    ud, gpd = gelu_both(dot(nd, w_fc2))
    output = hc + dot(ud, w_out2)

    Gm = cotangent.reshape(B, PT, D2)
    gw_out2 = wgrad(ud, Gm)
    gid = (gpd * dot_t(Gm, w_out2)).astype(bf16)
    gw_fc2 = wgrad(nd, gid)
    dx, gg_mlp2 = norm_back(dot_t(gid, w_fc2), unit_d, inv_d, gain_mlp2)
    Gh = (Gm.astype(f32) + dx).astype(bf16)
    gw_proj2 = wgrad(zc, Gh)
    gw_skip = wgrad(pc, Gh)
    gz = dot_t(Gh, w_proj2).astype(bf16)
    dq, dk, dv = attend_back(qc, Kc, Vc, bias, lse_c, gz, H2)
    gqc = (gz.astype(f32) + dq).astype(bf16)
    dKV = jnp.concatenate([dk, dv], axis=-1).astype(bf16)
    gw_qkv2 = jnp.concatenate([wgrad(pc, gqc), wgrad(kvc, dKV)], axis=-1)
    dpc = dot_t(gqc, w_qkv2[:, :D2]) + dot_t(Gh, w_skip) + recall(dot_t(dKV, w_qkv2[:, D2:]))
    dnc = jnp.broadcast_to((0.25 * dpc)[:, None], middle.shape)
    Gmid, gg_attn2 = norm_back(dnc, unit_c, inv_c, gain_attn2)

    Gm1 = Gmid.astype(bf16)
    gw_out1 = wgrad(ub, Gm1)
    gib = (gpb * dot_t(Gm1, w_out1)).astype(bf16)
    gw_fc1 = wgrad(nb, gib)
    dx, gg_mlp1 = norm_back(dot_t(gib, w_fc1), unit_b, inv_b, gain_mlp1)
    Gha = Gmid + dx
    Gh = Gha.astype(bf16).reshape(B, QT, D1)
    gw_proj1 = wgrad(za, Gh)
    gz = dot_t(Gh, w_proj1).astype(bf16)
    dq, dk, dv = attend_back(qa, Ka, Va, bias, lse_a, gz, H1)
    gqa = (gz.astype(f32) + dq).astype(bf16)
    dKV = jnp.concatenate([dk, dv], axis=-1).astype(bf16)
    gw_qkv1 = jnp.concatenate([wgrad(na, gqa), wgrad(kva, dKV)], axis=-1)
    dkv = recall(dot_t(dKV, w_qkv1[:, D1:]))
    dna = dot_t(gqa, w_qkv1[:, :D1]).reshape(x.shape) + (0.25 * dkv)[:, None]
    dx, gg_attn1 = norm_back(dna, unit_a, inv_a, gain_attn1)
    gx = (Gha + dx).astype(bf16)
    gx = gx.reshape(B, 2, 2, FR, HT // 2, WD // 2, D1).transpose(0, 3, 4, 1, 5, 2, 6)

    gains = lax.psum((gg_attn1, gg_mlp1, gg_attn2, gg_mlp2), ("group", "clip", "micro"))
    grads = (gw_qkv1, gw_proj1, gw_fc1, gw_out1, gw_qkv2, gw_proj2, gw_skip, gw_fc2, gw_out2)
    shares = tuple(reduce_share(g) for g in grads)
    return (output.astype(bf16).reshape(cotangent.shape), gx.reshape(inputs.shape)) + tuple(gains) + shares


def solution(mesh):
    tokens = P("group", "micro", "clip", None, None)
    share = P(("clip", "micro"))
    return jax.shard_map(
        body,
        mesh=mesh,
        in_specs=(tokens, P("group"), tokens) + (P(),) * 13,
        out_specs=(tokens, tokens) + (P(),) * 4 + (share,) * 9,
        check_vma=False,
    )
```

time: 1980 us -> 974 us (0.49)
  blocking collectives: 751 us -> 40.2 us
  local copies, waits for them, and re-layouts: 440 us -> 208 us
  other arithmetic: 295 us -> 171 us
  waiting for transfers between devices: 27.1 us -> 133 us
  matrix products: 392 us -> 336 us
  starting transfers between devices: 37.4 us -> 68.9 us
    unnamed x1 -> x0, blocking collectives: 686 us -> none
    ppermute x16 -> x62, waiting for transfers between devices: 0.04 us -> 133 us  [the longest x45 76.9 us: halve(): got = lax.ppermute(theirs, axis, [(i, i ^ 1 << bit) for i in range(n)])]
    reshape x20 -> x12, local copies, waits for them, and re-layouts: 140 us -> 53.9 us  [the longest x4 27.5 us: attend(): return (o.reshape(q.shape), top + jnp.log(total))]
    while x72 -> x0, local copies, waits for them, and re-layouts: 77 us -> none  [the longest x6 42.3 us: attention_backward(): lax.map(partial(attend_backward, valid=valid, heads=heads), (queries, all...]
    dot_general x55 -> x49, matrix products: 392 us -> 336 us  [the longest x11 55.4 us: dot(): return jnp.einsum('...nc,cf->...nf', a, b, preferred_element_type=f32)]
    convert_element_type x28 -> x39, other arithmetic: 145 us -> 97.6 us  [the longest x2 54.3 us: attend_back(): ds = (p * (dp - delta)).astype(bf16)]
    reduce_sum x19 -> x11, other arithmetic: 89.1 us -> 43.8 us  [the longest x2 27.5 us: attend(): total = jnp.sum(e, axis=-1, keepdims=True)]
    dynamic_update_slice x20 -> x0, local copies, waits for them, and re-layouts: 45.2 us -> none  [the longest x16 37.7 us: attention_forward(): lax.map(partial(attend_forward, valid=valid, heads=heads), (queries, all_...]
  transfers between devices with their start and end apart: 18 -> 62, of which waited for: 1 -> 34; matrix products, arithmetic and copies ran while one was open for 14% -> 41% of each run, Pallas kernels for 0% -> 0%
where the time goes in v1:
time: 974 us; the launch traced here: 963 us
  matrix products  336 us (34%)
  local copies, waits for them, and re-layouts  208 us (21%)
  other arithmetic  171 us (18%)
  waiting for transfers between devices  133 us (14%)
  starting transfers between devices  68.9 us (7%)
  blocking collectives  40.2 us (4%)
    ppermute x45, waiting for transfers between devices, halve(): got = lax.ppermute(theirs, axis, [(i, i ^ 1 << bit) for i in range(n)])  76.9 us
    dot_general x11, matrix products, dot(): return jnp.einsum('...nc,cf->...nf', a, b, preferred_element_type=f32)  55.4 us
    dot_general x11, matrix products, dot_t(): return jnp.einsum('...nf,cf->...nc', a, b, preferred_element_type=f32)  54.5 us
    convert_element_type x2, other arithmetic, attend_back(): ds = (p * (dp - delta)).astype(bf16)  54.3 us
    dot_general x2, matrix products, attend_back(): dp = jnp.einsum('bnhd,bkhd->bhnk', sg, sv, preferred_element_type=f32)  43.3 us
    dot_general x11, matrix products, wgrad(): return jnp.einsum('nc,nf->cf', a, b, preferred_element_type=f32)  42.9 us
    psum x1, blocking collectives, body(): lax.psum((gg_attn1, gg_mlp1, gg_attn2, gg_mlp2), ('group', 'clip', 'micro'))  40.2 us
    ppermute x45, starting transfers between devices, halve(): got = lax.ppermute(theirs, axis, [(i, i ^ 1 << bit) for i in range(n)])  39.7 us
  transfers between devices with their start and end apart: 62, of which 34 were waited for; matrix products, arithmetic and copies ran while one was open for 41% of the time, Pallas kernels for 0%

profile of v1, /device:TPU:0, one launch (start us, length us, event | category | flops | bytes accessed | tf_op | source)
XLA Modules:
  0.0 962.6 jit_solution(8923637272299415587)
XLA Ops:
  0.9 6.5 reshape.763
  17.2 4.9 collective-permute-start.1
  33.5 4.6 fusion.61
  40.4 5.0 convert_element_type.789
  45.4 7.0 reshape_reshape.10
  52.4 6.1 copy.194
  58.5 4.8 copy.218
  72.4 17.8 %fusion.225 = (f32[2,4,1568]{2,1,0:T(4,128)S(1)}, f32[2,4,1568,784]{2,3,1,0:T(8,128)}) fusion(f32[784]{0:T(1024)S(1)} %add_select_fusion, bf16[2,1568,4,96]{1,3,2,0:T(8,128)(2,1)} %copy.194, bf16[2,784,4,96]{1,3,2,0:T(8,128)(2,1)S(1)} %bitcast.563), kind=kOutput, calls=%fused_computation.486 | convolution fusion | flops 1917714176 | bytes 43003968 | tf_op jit(solution)/shard_map/bnhd,bkhd->bhnk/dot_general | solution.py:64
  90.2 16.4 %fusion = f32[2,4,1568]{2,1,0:T(4,128)S(1)} fusion(f32[2,4,1568,784]{2,3,1,0:T(8,128)} %get-tuple-element.155, f32[2,4,1568]{2,1,0:T(4,128)S(1)} %get-tuple-element.154), kind=kLoop, calls=%fused_computation.6 | loop fusion | flops 19656448 | bytes 39438336 | tf_op jit(solution)/shard_map/reduce_sum | solution.py:70
  106.7 19.2 %fusion.36 = f32[2,1568,4,96]{1,3,2,0:T(8,128)} fusion(bf16[2,784,4,96]{1,3,2,0:T(8,128)(2,1)S(1)} %bitcast.588, f32[2,4,1568,784]{2,3,1,0:T(8,128)} %get-tuple-element.155, f32[2,4,1568]{2,1,0:T(4,128)S(1)} %fusion, f32[2,4,1568]{2,1,0:T(4,128)S(1)} %get-tuple-element.154), kind=kOutput, calls=%fused_computation.99 | convolution fusion | flops 1917726720 | bytes 45459456 | tf_op jit(solution)/shard_map/bhnk,bkhd->bnhd/dot_general | solution.py:71
  125.9 8.6 copy.217
  134.5 9.7 %reshape.788 = f32[2,4,392,384]{2,1,3,0:T(4,128)} reshape(f32[2,1568,4,96]{1,3,2,0:T(8,128)} %fusion.36) | data formatting | bytes 9633792 | tf_op jit(solution)/shard_map/reshape | solution.py:74
  144.2 7.3 copy.238
  151.5 6.5 fusion.226
  161.6 10.1 %multiply_convert_fusion.2 = (bf16[2,4,392,1536]{3,2,1,0:T(8,128)(2,1)S(1)}, f32[2,4,392,1536]{3,2,1,0:T(8,128)}) fusion(bf16[2,4,392,384]{3,2,1,0:T(8,128)(2,1)S(1)} %multiply_convert_fusion.7, bf16[384,1536]{1,0:T(8,128)(2,1)S(1)} %copy-done), kind=kOutput, calls=%fused_computation.25 | convolution fusion | flops 3723460608 | bytes 32489472 | tf_op jit(solution)/shard_map/...nc,cf->...nf/dot_general | solution.py:46
  171.7 5.5 fusion.227
  189.2 7.1 reshape.723
  196.3 4.3 copy.219
  206.4 13.5 %copy.220 = bf16[1536,3136]{1,0:T(8,128)(2,1)} copy(bf16[1536,3136]{0,1:T(8,128)(2,1)} %bitcast.550) | data formatting | bytes 19267584 | tf_op jit(solution)/shard_map/nc,nf->cf/dot_general | solution.py:56
  219.8 5.9 add_convert_fusion
  233.0 4.5 copy.198
  237.5 4.4 copy.197
  241.9 12.9 %fusion.24 = (f32[2,8,392]{2,1,0:T(8,128)S(1)}, f32[2,8,392,784]{3,2,1,0:T(8,128)}) fusion(f32[784]{0:T(1024)S(1)} %add_select_fusion, bf16[2,392,8,96]{1,3,2,0:T(8,128)(2,1)S(1)} %bitcast.555, bf16[2,784,8,96]{1,3,2,0:T(8,128)(2,1)} %bitcast.553), kind=kOutput, calls=%fused_computation.40 | convolution fusion | flops 958857088 | bytes 23309888 | tf_op jit(solution)/shard_map/bnhd,bkhd->bhnk/dot_general | solution.py:64
  254.9 11.1 %fusion.6 = f32[2,8,392]{2,1,0:T(8,128)S(1)} fusion(f32[2,8,392]{2,1,0:T(8,128)S(1)} %get-tuple-element.162, f32[784]{0:T(1024)S(1)} %add_select_fusion, f32[2,8,392,784]{3,2,1,0:T(8,128)} %get-tuple-element.163), kind=kLoop, calls=%fused_computation.18 | loop fusion | flops 19662720 | bytes 19722304 | tf_op jit(solution)/shard_map/reduce_sum | solution.py:70
  266.0 11.9 %fusion.17 = f32[2,8,96,392]{3,2,1,0:T(8,128)} fusion(bf16[2,784,8,96]{1,3,2,0:T(8,128)(2,1)S(1)} %bitcast.567, f32[2,8,392]{2,1,0:T(8,128)S(1)} %fusion.6, f32[2,8,392]{2,1,0:T(8,128)S(1)} %get-tuple-element.162, f32[2,8,392,784]{3,2,1,0:T(8,128)} %get-tuple-element.163, f32[784]{0:T(1024)S(1)} %add_select_fusion), kind=kOutput, calls=%fused_computation.31 | convolution fusion | flops 968697856 | bytes 24539200 | tf_op jit(solution)/shard_map/bhnk,bkhd->bnhd/dot_general | solution.py:71
  286.9 7.7 multiply_convert_fusion.3
  294.6 9.2 fusion.23
  303.8 4.9 multiply_reduce_fusion.13
  315.7 11.8 %fusion.58 = bf16[2,8,96,784]{3,2,1,0:T(8,128)(2,1)} fusion(bf16[2,392,8,96]{1,3,2,0:T(8,128)(2,1)} %bitcast.585, f32[2,8,392]{2,1,0:T(8,128)S(1)} %log_add_fusion.1, f32[784]{0:T(1024)S(1)} %add_select_fusion, f32[2,8,392,784]{3,2,1,0:T(8,128)} %get-tuple-element.163), kind=kOutput, calls=%fused_computation.139 | convolution fusion | flops 964984832 | bytes 23309888 | tf_op jit(solution)/shard_map/bhnk,bnhd->bkhd/dot_general | solution.py:86
  327.4 16.3 %multiply_reduce_fusion.1 = (f32[2,8,392]{2,1,0:T(8,128)S(1)}, f32[2,8,392,784]{3,2,1,0:T(8,128)}) fusion(f32[2,8,392]{2,1,0:T(8,128)S(1)} %log_add_fusion.1, f32[784]{0:T(1024)S(1)} %add_select_fusion, f32[2,8,392,784]{3,2,1,0:T(8,128)} %get-tuple-element.163, bf16[2,392,8,96]{1,3,2,0:T(8,128)(2,1)} %bitcast.586, bf16[2,784,8,96]{1,3,2,0:T(8,128)(2,1)} %bitcast.566), kind=kOutput, calls=%fused_computation.10 | convolution fusion | flops 968691584 | bytes 43003968 | tf_op jit(solution)/shard_map/bnhd,bkhd->bhnk/dot_general | solution.py:81
  343.8 20.7 %multiply_convert_fusion.1 = bf16[2,8,392,784]{3,2,1,0:T(8,128)(2,1)} fusion(f32[2,8,392,784]{3,2,1,0:T(8,128)} %get-tuple-element.170, f32[2,8,392]{2,1,0:T(8,128)S(1)} %get-tuple-element.169, f32[2,8,392]{2,1,0:T(8,128)S(1)} %log_add_fusion.1, f32[784]{0:T(1024)S(1)} %add_select_fusion, f32[2,8,392,784]{3,2,1,0:T(8,128)} %get-tuple-element.163), kind=kLoop, calls=%fused_computation.9 | loop fusion | flops 29503488 | bytes 49225792 | tf_op jit(solution)/shard_map/convert_element_type | solution.py:83
  364.5 9.4 convolution_multiply_fusion.1
  373.9 7.9 multiply_convert_fusion.4
  386.0 9.5 fusion.71
  401.4 4.4 copy.206
  405.8 7.6 copy.224
  413.4 7.4 fusion.238
  425.2 6.9 fusion.237
  437.8 4.5 copy.205
  466.0 8.0 collective-permute-done.5
  484.0 13.2 %fusion.12 = bf16[2,4,392,1536]{3,2,1,0:T(8,128)(2,1)S(1)} fusion(f32[2,4,392,1536]{3,2,1,0:T(8,128)} %get-tuple-element.159, bf16[2,4,392,384]{3,2,1,0:T(8,128)(2,1)S(1)} %fusion.37, bf16[1536,384]{1,0:T(8,128)(2,1)S(1)} %copy-done.161), kind=kOutput, calls=%fused_computation.24 | convolution fusion | flops 3747545088 | bytes 32489472 | tf_op jit(solution)/shard_map/...nf,cf->...nc/dot_general | solution.py:50
  497.3 7.3 multiply_reduce_fusion.5
  504.6 5.1 fusion.220
  514.3 4.5 copy.207
  518.7 18.3 %fusion.62 = bf16[2,4,96,784]{3,2,1,0:T(8,128)(2,1)} fusion(bf16[2,1568,4,96]{1,3,2,0:T(8,128)(2,1)} %bitcast.551, f32[2,4,1568,784]{2,3,1,0:T(8,128)} %get-tuple-element.155, f32[2,4,1568]{2,1,0:T(4,128)S(1)} %bitcast.592), kind=kOutput, calls=%fused_computation.156 | convolution fusion | flops 1908494336 | bytes 43000832 | tf_op jit(solution)/shard_map/bhnk,bnhd->bkhd/dot_general | solution.py:86
  537.1 27.0 %multiply_reduce_fusion = (f32[2,4,1568]{2,1,0:T(4,128)S(1)}, f32[2,4,1568,784]{2,3,1,0:T(8,128)}) fusion(f32[2,4,1568,784]{2,3,1,0:T(8,128)} %get-tuple-element.155, f32[2,4,1568]{2,1,0:T(4,128)S(1)} %bitcast.593, bf16[2,1568,4,96]{1,3,2,0:T(8,128)(2,1)} %bitcast.552, bf16[2,784,4,96]{1,3,2,0:T(8,128)(2,1)S(1)} %bitcast.589), kind=kOutput, calls=%fused_computation.1 | convolution fusion | flops 1917714176 | bytes 82388992 | tf_op jit(solution)/shard_map/bnhd,bkhd->bhnk/dot_general | solution.py:81
  564.1 33.6 %multiply_convert_fusion = bf16[2,4,1568,784]{2,3,1,0:T(8,128)(2,1)} fusion(f32[2,4,1568,784]{2,3,1,0:T(8,128)} %get-tuple-element.175, f32[2,4,1568,784]{2,3,1,0:T(8,128)} %get-tuple-element.155, f32[2,4,1568]{2,1,0:T(4,128)S(1)} %get-tuple-element.174, f32[2,4,1568]{2,1,0:T(4,128)S(1)} %bitcast.594), kind=kLoop, calls=%fused_computation | loop fusion | flops 39337984 | bytes 98445312 | tf_op jit(solution)/shard_map/convert_element_type | solution.py:83
  597.7 10.9 %multiply_convert_fusion.9 = bf16[2,4,96,784]{3,2,1,0:T(8,128)(2,1)S(1)} fusion(bf16[2,1568,4,96]{1,3,2,0:T(8,128)(2,1)S(1)} %copy-done.5, bf16[2,4,1568,784]{2,3,1,0:T(8,128)(2,1)} %multiply_convert_fusion), kind=kOutput, calls=%fused_computation.106 | convolution fusion | flops 1889427456 | bytes 23281664 | tf_op jit(solution)/shard_map/bhnk,bnhd->bkhd/dot_general | solution.py:85
  608.6 13.6 %convolution_multiply_fusion = f32[2,4,96,1568]{3,2,1,0:T(8,128)} fusion(bf16[2,784,4,96]{1,3,2,0:T(8,128)(2,1)S(1)} %bitcast.564, bf16[2,4,1568,784]{2,3,1,0:T(8,128)(2,1)} %multiply_convert_fusion), kind=kOutput, calls=%fused_computation.98 | convolution fusion | flops 1889427456 | bytes 25690112 | tf_op jit(solution)/shard_map/bhnk,bkhd->bnhd/dot_general | solution.py:84
  622.2 6.8 fusion.233
  633.7 5.9 copy.208
  639.6 5.1 add_convert_fusion.2
  658.8 5.4 fusion.234
  711.7 8.5 collective-permute-done.7
  722.9 5.0 bitcast_add_fusion
  730.5 6.7 add_convert_fusion.1
  742.5 40.2 %all-reduce = (f32[384]{0:T(512)}, f32[384]{0:T(512)}, f32[384]{0:T(512)}, f32[768]{0:T(1024)}) all-reduce(f32[384]{0:T(512)S(1)} %get-tuple-element.92, f32[384]{0:T(512)S(1)} %copy-done.142, f32[384]{0:T(512)S(1)} %copy-done.138, f32[768]{0:T(1024)S(1)} %copy-done.141), channel_id=1, replica_groups=mesh['group'=2,'clip'=8,'micro'=2] {'group','clip','micro'}, use_global_device_ids=true, to_apply=%region_25.26 | all-reduce | flops 1920 | bytes 15360 | tf_op jit(solution)/shard_map/psum | solution.py:224
  789.4 5.1 collective-permute-done.39
  819.2 4.6 collective-permute-done.42
  824.0 4.5 collective-permute-done.12
  867.0 4.2 collective-permute-done.35
  890.7 27.3 %collective-permute-done.37 = bf16[24,1152]{1,0:T(8,128)(2,1)} collective-permute-done((bf16[24,1152]{1,0:T(8,128)(2,1)}, bf16[24,1152]{1,0:T(8,128)(2,1)}, u32[]{:S(2)}, u32[]{:S(2)}) %collective-permute-start.37) | collective-permute-done | bytes 55328 | tf_op jit(solution)/shard_map/ppermute | solution.py:142
  943.5 5.0 collective-permute-done.53
  950.2 5.6 collective-permute-done.54
  (706 shorter events, 332.0 us)
Async XLA Ops:
  0.6 160.9 %copy-start = (bf16[384,1536]{1,0:T(8,128)(2,1)S(1)}, bf16[384,1536]{1,0:T(8,128)(2,1)}, u32[]{:S(2)}) copy-start(bf16[384,1536]{1,0:T(8,128)(2,1)} %param.23) | copy-start | bytes 3538948
  17.2 46.2 %collective-permute-start.1 = (bf16[2,196,384]{2,1,0:T(8,128)(2,1)}, bf16[2,196,384]{2,1,0:T(8,128)(2,1)S(1)}, u32[]{:S(2)}, u32[]{:S(2)}) collective-permute-start(bf16[2,196,384]{2,1,0:T(8,128)(2,1)} %fusion.81), channel_id=1, source_target_pairs={{0,4},{2,6},{4,8},{6,10},{8,12},{10,14},{1,5},{3,7},{5,9},{7,11},{... | collective-permute-start | bytes 903176 | tf_op jit(solution)/shard_map/ppermute | solution.py:27
  22.2 41.3 %collective-permute-start = (bf16[2,196,384]{2,1,0:T(8,128)(2,1)}, bf16[2,196,384]{2,1,0:T(8,128)(2,1)}, u32[]{:S(2)}, u32[]{:S(2)}) collective-permute-start(bf16[2,196,384]{2,1,0:T(8,128)(2,1)} %fusion.81), channel_id=1, source_target_pairs={{0,2},{2,4},{4,6},{6,8},{8,10},{10,12},{12,14},{1,3},{3,5},{5,7},{... | collective-permute-start | bytes 903176 | tf_op jit(solution)/shard_map/ppermute | solution.py:27
  181.5 44.9 %collective-permute-start.3 = (bf16[2,196,384]{2,1,0:T(8,128)(2,1)}, bf16[2,196,384]{2,1,0:T(8,128)(2,1)}, u32[]{:S(2)}, u32[]{:S(2)}) collective-permute-start(bf16[2,196,384]{2,1,0:T(8,128)(2,1)} %fusion.82), channel_id=1, source_target_pairs={{0,4},{2,6},{4,8},{6,10},{8,12},{10,14},{1,5},{3,7},{5,9},{7,11},{... | collective-permute-start | bytes 903176 | tf_op jit(solution)/shard_map/ppermute | solution.py:27
  185.0 41.4 %collective-permute-start.2 = (bf16[2,196,384]{2,1,0:T(8,128)(2,1)}, bf16[2,196,384]{2,1,0:T(8,128)(2,1)}, u32[]{:S(2)}, u32[]{:S(2)}) collective-permute-start(bf16[2,196,384]{2,1,0:T(8,128)(2,1)} %fusion.82), channel_id=1, source_target_pairs={{0,2},{2,4},{4,6},{6,8},{8,10},{10,12},{12,14},{1,3},{3,5},{5,7},{... | collective-permute-start | bytes 903176 | tf_op jit(solution)/shard_map/ppermute | solution.py:27
  397.2 65.4 %collective-permute-start.44 = (bf16[8,24,768]{2,1,0:T(8,128)(2,1)}, bf16[8,24,768]{2,1,0:T(8,128)(2,1)}, u32[]{:S(2)}, u32[]{:S(2)}) collective-permute-start(bf16[8,24,768]{2,1,0:T(8,128)(2,1)} %fusion.144), channel_id=1, source_target_pairs={{0,1},{1,0},{2,3},{3,2},{4,5},{5,4},{6,7},{7,6},{8,9},{9,8},{10,11... | collective-permute-start | bytes 884744 | tf_op jit(solution)/shard_map/ppermute | solution.py:121
  401.2 304.8 %collective-permute-start.38 = (bf16[8,48,768]{2,1,0:T(8,128)(2,1)}, bf16[8,48,768]{2,1,0:T(8,128)(2,1)}, u32[]{:S(2)}, u32[]{:S(2)}) collective-permute-start(bf16[8,48,768]{2,1,0:T(8,128)(2,1)} %fusion.111), channel_id=1, source_target_pairs={{0,1},{1,0},{2,3},{3,2},{4,5},{5,4},{6,7},{7,6},{8,9},{9,8},{10,11... | collective-permute-start | bytes 1769480 | tf_op jit(solution)/shard_map/ppermute | solution.py:121
  422.6 449.1 %collective-permute-start.56 = (bf16[8,192,768]{2,1,0:T(8,128)(2,1)}, bf16[8,192,768]{2,1,0:T(8,128)(2,1)}, u32[]{:S(2)}, u32[]{:S(2)}) collective-permute-start(bf16[8,192,768]{2,1,0:T(8,128)(2,1)} %fusion.47), channel_id=1, source_target_pairs={{0,1},{1,0},{2,3},{3,2},{4,5},{5,4},{6,7},{7,6},{8,9},{9,8},{10,11... | collective-permute-start | bytes 7077896 | tf_op jit(solution)/shard_map/ppermute | solution.py:121
  437.5 441.0 %collective-permute-start.50 = (bf16[8,48,3072]{2,1,0:T(8,128)(2,1)}, bf16[8,48,3072]{2,1,0:T(8,128)(2,1)}, u32[]{:S(2)}, u32[]{:S(2)}) collective-permute-start(bf16[8,48,3072]{2,1,0:T(8,128)(2,1)} %fusion.46), channel_id=1, source_target_pairs={{0,1},{1,0},{2,3},{3,2},{4,5},{5,4},{6,7},{7,6},{8,9},{9,8},{10,11... | collective-permute-start | bytes 7077896 | tf_op jit(solution)/shard_map/ppermute | solution.py:121
  452.9 12.9 %collective-permute-start.4 = (bf16[2,196,384]{2,1,0:T(8,128)(2,1)S(1)}, bf16[2,196,384]{2,1,0:T(8,128)(2,1)S(1)}, u32[]{:S(2)}, u32[]{:S(2)}) collective-permute-start(bf16[2,196,384]{2,1,0:T(8,128)(2,1)S(1)} %get-tuple-element.122), channel_id=1, source_target_pairs={{2,0},{4,2},{6,4},{8,6},{10,8},{12,10},{14,12},{3,1},{5,3},{7,5},{... | collective-permute-start | bytes 903176 | tf_op jit(solution)/shard_map/ppermute | solution.py:27
  462.6 11.4 %collective-permute-start.5 = (bf16[2,196,384]{2,1,0:T(8,128)(2,1)S(1)}, bf16[2,196,384]{2,1,0:T(8,128)(2,1)S(1)}, u32[]{:S(2)}, u32[]{:S(2)}) collective-permute-start(bf16[2,196,384]{2,1,0:T(8,128)(2,1)S(1)} %get-tuple-element.123), channel_id=1, source_target_pairs={{4,0},{6,2},{8,4},{10,6},{12,8},{14,10},{5,1},{7,3},{9,5},{11,7},{... | collective-permute-start | bytes 903176 | tf_op jit(solution)/shard_map/ppermute | solution.py:27
  465.8 318.5 %collective-permute-start.32 = (bf16[8,24,2304]{2,1,0:T(8,128)(2,1)}, bf16[8,24,2304]{2,1,0:T(8,128)(2,1)}, u32[]{:S(2)}, u32[]{:S(2)}) collective-permute-start(bf16[8,24,2304]{2,1,0:T(8,128)(2,1)} %fusion.98), channel_id=1, source_target_pairs={{0,1},{1,0},{2,3},{3,2},{4,5},{5,4},{6,7},{7,6},{8,9},{9,8},{10,11... | collective-permute-start | bytes 2654216 | tf_op jit(solution)/shard_map/ppermute | solution.py:121
  474.0 192.6 %collective-permute-start.45 = (bf16[8,24,384]{2,1,0:T(8,128)(2,1)}, bf16[8,24,384]{2,1,0:T(8,128)(2,1)}, u32[]{:S(2)}, u32[]{:S(2)}) collective-permute-start(bf16[8,24,384]{2,1,0:T(8,128)(2,1)} %fusion.175), channel_id=1, source_target_pairs={{0,16},{16,0},{1,17},{17,1},{2,18},{18,2},{3,19},{19,3},{4,20},{20... | collective-permute-start | bytes 442376 | tf_op jit(solution)/shard_map/ppermute | solution.py:121
  666.6 1.4 collective-permute-start.14
  668.0 4.9 collective-permute-start.46
  672.9 4.6 collective-permute-start.15
  677.5 4.0 collective-permute-start.47
  681.5 4.1 collective-permute-start.16
  685.6 3.9 collective-permute-start.17
  689.5 4.7 collective-permute-start.48
  694.2 4.6 collective-permute-start.18
  698.8 3.8 collective-permute-start.49
  702.5 9.2 collective-permute-start.6
  706.0 3.7 collective-permute-start.19
  709.7 10.5 %collective-permute-start.7 = (bf16[2,196,384]{2,1,0:T(8,128)(2,1)S(1)}, bf16[2,196,384]{2,1,0:T(8,128)(2,1)S(1)}, u32[]{:S(2)}, u32[]{:S(2)}) collective-permute-start(bf16[2,196,384]{2,1,0:T(8,128)(2,1)S(1)} %copy-done.85), channel_id=1, source_target_pairs={{4,0},{6,2},{8,4},{10,6},{12,8},{14,10},{5,1},{7,3},{9,5},{11,7},{... | collective-permute-start | bytes 903176 | tf_op jit(solution)/shard_map/ppermute | solution.py:27
  711.7 84.7 %collective-permute-start.20 = (bf16[8,24,1536]{2,1,0:T(8,128)(2,1)}, bf16[8,24,1536]{2,1,0:T(8,128)(2,1)}, u32[]{:S(2)}, u32[]{:S(2)}) collective-permute-start(bf16[8,24,1536]{2,1,0:T(8,128)(2,1)} %fusion.109), channel_id=1, source_target_pairs={{0,1},{1,0},{2,3},{3,2},{4,5},{5,4},{6,7},{7,6},{8,9},{9,8},{10,11... | collective-permute-start | bytes 1769480 | tf_op jit(solution)/shard_map/ppermute | solution.py:121
  720.2 62.4 %collective-permute-start.8 = (bf16[8,24,1152]{2,1,0:T(8,128)(2,1)}, bf16[8,24,1152]{2,1,0:T(8,128)(2,1)}, u32[]{:S(2)}, u32[]{:S(2)}) collective-permute-start(bf16[8,24,1152]{2,1,0:T(8,128)(2,1)} %fusion.140), channel_id=1, source_target_pairs={{0,1},{1,0},{2,3},{3,2},{4,5},{5,4},{6,7},{7,6},{8,9},{9,8},{10,11... | collective-permute-start | bytes 1327112 | tf_op jit(solution)/shard_map/ppermute | solution.py:121
  740.7 42.0 %copy-start.33 = (f32[384,1152]{1,0:T(8,128)S(1)}, f32[384,1152]{1,0:T(8,128)}, u32[]{:S(2)}) copy-start(f32[384,1152]{1,0:T(8,128)} %copy-done.32) | copy-start | bytes 5308420
  782.7 15.6 %collective-permute-start.26 = (bf16[8,96,384]{2,1,0:T(8,128)(2,1)}, bf16[8,96,384]{2,1,0:T(8,128)(2,1)S(1)}, u32[]{:S(2)}, u32[]{:S(2)}) collective-permute-start(bf16[8,96,384]{2,1,0:T(8,128)(2,1)} %fusion.110), channel_id=1, source_target_pairs={{0,1},{1,0},{2,3},{3,2},{4,5},{5,4},{6,7},{7,6},{8,9},{9,8},{10,11... | collective-permute-start | bytes 1769480 | tf_op jit(solution)/shard_map/ppermute | solution.py:121
  784.3 10.2 %collective-permute-start.39 = (bf16[8,48,384]{2,1,0:T(8,128)(2,1)S(1)}, bf16[8,48,384]{2,1,0:T(8,128)(2,1)S(1)}, u32[]{:S(2)}, u32[]{:S(2)}) collective-permute-start(bf16[8,48,384]{2,1,0:T(8,128)(2,1)S(1)} %copy-done.86), channel_id=1, source_target_pairs={{0,16},{16,0},{1,17},{17,1},{2,18},{18,2},{3,19},{19,3},{4,20},{20... | collective-permute-start | bytes 884744 | tf_op jit(solution)/shard_map/ppermute | solution.py:121
  794.5 8.9 collective-permute-start.9
  796.4 51.2 %collective-permute-start.33 = (bf16[8,24,1152]{2,1,0:T(8,128)(2,1)}, bf16[8,24,1152]{2,1,0:T(8,128)(2,1)}, u32[]{:S(2)}, u32[]{:S(2)}) collective-permute-start(bf16[8,24,1152]{2,1,0:T(8,128)(2,1)} %fusion.141), channel_id=1, source_target_pairs={{0,16},{16,0},{1,17},{17,1},{2,18},{18,2},{3,19},{19,3},{4,20},{20... | collective-permute-start | bytes 1327112 | tf_op jit(solution)/shard_map/ppermute | solution.py:121
  798.3 7.0 collective-permute-start.40
  803.4 31.8 %collective-permute-start.21 = (bf16[8,24,768]{2,1,0:T(8,128)(2,1)}, bf16[8,24,768]{2,1,0:T(8,128)(2,1)}, u32[]{:S(2)}, u32[]{:S(2)}) collective-permute-start(bf16[8,24,768]{2,1,0:T(8,128)(2,1)} %fusion.147), channel_id=1, source_target_pairs={{0,16},{16,0},{1,17},{17,1},{2,18},{18,2},{3,19},{19,3},{4,20},{20... | collective-permute-start | bytes 884744 | tf_op jit(solution)/shard_map/ppermute | solution.py:121
  805.3 4.9 collective-permute-start.10
  810.3 4.4 collective-permute-start.41
  814.6 4.2 collective-permute-start.11
  818.8 4.9 collective-permute-start.42
  823.7 4.8 collective-permute-start.12
  828.5 4.0 collective-permute-start.43
  832.5 8.1 collective-permute-start.27
  835.2 9.5 collective-permute-start.13
  840.6 9.8 %collective-permute-start.22 = (bf16[4,24,768]{2,1,0:T(8,128)(2,1)}, bf16[4,24,768]{2,1,0:T(8,128)(2,1)}, u32[]{:S(2)}, u32[]{:S(2)}) collective-permute-start(bf16[4,24,768]{2,1,0:T(8,128)(2,1)} %fusion.171), channel_id=1, source_target_pairs={{0,2},{2,0},{4,6},{6,4},{8,10},{10,8},{12,14},{14,12},{1,3},{3,1},... | collective-permute-start | bytes 442376 | tf_op jit(solution)/shard_map/ppermute | solution.py:121
  844.7 6.7 collective-permute-start.28
  849.0 17.4 %collective-permute-start.34 = (bf16[4,24,1152]{2,1,0:T(8,128)(2,1)S(1)}, bf16[4,24,1152]{2,1,0:T(8,128)(2,1)S(1)}, u32[]{:S(2)}, u32[]{:S(2)}) collective-permute-start(bf16[4,24,1152]{2,1,0:T(8,128)(2,1)S(1)} %fusion.162), channel_id=1, source_target_pairs={{0,2},{2,0},{4,6},{6,4},{8,10},{10,8},{12,14},{14,12},{1,3},{3,1},... | collective-permute-start | bytes 663560 | tf_op jit(solution)/shard_map/ppermute | solution.py:121
  851.4 4.9 collective-permute-start.23
  852.5 4.8 collective-permute-start.29
  856.3 5.3 collective-permute-start.24
  857.3 5.1 collective-permute-start.30
  861.6 4.0 collective-permute-start.25
  862.4 4.6 collective-permute-start.31
  866.4 4.8 collective-permute-start.35
  871.3 13.9 %collective-permute-start.36 = (bf16[1,24,1152]{2,1,0:T(8,128)(2,1)S(1)}, bf16[1,24,1152]{2,1,0:T(8,128)(2,1)S(1)}, u32[]{:S(2)}, u32[]{:S(2)}) collective-permute-start(bf16[1,24,1152]{2,1,0:T(8,128)(2,1)S(1)} %dynamic-slice_convert_fusion.26), channel_id=1, source_target_pairs={{0,8},{2,10},{4,12},{6,14},{8,0},{10,2},{12,4},{14,6},{1,9},{3,11}... | collective-permute-start | bytes 165896 | tf_op jit(solution)/shard_map/ppermute | solution.py:121
  877.7 41.2 %collective-permute-start.57 = (bf16[8,192,384]{2,1,0:T(8,128)(2,1)}, bf16[8,192,384]{2,1,0:T(8,128)(2,1)}, u32[]{:S(2)}, u32[]{:S(2)}) collective-permute-start(bf16[8,192,384]{2,1,0:T(8,128)(2,1)} %fusion.84), channel_id=1, source_target_pairs={{0,16},{16,0},{1,17},{17,1},{2,18},{18,2},{3,19},{19,3},{4,20},{20... | collective-permute-start | bytes 3538952 | tf_op jit(solution)/shard_map/ppermute | solution.py:121
  884.1 39.1 %collective-permute-start.51 = (bf16[8,48,1536]{2,1,0:T(8,128)(2,1)}, bf16[8,48,1536]{2,1,0:T(8,128)(2,1)}, u32[]{:S(2)}, u32[]{:S(2)}) collective-permute-start(bf16[8,48,1536]{2,1,0:T(8,128)(2,1)} %fusion.83), channel_id=1, source_target_pairs={{0,16},{16,0},{1,17},{17,1},{2,18},{18,2},{3,19},{19,3},{4,20},{20... | collective-permute-start | bytes 3538952 | tf_op jit(solution)/shard_map/ppermute | solution.py:121
  885.9 32.2 %collective-permute-start.37 = (bf16[24,1152]{1,0:T(8,128)(2,1)}, bf16[24,1152]{1,0:T(8,128)(2,1)}, u32[]{:S(2)}, u32[]{:S(2)}) collective-permute-start(bf16[24,1152]{1,0:T(8,128)(2,1)} %fusion.184), channel_id=1, source_target_pairs={{0,16},{16,0},{1,17},{17,1},{2,18},{18,2},{3,19},{19,3},{4,20},{20... | collective-permute-start | bytes 165896 | tf_op jit(solution)/shard_map/ppermute | solution.py:142
  922.4 10.2 %collective-permute-start.58 = (bf16[4,192,384]{2,1,0:T(8,128)(2,1)}, bf16[4,192,384]{2,1,0:T(8,128)(2,1)}, u32[]{:S(2)}, u32[]{:S(2)}) collective-permute-start(bf16[4,192,384]{2,1,0:T(8,128)(2,1)} %fusion.113), channel_id=1, source_target_pairs={{0,2},{2,0},{4,6},{6,4},{8,10},{10,8},{12,14},{14,12},{1,3},{3,1},... | collective-permute-start | bytes 1769480 | tf_op jit(solution)/shard_map/ppermute | solution.py:121
  926.0 12.9 %collective-permute-start.52 = (bf16[4,48,1536]{2,1,0:T(8,128)(2,1)}, bf16[4,48,1536]{2,1,0:T(8,128)(2,1)}, u32[]{:S(2)}, u32[]{:S(2)}) collective-permute-start(bf16[4,48,1536]{2,1,0:T(8,128)(2,1)} %fusion.112), channel_id=1, source_target_pairs={{0,2},{2,0},{4,6},{6,4},{8,10},{10,8},{12,14},{14,12},{1,3},{3,1},... | collective-permute-start | bytes 1769480 | tf_op jit(solution)/shard_map/ppermute | solution.py:121
  934.2 7.7 collective-permute-start.59
  940.2 8.4 collective-permute-start.53
  942.0 7.5 collective-permute-start.60
  948.6 7.2 collective-permute-start.54
  949.5 7.0 collective-permute-start.61
  955.9 5.2 collective-permute-start.55
  (180 other events, 1348.6 us)

commit v2 on v1

v2 whole, which is shorter than its diff:
```python
from functools import partial

import jax
import jax.numpy as jnp
from jax import lax
from jax.experimental import pallas as pl
from jax.experimental.pallas import tpu as pltpu
from jax.sharding import PartitionSpec as P

D1 = 384
D2 = 768
F1 = 1536
F2 = 3072
QT = 1568
PT = 392
MT = 196
HD = 96
FR = 8
HT = 14
WD = 14
H1 = 4
H2 = 8
CELL = (HT // 2) * (WD // 2)
LANE = 128
PR = 400
MR = 208
KR = PR + 2 * MR
TILE = 224
STEPS = QT // TILE
W1 = H1 * LANE
W2 = H2 * LANE
epsilon = 1e-06
f32 = jnp.float32
bf16 = jnp.bfloat16
SCALE = HD ** (-0.5)
RATE = SCALE * 1.4426950408889634
VMEM = pltpu.VMEM


def mm(a, b):
    return lax.dot_general(a, b, (((1,), (0,)), ((), ())), preferred_element_type=f32)


def mm_nt(a, b):
    return lax.dot_general(a, b, (((1,), (1,)), ((), ())), preferred_element_type=f32)


def mm_tn(a, b):
    return lax.dot_general(a, b, (((0,), (0,)), ((), ())), preferred_element_type=f32)


def lanes(shape):
    return lax.broadcasted_iota(jnp.int32, shape, len(shape) - 1)


def rows_of(shape):
    return lax.broadcasted_iota(jnp.int32, shape, len(shape) - 2)


def norm_stats(values):
    center = values - jnp.mean(values, axis=-1, keepdims=True)
    inv = lax.rsqrt(jnp.mean(center * center, axis=-1, keepdims=True) + epsilon)
    return (center * inv, inv)


def norm_back(grad, unit, inv, gain):
    du = grad * gain
    dg = jnp.sum(grad * unit, axis=0, keepdims=True)
    dx = inv * (
        du - jnp.mean(du, axis=-1, keepdims=True) - unit * jnp.mean(du * unit, axis=-1, keepdims=True)
    )
    return (dx, dg)


def gelu_both(x):
    z = jnp.abs(x)
    t = 1.0 / (1.0 + 0.23164188 * z)
    e = jnp.exp2(x * x * -0.7213475204444817)
    poly = t * (0.127414796 + t * (-0.142248368 + t * (0.7107068705 + t * (-0.7265760135 + t * 0.5307027145))))
    tail = poly * e
    phi = jnp.where(x >= 0.0, 1.0 - tail, tail)
    return (x * phi, phi + (x * 0.3989422804014327) * e)


def split3(v):
    hi = v.astype(bf16).astype(f32)
    mid = (v - hi).astype(bf16).astype(f32)
    return (hi, mid, v - hi - mid)


def put3(base, v):
    hi, mid, low = split3(v)
    lane = lanes(base.shape)
    return jnp.where(
        lane < HD, base, jnp.where(lane == HD, hi, jnp.where(lane == HD + 1, mid, jnp.where(lane == HD + 2, low, base)))
    )


def tmean_matrix():
    rows = rows_of((MR, PR))
    cols = lanes((MR, PR))
    hit = rows < 0
    for pair in range(FR // 2):
        inside = (rows >= pair * CELL) & (rows < (pair + 1) * CELL)
        shift_by = cols - rows - pair * CELL
        hit = hit | (inside & ((shift_by == 0) | (shift_by == CELL)))
    return jnp.where(hit, 0.5, 0.0).astype(bf16)


def pool_rows(ref):
    total = ref[0:PT, :] + ref[PT : 2 * PT, :] + ref[2 * PT : 3 * PT, :] + ref[3 * PT : 4 * PT, :]
    return jnp.concatenate([0.25 * total, jnp.zeros((PR - PT, total.shape[1]), f32)], axis=0).astype(bf16)


def call(kernel, grid, ins, outs, scratch=(), flops=0, name=None):
    arrays = [a for a, _ in ins]
    moved = sum(a.size * a.dtype.itemsize for a in arrays) + sum(s.size * s.dtype.itemsize for s, _ in outs)
    return pl.pallas_call(
        kernel,
        grid=grid,
        in_specs=[s for _, s in ins],
        out_specs=[s for _, s in outs],
        out_shape=[o for o, _ in outs],
        scratch_shapes=list(scratch),
        compiler_params=pltpu.CompilerParams(
            vmem_limit_bytes=58 * 1024 * 1024, dimension_semantics=("arbitrary",) * len(grid)
        ),
        cost_estimate=pl.CostEstimate(flops=int(flops), bytes_accessed=int(moved), transcendentals=0),
        name=name,
    )(*arrays)


def whole(array):
    return (array, pl.BlockSpec(array.shape, lambda i: (0,) * array.ndim))


def rows_tiled(array, tile=TILE):
    return (array, pl.BlockSpec((tile, array.shape[1]), lambda i: (i, 0)))


def cols_tiled(array, tile, first=0):
    return (array, pl.BlockSpec((array.shape[0], tile), lambda i: (0, i + first)))


def shape_of(shape, dtype):
    return jax.ShapeDtypeStruct(shape, dtype)


def pad_kernel(wa, pa, wc, pc, wa_out, pa_out, wc_out, pc_out):
    for src, dst in ((wa, wa_out), (wc, wc_out)):
        blank = jnp.zeros((src.shape[0], LANE - HD), bf16)
        for j in range(src.shape[1] // HD):
            dst[:, LANE * j : LANE * (j + 1)] = jnp.concatenate([src[:, HD * j : HD * (j + 1)], blank], axis=1)
    for src, dst in ((pa, pa_out), (pc, pc_out)):
        blank = jnp.zeros((LANE - HD, src.shape[1]), bf16)
        for j in range(src.shape[0] // HD):
            dst[LANE * j : LANE * j + HD, :] = src[HD * j : HD * (j + 1), :]
            dst[LANE * j + HD : LANE * (j + 1), :] = blank


def pad_weights(w_qkv1, w_proj1, w_qkv2, w_proj2):
    outs = [
        shape_of((D1, 3 * W1), bf16),
        shape_of((W1, D1), bf16),
        shape_of((D1, 3 * W2), bf16),
        shape_of((W2, D2), bf16),
    ]
    return call(
        pad_kernel,
        (1,),
        [whole(w) for w in (w_qkv1, w_proj1, w_qkv2, w_proj2)],
        [whole(o) for o in outs],
        name="pad_heads",
    )


def source_of(rows_shape, start):
    r = rows_of(rows_shape)
    s = r // 56
    p = r - s * 56 + start
    f = p // CELL
    rest = p - f * CELL
    r2 = rest // 7
    c2 = rest - r2 * 7
    a = s // 2
    return f * (HT * WD) + r2 * (2 * WD) + a * WD + c2 * 2 + (s - 2 * a)


def first_kernel(x, gain, xp, na, kv, mem, xs):
    for i in range(7):
        lo = 196 * i // 16 * 16
        hi = min(QT, (196 * i + 392 + 15) // 16 * 16)
        shape = (TILE, hi - lo)
        pick = jnp.where(source_of(shape, 56 * i) == lanes(shape) + lo, 1.0, 0.0).astype(bf16)
        out = mm(pick, x[0, 0, 0, lo:hi, :])
        for s in range(4):
            xs[PT * s + 56 * i : PT * s + 56 * (i + 1), :] = out[56 * s : 56 * (s + 1)]
    for i in range(STEPS):
        at = slice(TILE * i, TILE * (i + 1))
        v = xs[at, :]
        unit, _ = norm_stats(v)
        n = (unit * gain[...]).astype(bf16)
        xp[at, :] = v.astype(bf16)
        na[at, :] = n
        xs[at, :] = n.astype(f32)
    pooled = pool_rows(xs)
    kv[...] = pooled
    mem[...] = mm(tmean_matrix(), pooled).astype(bf16)


def first(inputs, video, gain):
    outs = [
        shape_of((QT, D1), bf16),
        shape_of((QT, D1), bf16),
        shape_of((PR, D1), bf16),
        shape_of((MR, D1), bf16),
    ]
    x_spec = pl.BlockSpec((1, 1, 1, QT, D1), lambda i: (0, video, 0, 0, 0))
    return call(
        first_kernel,
        (1,),
        [(inputs, x_spec), whole(gain)],
        [whole(o) for o in outs],
        [VMEM((QT, D1), f32)],
        flops=2 * QT * 416 * D1,
        name="first_norm",
    )


def keys_ext(kall, wk, wv, kext, heads, k_out, v_out):
    k = mm(kall, wk)
    v = mm(kall, wv)
    lane = lanes((KR, LANE))
    ones = jnp.where((lane >= HD) & (lane < HD + 3), 1.0, 0.0)
    for h in range(heads):
        at = slice(LANE * h, LANE * (h + 1))
        k_out[:, at] = (k[:, at] + kext).astype(bf16)
        v_out[:, at] = (v[:, at] + ones).astype(bf16)


def head_forward(q, k, v):
    s = mm_nt(q, k)
    top = jnp.max(s, axis=-1, keepdims=True)
    e = jnp.exp2((s - top) * RATE).astype(bf16)
    mixed = mm(e, v)
    total = mixed[:, HD : HD + 1]
    lse = top + jnp.log(total) * (1.0 / SCALE)
    return (mixed * (1.0 / total), put3(q.astype(f32), -lse).astype(bf16))


def one_lane(shape):
    return jnp.where(lanes(shape) % LANE == HD + 3, 1.0, 0.0)


def block1_kernel(
    kv, near, far, kext, na, xp, wq, wk, wv, wp, gain_m, wfc, wout, gain_c,
    kall, k_out, v_out, qe, o_out, za, ha_out, nb_out, ub_out, gp_out, mid_out, pc, mem, xs,
):
    step = pl.program_id(0)

    @pl.when(step == 0)
    def _():
        kall[0:PR, :] = kv[...]
        kall[PR : PR + MR, :] = near[...]
        kall[PR + MR : KR, :] = far[...]
        keys_ext(kall[...], wk[...], wv[...], kext[...], H1, k_out, v_out)

    q = (mm(na[...], wq[...]) + one_lane((TILE, W1))).astype(bf16)
    for h in range(H1):
        at = slice(LANE * h, LANE * (h + 1))
        o, qx = head_forward(q[:, at], k_out[:, at], v_out[:, at])
        qe[:, at] = qx
        o_out[:, at] = o.astype(bf16)
        za[:, at] = (o + q[:, at].astype(f32)).astype(bf16)
    ha = xp[...].astype(f32) + mm(za[...], wp[...])
    ha_out[...] = ha
    unit, _ = norm_stats(ha)
    nb = (unit * gain_m[...]).astype(bf16)
    nb_out[...] = nb
    part = F1 // 3
    mid = ha
    for j in range(3):
        at = slice(part * j, part * (j + 1))
        act, slope = gelu_both(mm(nb, wfc[:, at]))
        act = act.astype(bf16)
        ub_out[:, at] = act
        gp_out[:, at] = slope.astype(bf16)
        mid = mid + mm(act, wout[at, :])
    mid_out[...] = mid
    unit, _ = norm_stats(mid)
    xs[pl.ds(pl.multiple_of(step * TILE, TILE), TILE), :] = (unit * gain_c[...]).astype(bf16).astype(f32)

    @pl.when(step == STEPS - 1)
    def _():
        pooled = pool_rows(xs)
        pc[...] = pooled
        mem[...] = mm(tmean_matrix(), pooled).astype(bf16)


def block1(kv, near, far, kext, na, xp, w, wp, gain_m, wfc, wout, gain_c):
    ins = [whole(kv), whole(near), whole(far), whole(kext), rows_tiled(na), rows_tiled(xp)]
    ins += [cols_fixed(w, W1, j) for j in range(3)]
    ins += [whole(wp), whole(gain_m), whole(wfc), whole(wout), whole(gain_c)]
    outs = [
        whole(shape_of((KR, D1), bf16)),
        whole(shape_of((KR, W1), bf16)),
        whole(shape_of((KR, W1), bf16)),
        rows_tiled(shape_of((QT, W1), bf16)),
        rows_tiled(shape_of((QT, W1), bf16)),
        rows_tiled(shape_of((QT, W1), bf16)),
        rows_tiled(shape_of((QT, D1), f32)),
        rows_tiled(shape_of((QT, D1), bf16)),
        rows_tiled(shape_of((QT, F1), bf16)),
        rows_tiled(shape_of((QT, F1), bf16)),
        rows_tiled(shape_of((QT, D1), f32)),
        whole(shape_of((PR, D1), bf16)),
        whole(shape_of((MR, D1), bf16)),
    ]
    flops = 2 * QT * (D1 * W1 * 2 + 2 * D1 * F1 + 4 * KR * W1)
    return call(block1_kernel, (STEPS,), ins, outs, [VMEM((QT, D1), f32)], flops=flops, name="block1_forward")


def cols_fixed(array, tile, at):
    return (array, pl.BlockSpec((array.shape[0], tile), lambda i: (0, at)))


PAIR = 2 * LANE


def block2_kernel(pc, near, far, kext, wq, wk, wv, wskip, wp, kall, k_out, v_out, qe, o_out, zc, hc):
    @pl.when(pl.program_id(0) == 0)
    def _():
        kall[0:PR, :] = pc[...]
        kall[PR : PR + MR, :] = near[...]
        kall[PR + MR : KR, :] = far[...]
        hc[...] = mm(pc[...], wskip[...])

    keys_ext(kall[...], wk[...], wv[...], kext[...], 2, k_out, v_out)
    q = (mm(pc[...], wq[...]) + one_lane((PR, PAIR))).astype(bf16)
    for h in range(2):
        at = slice(LANE * h, LANE * (h + 1))
        o, qx = head_forward(q[:, at], k_out[:, at], v_out[:, at])
        qe[:, at] = qx
        o_out[:, at] = o.astype(bf16)
        zc[:, at] = (o + q[:, at].astype(f32)).astype(bf16)
    hc[...] += mm(zc[...], wp[...])


def block2(pc, near, far, kext, w, wskip, wp):
    pairs = H2 // 2
    ins = [whole(pc), whole(near), whole(far), whole(kext)]
    ins += [cols_tiled(w, PAIR, j * pairs) for j in range(3)]
    ins += [whole(wskip), rows_tiled(wp, PAIR)]
    outs = [whole(shape_of((KR, D1), bf16))]
    outs += [cols_tiled(shape_of((n, W2), bf16), PAIR) for n in (KR, KR, PR, PR, PR)]
    outs += [whole(shape_of((PR, D2), f32))]
    flops = 2 * (PR * D1 * (W2 + D2) + 2 * KR * D1 * W2 + PR * W2 * D2 + 4 * PR * KR * W2)
    return call(block2_kernel, (pairs,), ins, outs, flops=flops, name="block2_attention")


PART = 768


def pick_share(micro, even, odd):
    first_ = micro == 0
    return (jnp.where(first_, even, odd).astype(bf16), jnp.where(first_, odd, even).astype(bf16))


def mlp2_kernel(micro, h0, h1, cot, gain, wfc, wout, out, gh, keep_fc, send_fc, keep_out, send_out, gg, hs, nd, ndt, gm, acc, dn):
    step = pl.program_id(0)

    @pl.when(step == 0)
    def _():
        blank = jnp.zeros((PR - PT, D2), f32)
        for b, h in enumerate((h0, h1)):
            at = slice(PR * b, PR * (b + 1))
            v = h[...]
            hs[at, :] = v
            unit, _ = norm_stats(v)
            nd[at, :] = (unit * gain[...]).astype(bf16)
            g = cot[0, b, 0].astype(f32)
            gm[at, :] = jnp.concatenate([g, blank], axis=0).astype(bf16)
        ndt[...] = nd[...].T

    act, slope = gelu_both(mm(nd[...], wfc[...]))
    act = act.astype(bf16)
    gi = (slope * mm_nt(gm[...], wout[...])).astype(bf16)
    m = micro[0]
    gw = mm_tn(act, gm[...])
    rows = keep_fc.shape[1]
    for i in range(keep_out.shape[0]):
        keep, send = pick_share(m, gw[8 * rows * i : 8 * rows * i + 4 * rows], gw[8 * rows * i + 4 * rows : 8 * rows * (i + 1)])
        for a in range(4):
            keep_out[i, :, D2 * a : D2 * (a + 1)] = keep[rows * a : rows * (a + 1)]
            send_out[i, :, D2 * a : D2 * (a + 1)] = send[rows * a : rows * (a + 1)]
    gw = mm(ndt[...], gi)
    for i in range(keep_fc.shape[0]):
        keep, send = pick_share(m, gw[2 * rows * i : 2 * rows * i + rows], gw[2 * rows * i + rows : 2 * rows * (i + 1)])
        keep_fc[i] = keep
        send_fc[i] = send
    o = mm(act, wout[...])
    d = mm_nt(gi, wfc[...])

    @pl.when(step == 0)
    def _():
        acc[...] = o
        dn[...] = d

    @pl.when(step > 0)
    def _():
        acc[...] += o
        dn[...] += d

    @pl.when(step == F2 // PART - 1)
    def _():
        v = hs[...]
        y = v + acc[...]
        unit, inv = norm_stats(v)
        dx, dg = norm_back(dn[...], unit, inv, gain[...])
        gg[...] = dg
        g = (gm[...].astype(f32) + dx).astype(bf16)
        for b in range(2):
            out[0, b, 0] = y[PR * b : PR * b + PT].astype(bf16)
            gh[b] = g[PR * b : PR * (b + 1)]


def scalar(value):
    return (value.astype(jnp.int32).reshape(1), pl.BlockSpec(memory_space=pltpu.SMEM))


def mlp2(micro, clips, h0, h1, cot, gain, wfc, wout):
    rows = D2 // (2 * clips)
    steps = F2 // PART
    ins = [scalar(micro), whole(h0), whole(h1), whole(cot), whole(gain), cols_tiled(wfc, PART), rows_tiled(wout, PART)]
    share = shape_of((clips, rows, F2), bf16)
    fc_spec = (share, pl.BlockSpec((clips, rows, PART), lambda i: (0, 0, i)))
    out_spec = (share, pl.BlockSpec((clips // steps, rows, F2), lambda i: (i, 0, 0)))
    outs = [
        whole(shape_of(cot.shape, bf16)),
        whole(shape_of((2, PR, D2), bf16)),
        fc_spec,
        fc_spec,
        out_spec,
        out_spec,
        whole(shape_of((1, D2), f32)),
    ]
    n = 2 * PR
    scratch = [
        VMEM((n, D2), f32),
        VMEM((n, D2), bf16),
        VMEM((D2, n), bf16),
        VMEM((n, D2), bf16),
        VMEM((n, D2), f32),
        VMEM((n, D2), f32),
    ]
    return call(mlp2_kernel, (steps,), ins, outs, scratch, flops=12 * n * D2 * F2, name="block2_mlp")


def head_backward(q, g, k, v, tiles):
    kt = k.T
    dk = jnp.zeros((KR, LANE), f32)
    dv = jnp.zeros((KR, LANE), f32)
    dqs = []
    for at in tiles:
        p = jnp.exp2(mm_nt(k, q[at]) * RATE)
        ds = (p * mm_nt(v, g[at])).astype(bf16)
        dv = dv + mm(p.astype(bf16), g[at])
        dk = dk + mm(ds, q[at])
        dqs.append((mm(kt, ds) * SCALE).T)
    return (dqs, dk * SCALE, dv)


def grad_ext(gz, o):
    delta = jnp.sum(jnp.where(lanes(gz.shape) < HD, gz.astype(f32) * o.astype(f32), 0.0), axis=-1, keepdims=True)
    return put3(gz.astype(f32), -delta).astype(bf16)


def att2_back_kernel(carry, *refs):
    n_in = 15 + (5 if carry else 0)
    gh, wp, qe, o, k, v, zc, pc, kall, wskip, wq, wk, wv, _, _ = refs[:15]
    before = refs[15:n_in]
    dnear, dfar, dpc, gq_w, gk_w, gv_w, gp_w, gs_w, dkv = refs[n_in:]
    step = pl.program_id(0)

    def out(ref, value, i):
        ref[...] = value + before[i][...] if carry else value

    @pl.when(step == 0)
    def _():
        dpc[...] = mm_nt(gh[0], wskip[...])
        out(gs_w, mm_tn(pc[...], gh[0]), 4)
        dkv[...] = jnp.zeros_like(dkv)

    gz = mm_nt(gh[0], wp[...]).astype(bf16)
    out(gp_w, mm_tn(zc[...], gh[0]), 3)
    gq, dk, dv = [], [], []
    for h in range(2):
        at = slice(LANE * h, LANE * (h + 1))
        g = grad_ext(gz[:, at], o[:, at])
        dqs, dkh, dvh = head_backward(qe[:, at], g, k[:, at], v[:, at], [slice(0, PR)])
        gq.append((gz[:, at].astype(f32) + dqs[0]).astype(bf16))
        dk.append(dkh.astype(bf16))
        dv.append(dvh.astype(bf16))
    gq = jnp.concatenate(gq, axis=1)
    dk = jnp.concatenate(dk, axis=1)
    dv = jnp.concatenate(dv, axis=1)
    dpc[...] += mm_nt(gq, wq[...])
    dkv[...] += mm_nt(dk, wk[...]) + mm_nt(dv, wv[...])
    out(gq_w, mm_tn(pc[...], gq), 0)
    out(gk_w, mm_tn(kall[...], dk), 1)
    out(gv_w, mm_tn(kall[...], dv), 2)

    @pl.when(step == H2 // 2 - 1)
    def _():
        dpc[...] += dkv[0:PR, :]
        dnear[...] = dkv[PR : PR + MR, :].astype(bf16)
        dfar[...] = dkv[PR + MR : KR, :].astype(bf16)


def att2_back(video, gh, wp, qe, o, k, v, zc, pc, kall, wskip, w, before):
    pairs = H2 // 2
    ins = [(gh, pl.BlockSpec((1, PR, D2), lambda i: (video, 0, 0))), rows_tiled(wp, PAIR)]
    ins += [cols_tiled(a, PAIR) for a in (qe, o, k, v, zc)]
    ins += [whole(pc), whole(kall), whole(wskip)]
    ins += [cols_tiled(w, PAIR, j * pairs) for j in range(3)]
    tiny = jnp.zeros((8, LANE), f32)
    ins += [whole(tiny), whole(tiny)]
    grads = [cols_tiled(shape_of((D1, W2), f32), PAIR) for _ in range(3)]
    grads += [rows_tiled(shape_of((W2, D2), f32), PAIR), whole(shape_of((D1, D2), f32))]
    if before is not None:
        ins += [(b, s) for b, (_, s) in zip(before, grads)]
    outs = [
        whole(shape_of((MR, D1), bf16)),
        whole(shape_of((MR, D1), bf16)),
        whole(shape_of((PR, D1), f32)),
    ] + grads
    flops = 2 * (10 * PR * KR * W2 + 4 * PR * D1 * W2 + 4 * KR * D1 * W2 + 4 * PR * W2 * D2)
    return call(
        partial(att2_back_kernel, before is not None),
        (pairs,),
        ins,
        outs,
        [VMEM((KR, D1), f32)],
        flops=flops,
        name="block2_attention_back",
    )


def mlp1_back_kernel(carry, *refs):
    n_in = 14 + (3 if carry else 0)
    dpc, rn, rf, gain_c, gain_m, mid, ha, nb, ub, gp, za, o, wout, wfc = refs[:14]
    n_in += 1
    wp = refs[14]
    before = refs[15:n_in]
    gha, gze, gg_c, gg_m, gw_out, gw_fc, gw_p, ds = refs[n_in:]
    step = pl.program_id(0)

    @pl.when(step == 0)
    def _():
        got = (rn[...].astype(f32) + rf[...].astype(f32)).astype(bf16)
        d = 0.25 * (dpc[...] + mm_tn(tmean_matrix(), got))
        for s in range(4):
            ds[PT * s : PT * (s + 1), :] = d[0:PT]
        gg_c[...] = jnp.zeros_like(gg_c)
        gg_m[...] = jnp.zeros_like(gg_m)
        for i, ref in enumerate((gw_out, gw_fc, gw_p)):
            ref[...] = before[i][...] if carry else jnp.zeros_like(ref)

    unit, inv = norm_stats(mid[...])
    dnc = ds[pl.ds(pl.multiple_of(step * TILE, TILE), TILE), :]
    gmid, dg = norm_back(dnc, unit, inv, gain_c[...])
    gg_c[...] += dg
    gm = gmid.astype(bf16)
    gmt = gm.T
    nbt = nb[...].T
    part = F1 // 3
    dn = jnp.zeros((TILE, D1), f32)
    for j in range(3):
        at = slice(part * j, part * (j + 1))
        gi = (gp[:, at].astype(f32) * mm_nt(gm, wout[at, :])).astype(bf16)
        gw_out[:, at] += mm(gmt, ub[:, at])
        gw_fc[:, at] += mm(nbt, gi)
        dn = dn + mm_nt(gi, wfc[:, at])
    unit, inv = norm_stats(ha[...])
    dx, dg = norm_back(dn, unit, inv, gain_m[...])
    gg_m[...] += dg
    g = gmid + dx
    gha[...] = g
    gh = g.astype(bf16)
    gw_p[...] += mm_tn(za[...], gh)
    gz = mm_nt(gh, wp[...]).astype(bf16)
    for h in range(H1):
        at = slice(LANE * h, LANE * (h + 1))
        gze[:, at] = grad_ext(gz[:, at], o[:, at])


def mlp1_back(dpc, rn, rf, gain_c, gain_m, mid, ha, nb, ub, gp, za, o, wout, wfc, wp, before):
    ins = [whole(a) for a in (dpc, rn, rf, gain_c, gain_m)]
    ins += [rows_tiled(a) for a in (mid, ha, nb, ub, gp, za, o)]
    ins += [whole(wout), whole(wfc), whole(wp)]
    grads = [whole(shape_of((D1, F1), f32)), whole(shape_of((D1, F1), f32)), whole(shape_of((W1, D1), f32))]
    if before is not None:
        ins += [(b, s) for b, (_, s) in zip(before, grads)]
    outs = [
        rows_tiled(shape_of((QT, D1), f32)),
        rows_tiled(shape_of((QT, W1), bf16)),
        whole(shape_of((1, D1), f32)),
        whole(shape_of((1, D1), f32)),
    ] + grads
    flops = 2 * QT * (4 * D1 * F1 + 2 * D1 * W1)
    return call(
        partial(mlp1_back_kernel, before is not None),
        (STEPS,),
        ins,
        outs,
        [VMEM((QT, D1), f32)],
        flops=flops,
        name="block1_mlp_back",
    )


QUERY_TILES = [slice(0, 512), slice(512, 1024), slice(1024, QT)]


def att1_back_kernel(carry, *refs):
    n_in = 9 + (3 if carry else 0)
    qe, gze, k, v, na, kall, wq, wk, wv = refs[:9]
    before = refs[9:n_in]
    dnear, dfar, down, dna, gq_w, gk_w, gv_w, dkv, nat = refs[n_in:]
    step = pl.program_id(0)

    def out(ref, value, i):
        ref[...] = value + before[i][...] if carry else value

    @pl.when(step == 0)
    def _():
        dkv[...] = jnp.zeros_like(dkv)
        dna[...] = jnp.zeros_like(dna)
        nat[...] = na[...].T

    gq, dk, dv = [[] for _ in QUERY_TILES], [], []
    for h in range(2):
        at = slice(LANE * h, LANE * (h + 1))
        g = gze[:, at]
        dqs, dkh, dvh = head_backward(qe[:, at], g, k[:, at], v[:, at], QUERY_TILES)
        for i, rows in enumerate(QUERY_TILES):
            gq[i].append((g[rows].astype(f32) + dqs[i]).astype(bf16))
        dk.append(dkh.astype(bf16))
        dv.append(dvh.astype(bf16))
    gq = jnp.concatenate([jnp.concatenate(t, axis=1) for t in gq], axis=0)
    lane = lanes((1, PAIR)) % LANE
    gq = jnp.where(lane < HD, gq, jnp.zeros_like(gq))
    dk = jnp.concatenate(dk, axis=1)
    dv = jnp.concatenate(dv, axis=1)
    dna[...] += mm_nt(gq, wq[...])
    dkv[...] += mm_nt(dk, wk[...]) + mm_nt(dv, wv[...])
    out(gq_w, mm(nat[...], gq), 0)
    out(gk_w, mm_tn(kall[...], dk), 1)
    out(gv_w, mm_tn(kall[...], dv), 2)

    @pl.when(step == H1 // 2 - 1)
    def _():
        down[...] = dkv[0:PR, :]
        dnear[...] = dkv[PR : PR + MR, :].astype(bf16)
        dfar[...] = dkv[PR + MR : KR, :].astype(bf16)


def att1_back(qe, gze, k, v, na, kall, w, before):
    pairs = H1 // 2
    ins = [cols_tiled(a, PAIR) for a in (qe, gze, k, v)]
    ins += [whole(na), whole(kall)]
    ins += [cols_tiled(w, PAIR, j * pairs) for j in range(3)]
    grads = [cols_tiled(shape_of((D1, W1), f32), PAIR) for _ in range(3)]
    if before is not None:
        ins += [(b, s) for b, (_, s) in zip(before, grads)]
    outs = [
        whole(shape_of((MR, D1), bf16)),
        whole(shape_of((MR, D1), bf16)),
        whole(shape_of((PR, D1), f32)),
        whole(shape_of((QT, D1), f32)),
    ] + grads
    flops = 2 * (10 * QT * KR * W1 + 2 * QT * D1 * W1 + 4 * KR * D1 * W1)
    return call(
        partial(att1_back_kernel, before is not None),
        (pairs,),
        ins,
        outs,
        [VMEM((KR, D1), f32), VMEM((D1, QT), bf16)],
        flops=flops,
        name="block1_attention_back",
    )


def last_kernel(dna, down, rn, rf, xp, gha, gain, gx, gg, gs, ds):
    got = (rn[...].astype(f32) + rf[...].astype(f32)).astype(bf16)
    d = 0.25 * (down[...] + mm_tn(tmean_matrix(), got))
    for s in range(4):
        ds[PT * s : PT * (s + 1), :] = d[0:PT]
    total = jnp.zeros((1, D1), f32)
    for i in range(STEPS):
        at = slice(TILE * i, TILE * (i + 1))
        unit, inv = norm_stats(xp[at, :].astype(f32))
        dx, dg = norm_back(dna[at, :] + ds[at, :], unit, inv, gain[...])
        total = total + dg
        gs[at, :] = gha[at, :] + dx
    gg[...] = total
    for i in range(STEPS):
        lo = min(CELL * i // 8 * 8, PT - 112)
        window = jnp.concatenate([gs[PT * s + lo : PT * s + lo + 112, :] for s in range(4)], axis=0).astype(bf16)
        shape = (TILE, 4 * 112)
        t = rows_of(shape) + TILE * i
        f = t // (HT * WD)
        rest = t - f * (HT * WD)
        r = rest // WD
        c = rest - r * WD
        r2 = r // 2
        c2 = c // 2
        s = 2 * (r - 2 * r2) + (c - 2 * c2)
        p = f * CELL + r2 * 7 + c2
        pick = jnp.where(s * 112 + p - lo == lanes(shape), 1.0, 0.0).astype(bf16)
        gx[TILE * i : TILE * (i + 1), :] = mm(pick, window).astype(bf16)


def last(dna, down, rn, rf, xp, gha, gain):
    outs = [shape_of((QT, D1), bf16), shape_of((1, D1), f32)]
    return call(
        last_kernel,
        (1,),
        [whole(a) for a in (dna, down, rn, rf, xp, gha, gain)],
        [whole(o) for o in outs],
        [VMEM((QT, D1), f32), VMEM((QT, D1), f32)],
        flops=2 * QT * 448 * D1,
        name="last_norm_back",
    )


def shift(value, steps):
    count = lax.axis_size("clip")
    first_, last_ = (max(0, -steps), min(count, count - steps))
    return lax.ppermute(value, "clip", [(s, s + steps) for s in range(first_, last_)])


def swap(value, axis, bit=0):
    n = lax.axis_size(axis)
    return lax.ppermute(value, axis, [(i, i ^ (1 << bit)) for i in range(n)])


def strip(grad):
    return jnp.concatenate([grad[:, LANE * h : LANE * h + HD] for h in range(grad.shape[1] // LANE)], axis=1)


def pack2_kernel(micro, gq, gk, gv, gp, gs, keep_a, send_a, keep_b, send_b, qkv):
    for j, g in enumerate((gq, gk, gv)):
        qkv[:, D2 * j : D2 * (j + 1)] = strip(g[...])
    clips, rows, _ = keep_a.shape
    first_ = micro[0] == 0

    def proj(share, a):
        lo = rows * (2 * share + a)
        h = lo // HD
        if (lo + rows - 1) // HD == h:
            return gp[lo + (LANE - HD) * h : lo + (LANE - HD) * h + rows, :]
        cut = HD * (h + 1) - lo
        top = gp[lo + (LANE - HD) * h : lo + (LANE - HD) * h + cut, :]
        return jnp.concatenate([top, gp[LANE * (h + 1) : LANE * (h + 1) + rows - cut, :]], axis=0)

    for i in range(clips):
        for keep, send, piece in (
            (keep_a, send_a, lambda n: qkv[rows * n : rows * (n + 1), :]),
            (keep_b, send_b, lambda n: jnp.concatenate([proj(n, 0), proj(n, 1), gs[rows * n : rows * (n + 1), :]], axis=1)),
        ):
            k, t = pick_share(micro[0], piece(2 * i), piece(2 * i + 1))
            keep[i] = k
            send[i] = t


def pack2(micro, clips, grads):
    share = shape_of((clips, D1 // (2 * clips), 3 * D2), bf16)
    return call(
        pack2_kernel,
        (1,),
        [scalar(micro)] + [whole(g) for g in grads],
        [whole(share)] * 4,
        [VMEM((D1, 3 * D2), f32)],
        name="pack_block2_grads",
    )


def pack1_kernel(micro, gq, gk, gv, gp, gfc, gout, keep_a, send_a, keep_b, send_b, qkv, out):
    for j, g in enumerate((gq, gk, gv)):
        qkv[:, D1 * j : D1 * (j + 1)] = strip(g[...])
    for h in range(H1):
        qkv[HD * h : HD * (h + 1), 3 * D1 :] = gp[LANE * h : LANE * h + HD, :]
    out[...] = gout[...].T
    clips, rows, _ = keep_a.shape
    half = 2 * D1

    def piece_a(n):
        at = slice(rows * n, rows * (n + 1))
        return jnp.concatenate([gfc[at, :], qkv[at, :half]], axis=1)

    def piece_b(n):
        at = slice(rows * n, rows * (n + 1))
        blocks = [out[rows * (4 * n + a) : rows * (4 * n + a + 1), :] for a in range(4)]
        return jnp.concatenate(blocks + [qkv[at, half:]], axis=1)

    for i in range(clips):
        for keep, send, piece in ((keep_a, send_a, piece_a), (keep_b, send_b, piece_b)):
            k, t = pick_share(micro[0], piece(2 * i), piece(2 * i + 1))
            keep[i] = k
            send[i] = t


def pack1(micro, clips, grads):
    share = shape_of((clips, D1 // (2 * clips), 6 * D1), bf16)
    return call(
        pack1_kernel,
        (1,),
        [scalar(micro)] + [whole(g) for g in grads],
        [whole(share)] * 4,
        [VMEM((D1, 4 * D1), f32), VMEM((F1, D1), f32)],
        name="pack_block1_grads",
    )


def add_up(a, b):
    return a.astype(f32) + b.astype(f32)


def over_micro(parts):
    keep_a, send_a, keep_b, send_b = parts
    return (keep_a, swap(send_a, "micro"), keep_b, swap(send_b, "micro"))


def over_group(parts):
    keep_a, got_a, keep_b, got_b = parts
    first_ = lax.axis_index("group") == 0
    a, b = add_up(keep_a, got_a), add_up(keep_b, got_b)
    keep = jnp.where(first_, a, b).astype(bf16)
    send = jnp.where(first_, b, a).astype(bf16)
    return (keep, swap(send, "group"))


def over_clip(parts, bit):
    total = add_up(*parts).astype(bf16)
    bits = lax.axis_size("clip").bit_length() - 1
    v = total.reshape((2 ** (bits - bit - 1), 2) + total.shape[1:])
    mine = (lax.axis_index("clip") >> bit) & 1
    keep = lax.dynamic_index_in_dim(v, mine, 1, keepdims=False)
    send = lax.dynamic_index_in_dim(v, 1 - mine, 1, keepdims=False)
    return (keep, swap(send, "clip", bit))


def settle(parts):
    total = add_up(*parts).astype(bf16)[0]
    other = swap(total, "group")
    first_ = lax.axis_index("group") == 0
    return (jnp.where(first_, total, other).astype(f32), jnp.where(first_, other, total).astype(f32))


def stack_blocks(v, count):
    return jnp.concatenate(jnp.split(v, count, axis=1), axis=0)


def tied(held, *others):
    flat, tree = jax.tree.flatten((held, others))
    held, others = jax.tree.unflatten(tree, lax.optimization_barrier(flat))
    return (held, *others)


def body(inputs, offsets, cotangent, gain_attn1, w_qkv1, w_proj1, gain_mlp1, w_fc1, w_out1,
         gain_attn2, w_qkv2, w_proj2, w_skip, gain_mlp2, w_fc2, w_out2):
    videos = range(inputs.shape[1])
    clip = lax.axis_index("clip")
    g_a1, g_m1, g_a2, g_m2 = (g.reshape(1, -1) for g in (gain_attn1, gain_mlp1, gain_attn2, gain_mlp2))
    row = jnp.arange(KR, dtype=jnp.int32)[:, None]
    place = jnp.where(row < PR + MR, row - PR, row - PR - MR)
    later = (place // CELL >= offsets[0]) & (place < MT)
    hops = jnp.where(row < PR + MR, 1, 2)
    valid = jnp.where(row < PR, row < PT, later & (clip >= hops))
    lane = jnp.arange(LANE, dtype=jnp.int32)[None, :]
    kext = jnp.where(lane == HD + 3, jnp.where(valid, 0.0, -1e30), jnp.where((lane >= HD) & (lane < HD + 3), 1.0, 0.0))
    kext = kext.astype(f32)

    w1p, p1p, w2p, p2p = pad_weights(w_qkv1, w_proj1, w_qkv2, w_proj2)
    xp, na, kva, mema = zip(*[first(inputs, b, g_a1) for b in videos])
    a = [
        block1(kva[b], shift(mema[b], 1), shift(mema[b], 2), kext, na[b], xp[b], w1p, p1p, g_m1, w_fc1, w_out1, g_a2)
        for b in videos
    ]
    ka, Ka, Va, qea, oa, za, ha, nb, ub, gp, mid, pc, memc = zip(*a)
    c = [block2(pc[b], shift(memc[b], 1), shift(memc[b], 2), kext, w2p, w_skip, p2p) for b in videos]
    kc, Kc, Vc, qec, oc, zc, hc = zip(*c)
    micro, clips = lax.axis_index("micro"), lax.axis_size("clip")
    bits = clips.bit_length() - 1
    output, gh, keep_fc, send_fc, keep_out, send_out, gg_mlp2 = mlp2(micro, clips, hc[0], hc[1], cotangent, g_m2, w_fc2, w_out2)
    big = over_micro((keep_fc, send_fc, keep_out, send_out))

    before, dn2, df2, dpc = None, [], [], []
    for b in videos:
        if b == 1:
            big, gh = tied(big, gh)
            big = over_group(big)
        near, far, d, *before = att2_back(
            b, gh, p2p, qec[b], oc[b], Kc[b], Vc[b], zc[b], pc[b], kc[b], w_skip, w2p, before
        )
        dn2.append(shift(near, -1))
        df2.append(shift(far, -2))
        dpc.append(d)
    middle = over_micro(pack2(micro, clips, before))
    before, gha, gze, gg_c, gg_m = None, [], [], 0.0, 0.0
    for b in videos:
        d = dpc[b]
        if b == 1:
            big, middle, d = tied(big, middle, d)
            big = over_clip(big, 0)
            middle = over_group(middle)
        g, z, gc, gm, *before = mlp1_back(
            d, dn2[b], df2[b], g_a2, g_m1, mid[b], ha[b], nb[b], ub[b], gp[b], za[b], oa[b], w_out1, w_fc1, p1p, before
        )
        gha.append(g)
        gze.append(z)
        gg_c = gg_c + gc
        gg_m = gg_m + gm
    gw_out1t, gw_fc1, gp1 = before
    before, dn1, df1, down, dna = None, [], [], [], []
    for b in videos:
        z = gze[b]
        if b == 0:
            big, middle, z = tied(big, middle, z)
            big = over_clip(big, 1)
            middle = over_clip(middle, 0)
        else:
            big, middle, z = tied(big, middle, z)
            for bit in range(2, bits):
                big = over_clip(big, bit)
            middle = over_clip(middle, 1)
        near, far, d, dn, *before = att1_back(qea[b], z, Ka[b], Va[b], na[b], ka[b], w1p, before)
        dn1.append(shift(near, -1))
        df1.append(shift(far, -2))
        down.append(d)
        dna.append(dn)
    small = over_micro(pack1(micro, clips, list(before) + [gp1, gw_fc1, gw_out1t]))
    ends = [last(dna[b], down[b], dn1[b], df1[b], xp[b], gha[b], g_a1) for b in videos]
    gx = jnp.stack([e[0] for e in ends])
    gg_a = ends[0][1] + ends[1][1]
    gains = jnp.concatenate([gg_a, gg_m, gg_c, gg_mlp2], axis=1)
    gains = gains + swap(gains, "micro")
    gains = gains + swap(gains, "group")
    for bit in range(bits):
        gains = gains + swap(gains, "clip", bit)
    for bit in range(2, bits):
        middle = over_clip(middle, bit)
    small = over_group(small)
    for bit in range(bits):
        small = over_clip(small, bit)
    gw_fc2, gw_out2 = settle(big)
    gw_qkv2, rest2 = settle(middle)
    left, right = settle(small)
    r = rest2.shape[0]
    shares = (
        jnp.concatenate([left[:, F1:], right[:, F1 : F1 + D1]], axis=1),
        right[:, F1 + D1 :],
        left[:, :F1],
        stack_blocks(right[:, :F1], 4),
        gw_qkv2,
        stack_blocks(rest2[:, : 2 * D2], 2),
        rest2[:, 2 * D2 :],
        gw_fc2,
        stack_blocks(gw_out2, 4),
    )
    gains = jnp.split(gains.reshape(-1), [D1, 2 * D1, 3 * D1])
    return (output, gx.reshape(inputs.shape)) + tuple(gains) + tuple(v.reshape(-1) for v in shares)


def solution(mesh):
    tokens = P("group", "micro", "clip", None, None)
    share = P(("clip", "micro"))
    return jax.shard_map(
        body,
        mesh=mesh,
        in_specs=(tokens, P("group"), tokens) + (P(),) * 13,
        out_specs=(tokens, tokens) + (P(),) * 4 + (share,) * 9,
        check_vma=False,
    )
```

time: 974 us -> 513 us (0.53)
  Pallas kernels: 0 us -> 340 us
  matrix products: 336 us -> 0 us
  local copies, waits for them, and re-layouts: 208 us -> 17.1 us
  other arithmetic: 171 us -> 18.9 us
  waiting for transfers between devices: 133 us -> 52.9 us
  blocking collectives: 40.2 us -> 0 us
    pallas_call x0 -> x18, Pallas kernels: none -> 340 us  [call(): pl.pallas_call(kernel, grid=grid, in_specs=[s for _, s in ins], out_specs...]
    dot_general x49 -> x0, matrix products: 336 us -> none  [the longest x11 55.4 us: dot(): return jnp.einsum('...nc,cf->...nf', a, b, preferred_element_type=f32)]
    convert_element_type x39 -> x15, other arithmetic: 97.6 us -> 15 us  [the longest x3 10.7 us: over_group(): send = jnp.where(first_, b, a).astype(bf16)]
    ppermute x62 -> x42, waiting for transfers between devices: 133 us -> 52.9 us  [the longest x26 52.9 us: swap(): return lax.ppermute(value, axis, [(i, i ^ 1 << bit) for i in range(n)])]
    convert_element_type x53 -> x0, local copies, waits for them, and re-layouts: 53.5 us -> none  [the longest x3 13.3 us: body(): x = x.reshape(B, 4, PT, D1).astype(f32)]
    reshape x12, local copies, waits for them, and re-layouts: 53.9 us -> 8.43 us  [the longest x8 5.48 us: body(): v.reshape(-1)]
    reduce_sum x11 -> x0, other arithmetic: 43.8 us -> none  [the longest x2 27.5 us: attend(): total = jnp.sum(e, axis=-1, keepdims=True)]
    psum x1 -> x0, blocking collectives: 40.2 us -> none  [body(): lax.psum((gg_attn1, gg_mlp1, gg_attn2, gg_mlp2), ('group', 'clip', 'micro'))]
  transfers between devices with their start and end apart: 62 -> 42, of which waited for: 34 -> 13; matrix products, arithmetic and copies ran while one was open for 41% -> 4% of each run, Pallas kernels for 0% -> 55%
where the time goes in v2:
time: 513 us; the launch traced here: 507 us
  Pallas kernels  340 us (66%)
  starting transfers between devices  76.4 us (15%)
  waiting for transfers between devices  52.9 us (10%)
  other arithmetic  18.9 us (4%)
  local copies, waits for them, and re-layouts  17.1 us (3%)
    pallas_call x18, Pallas kernels, call(): pl.pallas_call(kernel, grid=grid, in_specs=[s for _, s in ins], out_specs...  340 us
    ppermute x26, waiting for transfers between devices, swap(): return lax.ppermute(value, axis, [(i, i ^ 1 << bit) for i in range(n)])  52.9 us
    ppermute x26, starting transfers between devices, swap(): return lax.ppermute(value, axis, [(i, i ^ 1 << bit) for i in range(n)])  40.7 us
    ppermute x16, starting transfers between devices, shift(): lax.ppermute(value, 'clip', [(s, s + steps) for s in range(first_, last_)])  35.7 us
    convert_element_type x3, other arithmetic, over_group(): send = jnp.where(first_, b, a).astype(bf16)  10.7 us
  transfers between devices with their start and end apart: 42, of which 13 were waited for; matrix products, arithmetic and copies ran while one was open for 4% of the time, Pallas kernels for 55%

profile of v2, /device:TPU:0, one launch (start us, length us, event | category | flops | bytes accessed | tf_op | source)
XLA Modules:
  0.0 507.4 jit_solution(5016004257933684331)
XLA Ops:
  0.6 1.2 reshape.206.gain
  1.9 5.5 %first_norm.2 = (bf16[1568,384]{1,0:T(8,128)(2,1)}, bf16[1568,384]{1,0:T(8,128)(2,1)}, bf16[400,384]{1,0:T(8,128)(2,1)}, bf16[208,384]{1,0:T(8,128)(2,1)}) custom-call(bf16[1,2,1,1568,384]{4,3,2,1,0:T(8,128)(2,1)} %x.3, f32[1,384]{1,0:T(1,128)} %reshape.206.gain), custom_call_target="tpu_custom_call" | custom-call | flops 500957184 | bytes 5285376 | tf_op jit(solution)/shard_map/first_norm/pallas_call | solution.py:118
  7.4 5.0 collective-permute-start
  12.4 3.5 collective-permute-start.1
  15.9 5.5 %first_norm.3 = (bf16[1568,384]{1,0:T(8,128)(2,1)}, bf16[1568,384]{1,0:T(8,128)(2,1)}, bf16[400,384]{1,0:T(8,128)(2,1)}, bf16[208,384]{1,0:T(8,128)(2,1)}) custom-call(bf16[1,2,1,1568,384]{4,3,2,1,0:T(8,128)(2,1)} %x.3, f32[1,384]{1,0:T(1,128)} %reshape.206.gain), custom_call_target="tpu_custom_call" | custom-call | flops 500957184 | bytes 5285376 | tf_op jit(solution)/shard_map/first_norm/pallas_call | solution.py:118
  21.4 3.5 collective-permute-start.4
  24.9 3.6 collective-permute-start.5
  31.0 5.9 %pad_heads.1 = (bf16[384,1536]{1,0:T(8,128)(2,1)}, bf16[512,384]{1,0:T(8,128)(2,1)}, bf16[384,3072]{1,0:T(8,128)(2,1)}, bf16[1024,768]{1,0:T(8,128)(2,1)}) custom-call(bf16[384,1152]{1,0:T(8,128)(2,1)} %wa.1, bf16[384,384]{1,0:T(8,128)(2,1)} %pa.1, bf16[384,2304]{1,0:T(8,128)(2,1)} %wc.1, bf16[768,768]{1,0:T(8,128)(2,1)} %pc.1), custom_call_target="tpu_custom_call" | custom-call | bytes 9633792 | tf_op jit(solution)/shard_map/pad_heads/pallas_call | solution.py:118
  38.5 39.6 %block1_forward.2 = (bf16[816,384]{1,0:T(8,128)(2,1)}, bf16[816,512]{1,0:T(8,128)(2,1)}, bf16[816,512]{1,0:T(8,128)(2,1)}, bf16[1568,512]{1,0:T(8,128)(2,1)}, bf...) custom-call(bf16[400,384]{1,0:T(8,128)(2,1)} %get-tuple-element.152., ...), custom_call_target="tpu_custom_call" | custom-call | flops 10173284352 | bytes 32984064 | tf_op jit(solution)/shard_map/block1_forward/pallas_call | solution.py:118
  78.1 3.4 collective-permute-start.2
  81.5 1.9 collective-permute-start.3
  84.2 39.6 %block1_forward.3 = (bf16[816,384]{1,0:T(8,128)(2,1)}, bf16[816,512]{1,0:T(8,128)(2,1)}, bf16[816,512]{1,0:T(8,128)(2,1)}, bf16[1568,512]{1,0:T(8,128)(2,1)}, bf...) custom-call(bf16[400,384]{1,0:T(8,128)(2,1)} %get-tuple-element.163., ...), custom_call_target="tpu_custom_call" | custom-call | flops 10173284352 | bytes 32984064 | tf_op jit(solution)/shard_map/block1_forward/pallas_call | solution.py:118
  123.7 2.3 collective-permute-start.6
  126.1 1.9 collective-permute-start.7
  128.7 14.5 %block2_attention.2 = (bf16[816,384]{1,0:T(8,128)(2,1)}, bf16[816,1024]{1,0:T(8,128)(2,1)}, bf16[816,1024]{1,0:T(8,128)(2,1)}, bf16[400,1024]{1,0:T(8,128)(2,1)}...) custom-call(bf16[400,384]{1,0:T(8,128)(2,1)} %get-tuple-element.158.pc.refs_7_, ...), custom_call_target="tpu_custom_call" | custom-call | flops 5136973824 | bytes 17940480 | tf_op jit(solution)/shard_map/block2_attention/pallas_call | solution.py:118
  144.0 14.5 %block2_attention.3 = (bf16[816,384]{1,0:T(8,128)(2,1)}, bf16[816,1024]{1,0:T(8,128)(2,1)}, bf16[816,1024]{1,0:T(8,128)(2,1)}, bf16[400,1024]{1,0:T(8,128)(2,1)}...) custom-call(bf16[400,384]{1,0:T(8,128)(2,1)} %get-tuple-element.167.pc.refs_7_, ...), custom_call_target="tpu_custom_call" | custom-call | flops 5136973824 | bytes 17940480 | tf_op jit(solution)/shard_map/block2_attention/pallas_call | solution.py:118
  158.6 39.9 %block2_mlp.1 = (bf16[1,2,1,392,768]{4,3,2,1,0:T(8,128)(2,1)}, bf16[2,400,768]{2,1,0:T(8,128)(2,1)}, bf16[8,48,3072]{2,1,0:T(8,128)(2,1)}, bf16[8,48,3072]{2,1,0...) custom-call(s32[1]{0:T(128)} %bitcast.micro, ...), custom_call_target="tpu_custom_call" | custom-call | flops 22649241600 | bytes 24975364 | tf_op jit(solution)/shard_map/block2_mlp/pallas_call | solution.py:118
  199.1 6.8 %collective-permute-done.8 = bf16[8,48,3072]{2,1,0:T(8,128)(2,1)S(1)} collective-permute-done((bf16[8,48,3072]{2,1,0:T(8,128)(2,1)}, bf16[8,48,3072]{2,1,0:T(8,128)(2,1)S(1)}, u32[]{:S(2)}, u32[]{:S(2)}) %collective-permute-start.8) | collective-permute-done | bytes 2359328 | tf_op jit(solution)/shard_map/ppermute | solution.py:745
  207.3 7.5 %select_convert_fusion = (bf16[8,48,3072]{2,1,0:T(8,128)(2,1)}, bf16[8,48,3072]{2,1,0:T(8,128)(2,1)S(1)}) fusion(bf16[8,48,3072]{2,1,0:T(8,128)(2,1)} %copy-done.2, bf16[8,48,3072]{2,1,0:T(8,128)(2,1)} %get-tuple-element.177, bf16[8,48,3072]{2,1,0:T(8,128)(2,1)} %collective-permute-done.9, bf16[8,48,3072]{2,1,0:T(8,128)(2,1)} %get-tuple-element.179, pred[]{:T(512)S(6)} %eq.17), kind=kLoop, calls=%fused_computation.1 | loop fusion | flops 11796480 | bytes 14155777 | tf_op jit(solution)/shard_map/convert_element_type | solution.py:840
  214.7 1.5 collective-permute-start.10
  216.8 22.1 %block2_attention_back.2 = (bf16[208,384]{1,0:T(8,128)(2,1)}, bf16[208,384]{1,0:T(8,128)(2,1)}, f32[400,384]{1,0:T(8,128)}, f32[384,1024]{1,0:T(8,128)}, f32[384...) custom-call(bf16[2,400,768]{2,1,0:T(8,128)(2,1)} %get-tuple-element.181.refs_0_, ...), custom_call_target="tpu_custom_call" | custom-call | flops 13026459648 | bytes 27189248 | tf_op jit(solution)/shard_map/block2_attention_back/pallas_call | solution.py:118
  239.0 23.8 %block2_attention_back.3 = (bf16[208,384]{1,0:T(8,128)(2,1)}, bf16[208,384]{1,0:T(8,128)(2,1)}, f32[400,384]{1,0:T(8,128)}, f32[384,1024]{1,0:T(8,128)}, f32[384...) custom-call(bf16[2,400,768]{2,1,0:T(8,128)(2,1)} %get-tuple-element.181.refs_0_, ...), custom_call_target="tpu_custom_call" | custom-call | flops 13026459648 | bytes 36233216 | tf_op jit(solution)/shard_map/block2_attention_back/pallas_call | solution.py:118
  262.8 6.2 %pack_block2_grads.1 = (bf16[8,24,2304]{2,1,0:T(8,128)(2,1)}, bf16[8,24,2304]{2,1,0:T(8,128)(2,1)}, bf16[8,24,2304]{2,1,0:T(8,128)(2,1)}, bf16[8,24,2304]{2,1,0:T(8,128)(2,1)}) custom-call(s32[1]{0:T(128)} %bitcast.micro, f32[384,1024]{1,0:T(8,128)} %get-tuple-element.199.gq, f32[384,1024]{1,0:T(8,128)} %get-tuple-element.200.gk, ...), custom_call_target="tpu_custom_call" | custom-call | bytes 12582916 | tf_op jit(solution)/shard_map/pack_block2_grads/pallas_call | solution.py:118
  269.5 1.3 collective-permute-start.15
  270.8 1.3 collective-permute-start.16
  272.9 1.3 collective-permute-start.21
  274.2 1.3 collective-permute-start.22
  275.5 2.6 add_convert_fusion
  278.2 2.7 collective-permute-start.13
  281.0 2.7 select_convert_fusion.4
  284.9 24.4 %block1_mlp_back.2 = (f32[1568,384]{1,0:T(8,128)}, bf16[1568,512]{1,0:T(8,128)(2,1)}, f32[1,384]{1,0:T(1,128)}, f32[1,384]{1,0:T(1,128)}, f32[384,1536]{1,0:T(8,...) custom-call(f32[400,384]{1,0:T(8,128)} %get-tuple-element.215.refs_0_, bf16[208,384]{1,0:T(8,128)(2,1)} %copy-done.23, ...), custom_call_target="tpu_custom_call" | custom-call | flops 8631877632 | bytes 32077824 | tf_op jit(solution)/shard_map/block1_mlp_back/pallas_call | solution.py:118
  309.3 26.1 %block1_mlp_back.3 = (f32[1568,384]{1,0:T(8,128)}, bf16[1568,512]{1,0:T(8,128)(2,1)}, f32[1,384]{1,0:T(1,128)}, f32[1,384]{1,0:T(1,128)}, f32[384,1536]{1,0:T(8,...) custom-call(f32[400,384]{1,0:T(8,128)} %get-tuple-element.241.refs_0_, bf16[208,384]{1,0:T(8,128)(2,1)} %collective-permute-done.21.refs_1_, ...), custom_call_target="tpu_custom_call" | custom-call | flops 8631877632 | bytes 37582848 | tf_op jit(solution)/shard_map/block1_mlp_back/pallas_call | solution.py:118
  335.9 3.5 collective-permute-start.19
  339.7 1.2 collective-permute-start.20
  340.9 24.0 %block1_attention_back.2 = (bf16[208,384]{1,0:T(8,128)(2,1)}, bf16[208,384]{1,0:T(8,128)(2,1)}, f32[400,384]{1,0:T(8,128)}, f32[1568,384]{1,0:T(8,128)}, f32[384...) custom-call(bf16[1568,512]{1,0:T(8,128)(2,1)} %get-tuple-element.171.refs_0_, ...), custom_call_target="tpu_custom_call" | custom-call | flops 15618539520 | bytes 15953920 | tf_op jit(solution)/shard_map/block1_attention_back/pallas_call | solution.py:118
  364.9 1.3 collective-permute-start.17
  366.2 1.3 collective-permute-start.18
  367.6 24.2 %block1_attention_back.3 = (bf16[208,384]{1,0:T(8,128)(2,1)}, bf16[208,384]{1,0:T(8,128)(2,1)}, f32[400,384]{1,0:T(8,128)}, f32[1568,384]{1,0:T(8,128)}, f32[384...) custom-call(bf16[1568,512]{1,0:T(8,128)(2,1)} %get-tuple-element.236.refs_0_, ...), custom_call_target="tpu_custom_call" | custom-call | flops 15618539520 | bytes 18313216 | tf_op jit(solution)/shard_map/block1_attention_back/pallas_call | solution.py:118
  391.8 1.3 collective-permute-start.23
  393.1 1.5 collective-permute-start.24
  395.4 8.9 %last_norm_back.2 = (bf16[1568,384]{1,0:T(8,128)(2,1)}, f32[1,384]{1,0:T(1,128)}) custom-call(f32[1568,384]{1,0:T(8,128)} %get-tuple-element.230.dna, f32[400,384]{1,0:T(8,128)} %get-tuple-element.231.down, bf16[208,384]{1,0:T(8,128)(2,1)} %copy-done.8, bf16[208,384]{1,0:T(8,128)(2,1)} %copy-done.10, bf16[1568,384]{1,0:T(8,128)(2,1)} %get-tuple-element.155.xp, ...), custom_call_target="tpu_custom_call" | custom-call | flops 539492352 | bytes 8162304 | tf_op jit(solution)/shard_map/last_norm_back/pallas_call | solution.py:118
  404.3 6.0 %pack_block1_grads.1 = (bf16[8,24,2304]{2,1,0:T(8,128)(2,1)}, bf16[8,24,2304]{2,1,0:T(8,128)(2,1)}, bf16[8,24,2304]{2,1,0:T(8,128)(2,1)}, bf16[8,24,2304]{2,1,0:T(8,128)(2,1)}) custom-call(s32[1]{0:T(128)} %bitcast.micro, f32[384,512]{1,0:T(8,128)} %get-tuple-element.275.gq, f32[384,512]{1,0:T(8,128)} %get-tuple-element.276.gk, ...), custom_call_target="tpu_custom_call" | custom-call | bytes 11403268 | tf_op jit(solution)/shard_map/pack_block1_grads/pallas_call | solution.py:118
  411.6 8.9 %last_norm_back.3 = (bf16[1568,384]{1,0:T(8,128)(2,1)}, f32[1,384]{1,0:T(1,128)}) custom-call(f32[1568,384]{1,0:T(8,128)} %get-tuple-element.262.dna, f32[400,384]{1,0:T(8,128)} %get-tuple-element.263.down, bf16[208,384]{1,0:T(8,128)(2,1)} %copy-done.7, bf16[208,384]{1,0:T(8,128)(2,1)} %copy-done.9, bf16[1568,384]{1,0:T(8,128)(2,1)} %get-tuple-element.166.xp, ...), custom_call_target="tpu_custom_call" | custom-call | flops 539492352 | bytes 8162304 | tf_op jit(solution)/shard_map/last_norm_back/pallas_call | solution.py:118
  422.4 1.6 collective-permute-start.26
  424.0 5.4 %collective-permute-start.37 = (bf16[2,24,2304]{2,1,0:T(8,128)(2,1)S(1)}, bf16[2,24,2304]{2,1,0:T(8,128)(2,1)S(1)}, u32[]{:S(2)}, u32[]{:S(2)}) collective-permute-start(bf16[2,24,2304]{2,1,0:T(8,128)(2,1)S(1)} %dynamic-slice_bitcast_fusion.7), channel_id=1, source_target_pairs={{0,4},{2,6},{4,0},{6,2},{8,12},{10,14},{12,8},{14,10},{1,5},{3,7},... | collective-permute-start | bytes 663560 | tf_op jit(solution)/shard_map/ppermute | solution.py:745
  429.4 1.5 collective-permute-start.27
  431.1 2.0 collective-permute-done.27
  433.2 2.1 collective-permute-start.28
  435.3 4.2 collective-permute-start.40
  439.5 1.7 collective-permute-start.29
  441.2 1.9 maximum_bitcast_fusion
  443.2 8.0 %collective-permute-done.29 = f32[1,1920]{1,0:T(1,128)S(1)} collective-permute-done((f32[1,1920]{1,0:T(1,128)S(1)}, f32[1,1920]{1,0:T(1,128)S(1)}, u32[]{:S(2)}, u32[]{:S(2)}) %collective-permute-start.29) | collective-permute-done | bytes 7712 | tf_op jit(solution)/shard_map/ppermute | solution.py:745
  453.1 1.3 collective-permute-start.32
  455.3 4.6 collective-permute-done.38
  459.9 1.1 collective-permute-start.39
  460.9 14.8 %collective-permute-done.32 = bf16[8,24,2304]{2,1,0:T(8,128)(2,1)S(1)} collective-permute-done((bf16[8,24,2304]{2,1,0:T(8,128)(2,1)S(1)}, bf16[8,24,2304]{2,1,0:T(8,128)(2,1)S(1)}, u32[]{:S(2)}, u32[]{:S(2)}) %collective-permute-start.32) | collective-permute-done | bytes 884768 | tf_op jit(solution)/shard_map/ppermute | solution.py:745
  476.4 1.3 collective-permute-start.33
  477.6 5.3 %collective-permute-done.39 = bf16[24,2304]{1,0:T(8,128)(2,1)S(1)} collective-permute-done((bf16[24,2304]{1,0:T(8,128)(2,1)S(1)}, bf16[24,2304]{1,0:T(8,128)(2,1)S(1)}, u32[]{:S(2)}, u32[]{:S(2)}) %collective-permute-start.39) | collective-permute-done | bytes 110624 | tf_op jit(solution)/shard_map/ppermute | solution.py:745
  485.9 2.2 collective-permute-start.34
  488.2 3.8 collective-permute-done.34
  492.1 2.5 collective-permute-start.35
  495.6 2.3 collective-permute-done.35
  497.9 3.8 collective-permute-start.36
  502.6 1.8 collective-permute-done.36
  (164 shorter events, 26.6 us)
Async XLA Ops:
  7.4 21.8 %copy-start.13 = (f32[384]{0:T(512)S(1)}, f32[384]{0:T(512)}, u32[]{:S(2)}) copy-start(f32[384]{0:T(512)} %param.22) | copy-start | bytes 4612
  7.4 22.4 %copy-start.14 = (f32[384]{0:T(512)S(1)}, f32[384]{0:T(512)}, u32[]{:S(2)}) copy-start(f32[384]{0:T(512)} %param.25) | copy-start | bytes 4612
  7.4 23.0 %copy-start.12 = (f32[768]{0:T(1024)S(1)}, f32[768]{0:T(1024)}, u32[]{:S(2)}) copy-start(f32[768]{0:T(1024)} %param.29) | copy-start | bytes 9220
  7.4 30.3 %collective-permute-start = (bf16[208,384]{1,0:T(8,128)(2,1)}, bf16[208,384]{1,0:T(8,128)(2,1)S(1)}, u32[]{:S(2)}, u32[]{:S(2)}) collective-permute-start(bf16[208,384]{1,0:T(8,128)(2,1)} %get-tuple-element.153), channel_id=1, source_target_pairs={{0,2},{2,4},{4,6},{6,8},{8,10},{10,12},{12,14},{1,3},{3,5},{5,7},{... | collective-permute-start | bytes 479240 | tf_op jit(solution)/shard_map/ppermute | solution.py:740
  12.4 25.4 %collective-permute-start.1 = (bf16[208,384]{1,0:T(8,128)(2,1)}, bf16[208,384]{1,0:T(8,128)(2,1)S(1)}, u32[]{:S(2)}, u32[]{:S(2)}) collective-permute-start(bf16[208,384]{1,0:T(8,128)(2,1)} %get-tuple-element.153), channel_id=1, source_target_pairs={{0,4},{2,6},{4,8},{6,10},{8,12},{10,14},{1,5},{3,7},{5,9},{7,11},{... | collective-permute-start | bytes 479240 | tf_op jit(solution)/shard_map/ppermute | solution.py:740
  21.4 62.0 %collective-permute-start.4 = (bf16[208,384]{1,0:T(8,128)(2,1)}, bf16[208,384]{1,0:T(8,128)(2,1)S(1)}, u32[]{:S(2)}, u32[]{:S(2)}) collective-permute-start(bf16[208,384]{1,0:T(8,128)(2,1)} %get-tuple-element.164), channel_id=1, source_target_pairs={{0,2},{2,4},{4,6},{6,8},{8,10},{10,12},{12,14},{1,3},{3,5},{5,7},{... | collective-permute-start | bytes 479240 | tf_op jit(solution)/shard_map/ppermute | solution.py:740
  24.9 58.6 %collective-permute-start.5 = (bf16[208,384]{1,0:T(8,128)(2,1)}, bf16[208,384]{1,0:T(8,128)(2,1)S(1)}, u32[]{:S(2)}, u32[]{:S(2)}) collective-permute-start(bf16[208,384]{1,0:T(8,128)(2,1)} %get-tuple-element.164), channel_id=1, source_target_pairs={{0,4},{2,6},{4,8},{6,10},{8,12},{10,14},{1,5},{3,7},{5,9},{7,11},{... | collective-permute-start | bytes 479240 | tf_op jit(solution)/shard_map/ppermute | solution.py:740
  37.8 0.7 copy-start.25
  78.1 49.9 %collective-permute-start.2 = (bf16[208,384]{1,0:T(8,128)(2,1)}, bf16[208,384]{1,0:T(8,128)(2,1)S(1)}, u32[]{:S(2)}, u32[]{:S(2)}) collective-permute-start(bf16[208,384]{1,0:T(8,128)(2,1)} %get-tuple-element.159), channel_id=1, source_target_pairs={{0,2},{2,4},{4,6},{6,8},{8,10},{10,12},{12,14},{1,3},{3,5},{5,7},{... | collective-permute-start | bytes 479240 | tf_op jit(solution)/shard_map/ppermute | solution.py:740
  81.5 46.5 %collective-permute-start.3 = (bf16[208,384]{1,0:T(8,128)(2,1)}, bf16[208,384]{1,0:T(8,128)(2,1)S(1)}, u32[]{:S(2)}, u32[]{:S(2)}) collective-permute-start(bf16[208,384]{1,0:T(8,128)(2,1)} %get-tuple-element.159), channel_id=1, source_target_pairs={{0,4},{2,6},{4,8},{6,10},{8,12},{10,14},{1,5},{3,7},{5,9},{7,11},{... | collective-permute-start | bytes 479240 | tf_op jit(solution)/shard_map/ppermute | solution.py:740
  83.5 0.7 copy-start.22
  123.7 19.5 %collective-permute-start.6 = (bf16[208,384]{1,0:T(8,128)(2,1)}, bf16[208,384]{1,0:T(8,128)(2,1)S(1)}, u32[]{:S(2)}, u32[]{:S(2)}) collective-permute-start(bf16[208,384]{1,0:T(8,128)(2,1)} %get-tuple-element.168), channel_id=1, source_target_pairs={{0,2},{2,4},{4,6},{6,8},{8,10},{10,12},{12,14},{1,3},{3,5},{5,7},{... | collective-permute-start | bytes 479240 | tf_op jit(solution)/shard_map/ppermute | solution.py:740
  126.1 17.2 %collective-permute-start.7 = (bf16[208,384]{1,0:T(8,128)(2,1)}, bf16[208,384]{1,0:T(8,128)(2,1)S(1)}, u32[]{:S(2)}, u32[]{:S(2)}) collective-permute-start(bf16[208,384]{1,0:T(8,128)(2,1)} %get-tuple-element.168), channel_id=1, source_target_pairs={{0,4},{2,6},{4,8},{6,10},{8,12},{10,14},{1,5},{3,7},{5,9},{7,11},{... | collective-permute-start | bytes 479240 | tf_op jit(solution)/shard_map/ppermute | solution.py:740
  128.0 0.7 copy-start.27
  143.3 0.7 copy-start.29
  198.5 7.4 %collective-permute-start.8 = (bf16[8,48,3072]{2,1,0:T(8,128)(2,1)}, bf16[8,48,3072]{2,1,0:T(8,128)(2,1)S(1)}, u32[]{:S(2)}, u32[]{:S(2)}) collective-permute-start(bf16[8,48,3072]{2,1,0:T(8,128)(2,1)} %get-tuple-element.173), channel_id=1, source_target_pairs={{0,1},{1,0},{2,3},{3,2},{4,5},{5,4},{6,7},{7,6},{8,9},{9,8},{10,11... | collective-permute-start | bytes 7077896 | tf_op jit(solution)/shard_map/ppermute | solution.py:745
  198.6 8.2 %collective-permute-start.9 = (bf16[8,48,3072]{2,1,0:T(8,128)(2,1)}, bf16[8,48,3072]{2,1,0:T(8,128)(2,1)}, u32[]{:S(2)}, u32[]{:S(2)}) collective-permute-start(bf16[8,48,3072]{2,1,0:T(8,128)(2,1)} %get-tuple-element.175), channel_id=1, source_target_pairs={{0,1},{1,0},{2,3},{3,2},{4,5},{5,4},{6,7},{7,6},{8,9},{9,8},{10,11... | collective-permute-start | bytes 7077896 | tf_op jit(solution)/shard_map/ppermute | solution.py:745
  205.9 1.4 copy-start.2
  214.7 60.8 %collective-permute-start.10 = (bf16[8,48,3072]{2,1,0:T(8,128)(2,1)}, bf16[8,48,3072]{2,1,0:T(8,128)(2,1)}, u32[]{:S(2)}, u32[]{:S(2)}) collective-permute-start(bf16[8,48,3072]{2,1,0:T(8,128)(2,1)} %get-tuple-element.337), channel_id=1, source_target_pairs={{0,16},{16,0},{1,17},{17,1},{2,18},{18,2},{3,19},{19,3},{4,20},{20... | collective-permute-start | bytes 7077896 | tf_op jit(solution)/shard_map/ppermute | solution.py:745
  262.8 11.4 %copy-start.20 = (bf16[208,384]{1,0:T(8,128)(2,1)S(1)}, bf16[208,384]{1,0:T(8,128)(2,1)}, u32[]{:S(2)}) copy-start(bf16[208,384]{1,0:T(8,128)(2,1)} %get-tuple-element.243) | copy-start | bytes 479236
  269.0 3.9 collective-permute-start.11
  269.0 5.2 %collective-permute-start.12 = (bf16[8,24,2304]{2,1,0:T(8,128)(2,1)}, bf16[8,24,2304]{2,1,0:T(8,128)(2,1)}, u32[]{:S(2)}, u32[]{:S(2)}) collective-permute-start(bf16[8,24,2304]{2,1,0:T(8,128)(2,1)} %get-tuple-element.207), channel_id=1, source_target_pairs={{0,1},{1,0},{2,3},{3,2},{4,5},{5,4},{6,7},{7,6},{8,9},{9,8},{10,11... | collective-permute-start | bytes 2654216 | tf_op jit(solution)/shard_map/ppermute | solution.py:745
  269.5 14.2 %collective-permute-start.15 = (bf16[208,384]{1,0:T(8,128)(2,1)}, bf16[208,384]{1,0:T(8,128)(2,1)S(1)}, u32[]{:S(2)}, u32[]{:S(2)}) collective-permute-start(bf16[208,384]{1,0:T(8,128)(2,1)} %get-tuple-element.216), channel_id=1, source_target_pairs={{2,0},{4,2},{6,4},{8,6},{10,8},{12,10},{14,12},{3,1},{5,3},{7,5},{... | collective-permute-start | bytes 479240 | tf_op jit(solution)/shard_map/ppermute | solution.py:740
  270.8 14.1 %collective-permute-start.16 = (bf16[208,384]{1,0:T(8,128)(2,1)}, bf16[208,384]{1,0:T(8,128)(2,1)}, u32[]{:S(2)}, u32[]{:S(2)}) collective-permute-start(bf16[208,384]{1,0:T(8,128)(2,1)} %get-tuple-element.217), channel_id=1, source_target_pairs={{4,0},{6,2},{8,4},{10,6},{12,8},{14,10},{5,1},{7,3},{9,5},{11,7},{... | collective-permute-start | bytes 479240 | tf_op jit(solution)/shard_map/ppermute | solution.py:740
  272.9 36.4 %collective-permute-start.21 = (bf16[208,384]{1,0:T(8,128)(2,1)}, bf16[208,384]{1,0:T(8,128)(2,1)}, u32[]{:S(2)}, u32[]{:S(2)}) collective-permute-start(bf16[208,384]{1,0:T(8,128)(2,1)} %get-tuple-element.242), channel_id=1, source_target_pairs={{2,0},{4,2},{6,4},{8,6},{10,8},{12,10},{14,12},{3,1},{5,3},{7,5},{... | collective-permute-start | bytes 479240 | tf_op jit(solution)/shard_map/ppermute | solution.py:740
  274.2 35.1 %collective-permute-start.22 = (bf16[208,384]{1,0:T(8,128)(2,1)S(1)}, bf16[208,384]{1,0:T(8,128)(2,1)}, u32[]{:S(2)}, u32[]{:S(2)}) collective-permute-start(bf16[208,384]{1,0:T(8,128)(2,1)S(1)} %copy-done.20), channel_id=1, source_target_pairs={{4,0},{6,2},{8,4},{10,6},{12,8},{14,10},{5,1},{7,3},{9,5},{11,7},{... | collective-permute-start | bytes 479240 | tf_op jit(solution)/shard_map/ppermute | solution.py:740
  278.1 2.9 copy-start.5
  278.1 2.9 copy-start.6
  278.2 57.2 %collective-permute-start.13 = (bf16[4,48,3072]{2,1,0:T(8,128)(2,1)S(1)}, bf16[4,48,3072]{2,1,0:T(8,128)(2,1)S(1)}, u32[]{:S(2)}, u32[]{:S(2)}) collective-permute-start(bf16[4,48,3072]{2,1,0:T(8,128)(2,1)S(1)} %get-tuple-element.341), channel_id=1, source_target_pairs={{0,2},{2,0},{4,6},{6,4},{8,10},{10,8},{12,14},{14,12},{1,3},{3,1},... | collective-permute-start | bytes 3538952 | tf_op jit(solution)/shard_map/ppermute | solution.py:745
  284.4 51.0 %collective-permute-start.14 = (bf16[8,24,2304]{2,1,0:T(8,128)(2,1)}, bf16[8,24,2304]{2,1,0:T(8,128)(2,1)S(1)}, u32[]{:S(2)}, u32[]{:S(2)}) collective-permute-start(bf16[8,24,2304]{2,1,0:T(8,128)(2,1)} %get-tuple-element.339), channel_id=1, source_target_pairs={{0,16},{16,0},{1,17},{17,1},{2,18},{18,2},{3,19},{19,3},{4,20},{20... | collective-permute-start | bytes 2654216 | tf_op jit(solution)/shard_map/ppermute | solution.py:745
  335.9 31.6 %collective-permute-start.19 = (bf16[2,48,3072]{2,1,0:T(8,128)(2,1)S(1)}, bf16[2,48,3072]{2,1,0:T(8,128)(2,1)S(1)}, u32[]{:S(2)}, u32[]{:S(2)}) collective-permute-start(bf16[2,48,3072]{2,1,0:T(8,128)(2,1)S(1)} %get-tuple-element.343), channel_id=1, source_target_pairs={{0,4},{2,6},{4,0},{6,2},{8,12},{10,14},{12,8},{14,10},{1,5},{3,7},... | collective-permute-start | bytes 1769480 | tf_op jit(solution)/shard_map/ppermute | solution.py:745
  339.7 27.8 %collective-permute-start.20 = (bf16[4,24,2304]{2,1,0:T(8,128)(2,1)S(1)}, bf16[4,24,2304]{2,1,0:T(8,128)(2,1)S(1)}, u32[]{:S(2)}, u32[]{:S(2)}) collective-permute-start(bf16[4,24,2304]{2,1,0:T(8,128)(2,1)S(1)} %get-tuple-element.345), channel_id=1, source_target_pairs={{0,2},{2,0},{4,6},{6,4},{8,10},{10,8},{12,14},{14,12},{1,3},{3,1},... | collective-permute-start | bytes 1327112 | tf_op jit(solution)/shard_map/ppermute | solution.py:745
  364.9 29.8 %collective-permute-start.17 = (bf16[208,384]{1,0:T(8,128)(2,1)}, bf16[208,384]{1,0:T(8,128)(2,1)S(1)}, u32[]{:S(2)}, u32[]{:S(2)}) collective-permute-start(bf16[208,384]{1,0:T(8,128)(2,1)} %get-tuple-element.232), channel_id=1, source_target_pairs={{2,0},{4,2},{6,4},{8,6},{10,8},{12,10},{14,12},{3,1},{5,3},{7,5},{... | collective-permute-start | bytes 479240 | tf_op jit(solution)/shard_map/ppermute | solution.py:740
  366.2 28.5 %collective-permute-start.18 = (bf16[208,384]{1,0:T(8,128)(2,1)}, bf16[208,384]{1,0:T(8,128)(2,1)S(1)}, u32[]{:S(2)}, u32[]{:S(2)}) collective-permute-start(bf16[208,384]{1,0:T(8,128)(2,1)} %get-tuple-element.233), channel_id=1, source_target_pairs={{4,0},{6,2},{8,4},{10,6},{12,8},{14,10},{5,1},{7,3},{9,5},{11,7},{... | collective-permute-start | bytes 479240 | tf_op jit(solution)/shard_map/ppermute | solution.py:740
  367.5 27.1 %copy-start.16 = (f32[1,384]{1,0:T(1,128)S(1)}, f32[1,384]{1,0:T(1,128)}, u32[]{:S(2)}) copy-start(f32[1,384]{1,0:T(1,128)} %get-tuple-element.272) | copy-start | bytes 4612
  367.5 27.1 %copy-start.18 = (f32[1,384]{1,0:T(1,128)S(1)}, f32[1,384]{1,0:T(1,128)}, u32[]{:S(2)}) copy-start(f32[1,384]{1,0:T(1,128)} %get-tuple-element.273) | copy-start | bytes 4612
  367.5 27.1 %copy-start.15 = (f32[1,384]{1,0:T(1,128)S(1)}, f32[1,384]{1,0:T(1,128)}, u32[]{:S(2)}) copy-start(f32[1,384]{1,0:T(1,128)} %get-tuple-element.270) | copy-start | bytes 4612
  367.6 27.1 %copy-start.17 = (f32[1,384]{1,0:T(1,128)S(1)}, f32[1,384]{1,0:T(1,128)}, u32[]{:S(2)}) copy-start(f32[1,384]{1,0:T(1,128)} %get-tuple-element.271) | copy-start | bytes 4612
  391.8 19.0 %collective-permute-start.23 = (bf16[208,384]{1,0:T(8,128)(2,1)}, bf16[208,384]{1,0:T(8,128)(2,1)S(1)}, u32[]{:S(2)}, u32[]{:S(2)}) collective-permute-start(bf16[208,384]{1,0:T(8,128)(2,1)} %get-tuple-element.264), channel_id=1, source_target_pairs={{2,0},{4,2},{6,4},{8,6},{10,8},{12,10},{14,12},{3,1},{5,3},{7,5},{... | collective-permute-start | bytes 479240 | tf_op jit(solution)/shard_map/ppermute | solution.py:740
  393.1 17.7 %collective-permute-start.24 = (bf16[208,384]{1,0:T(8,128)(2,1)}, bf16[208,384]{1,0:T(8,128)(2,1)S(1)}, u32[]{:S(2)}, u32[]{:S(2)}) collective-permute-start(bf16[208,384]{1,0:T(8,128)(2,1)} %get-tuple-element.265), channel_id=1, source_target_pairs={{4,0},{6,2},{8,4},{10,6},{12,8},{14,10},{5,1},{7,3},{9,5},{11,7},{... | collective-permute-start | bytes 479240 | tf_op jit(solution)/shard_map/ppermute | solution.py:740
  410.3 42.2 %collective-permute-start.30 = (bf16[8,24,2304]{2,1,0:T(8,128)(2,1)}, bf16[8,24,2304]{2,1,0:T(8,128)(2,1)S(1)}, u32[]{:S(2)}, u32[]{:S(2)}) collective-permute-start(bf16[8,24,2304]{2,1,0:T(8,128)(2,1)} %get-tuple-element.282), channel_id=1, source_target_pairs={{0,1},{1,0},{2,3},{3,2},{4,5},{5,4},{6,7},{7,6},{8,9},{9,8},{10,11... | collective-permute-start | bytes 2654216 | tf_op jit(solution)/shard_map/ppermute | solution.py:745
  410.3 42.2 %collective-permute-start.31 = (bf16[8,24,2304]{2,1,0:T(8,128)(2,1)}, bf16[8,24,2304]{2,1,0:T(8,128)(2,1)S(1)}, u32[]{:S(2)}, u32[]{:S(2)}) collective-permute-start(bf16[8,24,2304]{2,1,0:T(8,128)(2,1)} %get-tuple-element.284), channel_id=1, source_target_pairs={{0,1},{1,0},{2,3},{3,2},{4,5},{5,4},{6,7},{7,6},{8,9},{9,8},{10,11... | collective-permute-start | bytes 2654216 | tf_op jit(solution)/shard_map/ppermute | solution.py:745
  410.8 0.7 copy-start.9
  411.6 8.9 %copy-start.19 = (f32[1,384]{1,0:T(1,128)S(1)}, f32[1,384]{1,0:T(1,128)}, u32[]{:S(2)}) copy-start(f32[1,384]{1,0:T(1,128)} %get-tuple-element.268) | copy-start | bytes 4612
  411.6 9.6 %copy-start.11 = (f32[1,768]{1,0:T(1,128)S(1)}, f32[1,768]{1,0:T(1,128)}, u32[]{:S(2)}) copy-start(f32[1,768]{1,0:T(1,128)} %get-tuple-element.274) | copy-start | bytes 9220
  421.1 1.2 collective-permute-start.25
  421.3 19.9 %copy-start.3 = (bf16[1568,384]{1,0:T(8,128)(2,1)S(1)}, bf16[1568,384]{1,0:T(8,128)(2,1)}, u32[]{:S(2)}) copy-start(bf16[1568,384]{1,0:T(8,128)(2,1)} %get-tuple-element.235) | copy-start | bytes 3612676
  421.4 19.9 %copy-start.4 = (bf16[1568,384]{1,0:T(8,128)(2,1)S(1)}, bf16[1568,384]{1,0:T(8,128)(2,1)}, u32[]{:S(2)}) copy-start(bf16[1568,384]{1,0:T(8,128)(2,1)} %get-tuple-element.267) | copy-start | bytes 3612676
  422.4 7.0 %collective-permute-start.26 = (f32[1,1920]{1,0:T(1,128)S(1)}, f32[1,1920]{1,0:T(1,128)S(1)}, u32[]{:S(2)}, u32[]{:S(2)}) collective-permute-start(f32[1,1920]{1,0:T(1,128)S(1)} %fusion.24), channel_id=1, source_target_pairs={{0,16},{16,0},{1,17},{17,1},{2,18},{18,2},{3,19},{19,3},{4,20},{20... | collective-permute-start | bytes 23048 | tf_op jit(solution)/shard_map/ppermute | solution.py:745
  424.0 28.4 %collective-permute-start.37 = (bf16[2,24,2304]{2,1,0:T(8,128)(2,1)S(1)}, bf16[2,24,2304]{2,1,0:T(8,128)(2,1)S(1)}, u32[]{:S(2)}, u32[]{:S(2)}) collective-permute-start(bf16[2,24,2304]{2,1,0:T(8,128)(2,1)S(1)} %dynamic-slice_bitcast_fusion.7), channel_id=1, source_target_pairs={{0,4},{2,6},{4,0},{6,2},{8,12},{10,14},{12,8},{14,10},{1,5},{3,7},... | collective-permute-start | bytes 663560 | tf_op jit(solution)/shard_map/ppermute | solution.py:745
  429.4 3.7 collective-permute-start.27
  433.2 6.3 %collective-permute-start.28 = (f32[1,1920]{1,0:T(1,128)S(1)}, f32[1,1920]{1,0:T(1,128)S(1)}, u32[]{:S(2)}, u32[]{:S(2)}) collective-permute-start(f32[1,1920]{1,0:T(1,128)S(1)} %add.153), channel_id=1, source_target_pairs={{0,4},{2,6},{4,0},{6,2},{8,12},{10,14},{12,8},{14,10},{1,5},{3,7},... | collective-permute-start | bytes 23048 | tf_op jit(solution)/shard_map/ppermute | solution.py:745
  435.3 19.1 %collective-permute-start.40 = (bf16[1,48,3072]{2,1,0:T(8,128)(2,1)S(1)}, bf16[1,48,3072]{2,1,0:T(8,128)(2,1)S(1)}, u32[]{:S(2)}, u32[]{:S(2)}) collective-permute-start(bf16[1,48,3072]{2,1,0:T(8,128)(2,1)S(1)} %constant_dynamic-slice_fusion), channel_id=1, source_target_pairs={{0,8},{2,10},{4,12},{6,14},{8,0},{10,2},{12,4},{14,6},{1,9},{3,11}... | collective-permute-start | bytes 884744 | tf_op jit(solution)/shard_map/ppermute | solution.py:745
  439.5 11.7 %collective-permute-start.29 = (f32[1,1920]{1,0:T(1,128)S(1)}, f32[1,1920]{1,0:T(1,128)S(1)}, u32[]{:S(2)}, u32[]{:S(2)}) collective-permute-start(f32[1,1920]{1,0:T(1,128)S(1)} %add.154), channel_id=1, source_target_pairs={{0,8},{2,10},{4,12},{6,14},{8,0},{10,2},{12,4},{14,6},{1,9},{3,11}... | collective-permute-start | bytes 23048 | tf_op jit(solution)/shard_map/ppermute | solution.py:745
  441.2 11.3 %copy-start = (bf16[8,24,2304]{2,1,0:T(8,128)(2,1)S(1)}, bf16[8,24,2304]{2,1,0:T(8,128)(2,1)}, u32[]{:S(2)}) copy-start(bf16[8,24,2304]{2,1,0:T(8,128)(2,1)} %get-tuple-element.281) | copy-start | bytes 2654212
  441.2 11.4 %copy-start.1 = (bf16[8,24,2304]{2,1,0:T(8,128)(2,1)S(1)}, bf16[8,24,2304]{2,1,0:T(8,128)(2,1)}, u32[]{:S(2)}) copy-start(bf16[8,24,2304]{2,1,0:T(8,128)(2,1)} %get-tuple-element.283) | copy-start | bytes 2654212
  452.5 7.4 %collective-permute-start.38 = (bf16[1,24,2304]{2,1,0:T(8,128)(2,1)S(1)}, bf16[1,24,2304]{2,1,0:T(8,128)(2,1)S(1)}, u32[]{:S(2)}, u32[]{:S(2)}) collective-permute-start(bf16[1,24,2304]{2,1,0:T(8,128)(2,1)S(1)} %constant_dynamic-slice_fusion.1), channel_id=1, source_target_pairs={{0,8},{2,10},{4,12},{6,14},{8,0},{10,2},{12,4},{14,6},{1,9},{3,11}... | collective-permute-start | bytes 331784 | tf_op jit(solution)/shard_map/ppermute | solution.py:745
  453.1 22.6 %collective-permute-start.32 = (bf16[8,24,2304]{2,1,0:T(8,128)(2,1)S(1)}, bf16[8,24,2304]{2,1,0:T(8,128)(2,1)S(1)}, u32[]{:S(2)}, u32[]{:S(2)}) collective-permute-start(bf16[8,24,2304]{2,1,0:T(8,128)(2,1)S(1)} %select_convert_fusion.2), channel_id=1, source_target_pairs={{0,16},{16,0},{1,17},{17,1},{2,18},{18,2},{3,19},{19,3},{4,20},{20... | collective-permute-start | bytes 2654216 | tf_op jit(solution)/shard_map/ppermute | solution.py:745
  454.5 33.7 %collective-permute-start.41 = (bf16[48,3072]{1,0:T(8,128)(2,1)S(1)}, bf16[48,3072]{1,0:T(8,128)(2,1)S(1)}, u32[]{:S(2)}, u32[]{:S(2)}) collective-permute-start(bf16[48,3072]{1,0:T(8,128)(2,1)S(1)} %fusion.3), channel_id=1, source_target_pairs={{0,16},{16,0},{1,17},{17,1},{2,18},{18,2},{3,19},{19,3},{4,20},{20... | collective-permute-start | bytes 884744 | tf_op jit(solution)/shard_map/ppermute | solution.py:745
  459.9 23.1 %collective-permute-start.39 = (bf16[24,2304]{1,0:T(8,128)(2,1)S(1)}, bf16[24,2304]{1,0:T(8,128)(2,1)S(1)}, u32[]{:S(2)}, u32[]{:S(2)}) collective-permute-start(bf16[24,2304]{1,0:T(8,128)(2,1)S(1)} %fusion.5), channel_id=1, source_target_pairs={{0,16},{16,0},{1,17},{17,1},{2,18},{18,2},{3,19},{19,3},{4,20},{20... | collective-permute-start | bytes 331784 | tf_op jit(solution)/shard_map/ppermute | solution.py:745
  476.4 9.4 %collective-permute-start.33 = (bf16[4,24,2304]{2,1,0:T(8,128)(2,1)S(1)}, bf16[4,24,2304]{2,1,0:T(8,128)(2,1)S(1)}, u32[]{:S(2)}, u32[]{:S(2)}) collective-permute-start(bf16[4,24,2304]{2,1,0:T(8,128)(2,1)S(1)} %dynamic-slice_bitcast_fusion.4), channel_id=1, source_target_pairs={{0,2},{2,0},{4,6},{6,4},{8,10},{10,8},{12,14},{14,12},{1,3},{3,1},... | collective-permute-start | bytes 1327112 | tf_op jit(solution)/shard_map/ppermute | solution.py:745
  485.9 6.1 %collective-permute-start.34 = (bf16[2,24,2304]{2,1,0:T(8,128)(2,1)S(1)}, bf16[2,24,2304]{2,1,0:T(8,128)(2,1)S(1)}, u32[]{:S(2)}, u32[]{:S(2)}) collective-permute-start(bf16[2,24,2304]{2,1,0:T(8,128)(2,1)S(1)} %dynamic-slice_bitcast_fusion.8), channel_id=1, source_target_pairs={{0,4},{2,6},{4,0},{6,2},{8,12},{10,14},{12,8},{14,10},{1,5},{3,7},... | collective-permute-start | bytes 663560 | tf_op jit(solution)/shard_map/ppermute | solution.py:745
  492.1 5.7 %collective-permute-start.35 = (bf16[1,24,2304]{2,1,0:T(8,128)(2,1)S(1)}, bf16[1,24,2304]{2,1,0:T(8,128)(2,1)S(1)}, u32[]{:S(2)}, u32[]{:S(2)}) collective-permute-start(bf16[1,24,2304]{2,1,0:T(8,128)(2,1)S(1)} %constant_dynamic-slice_fusion.2), channel_id=1, source_target_pairs={{0,8},{2,10},{4,12},{6,14},{8,0},{10,2},{12,4},{14,6},{1,9},{3,11}... | collective-permute-start | bytes 331784 | tf_op jit(solution)/shard_map/ppermute | solution.py:745
  497.9 6.5 %collective-permute-start.36 = (bf16[24,2304]{1,0:T(8,128)(2,1)S(1)}, bf16[24,2304]{1,0:T(8,128)(2,1)S(1)}, u32[]{:S(2)}, u32[]{:S(2)}) collective-permute-start(bf16[24,2304]{1,0:T(8,128)(2,1)S(1)} %fusion.4), channel_id=1, source_target_pairs={{0,16},{16,0},{1,17},{17,1},{2,18},{18,2},{3,19},{19,3},{4,20},{20... | collective-permute-start | bytes 331784 | tf_op jit(solution)/shard_map/ppermute | solution.py:745
  (8 other events, 5.4 us)

commit v3 on v2

--- a/solution.py
+++ b/solution.py
@@ -25,8 +25,10 @@
 PR = 400
 MR = 208
 KR = PR + 2 * MR
-TILE = 224
+TILE = 784
 STEPS = QT // TILE
+PIECE = 224
+PIECES = QT // PIECE
 W1 = H1 * LANE
 W2 = H2 * LANE
 epsilon = 1e-06
@@ -186,22 +188,22 @@
     return f * (HT * WD) + r2 * (2 * WD) + a * WD + c2 * 2 + (s - 2 * a)
 
 
-def first_kernel(x, gain, xp, na, kv, mem, xs):
+def first_kernel(x, gain, xn, kv, mem, xs):
     for i in range(7):
         lo = 196 * i // 16 * 16
         hi = min(QT, (196 * i + 392 + 15) // 16 * 16)
-        shape = (TILE, hi - lo)
+        shape = (PIECE, hi - lo)
         pick = jnp.where(source_of(shape, 56 * i) == lanes(shape) + lo, 1.0, 0.0).astype(bf16)
         out = mm(pick, x[0, 0, 0, lo:hi, :])
         for s in range(4):
             xs[PT * s + 56 * i : PT * s + 56 * (i + 1), :] = out[56 * s : 56 * (s + 1)]
-    for i in range(STEPS):
-        at = slice(TILE * i, TILE * (i + 1))
+    for i in range(PIECES):
+        at = slice(PIECE * i, PIECE * (i + 1))
         v = xs[at, :]
         unit, _ = norm_stats(v)
         n = (unit * gain[...]).astype(bf16)
-        xp[at, :] = v.astype(bf16)
-        na[at, :] = n
+        xn[at, :D1] = v.astype(bf16)
+        xn[at, D1:] = n
         xs[at, :] = n.astype(f32)
     pooled = pool_rows(xs)
     kv[...] = pooled
@@ -210,8 +212,7 @@
 
 def first(inputs, video, gain):
     outs = [
-        shape_of((QT, D1), bf16),
-        shape_of((QT, D1), bf16),
+        shape_of((QT, 2 * D1), bf16),
         shape_of((PR, D1), bf16),
         shape_of((MR, D1), bf16),
     ]
@@ -238,8 +239,7 @@
         v_out[:, at] = (v[:, at] + ones).astype(bf16)
 
 
-def head_forward(q, k, v):
-    s = mm_nt(q, k)
+def head_forward(q, s, v):
     top = jnp.max(s, axis=-1, keepdims=True)
     e = jnp.exp2((s - top) * RATE).astype(bf16)
     mixed = mm(e, v)
@@ -253,8 +253,8 @@
 
 
 def block1_kernel(
-    kv, near, far, kext, na, xp, wq, wk, wv, wp, gain_m, wfc, wout, gain_c,
-    kall, k_out, v_out, qe, o_out, za, ha_out, nb_out, ub_out, gp_out, mid_out, pc, mem, xs,
+    kv, near, far, kext, xn, wq, wk, wv, wp, gain_m, wfc, wout, gain_c,
+    kall, k_out, v_out, ozq, hm, ubgp, pc, mem, xs,
 ):
     step = pl.program_id(0)
 
@@ -265,28 +265,32 @@
         kall[PR + MR : KR, :] = far[...]
         keys_ext(kall[...], wk[...], wv[...], kext[...], H1, k_out, v_out)
 
-    q = (mm(na[...], wq[...]) + one_lane((TILE, W1))).astype(bf16)
-    for h in range(H1):
-        at = slice(LANE * h, LANE * (h + 1))
-        o, qx = head_forward(q[:, at], k_out[:, at], v_out[:, at])
-        qe[:, at] = qx
-        o_out[:, at] = o.astype(bf16)
-        za[:, at] = (o + q[:, at].astype(f32)).astype(bf16)
-    ha = xp[...].astype(f32) + mm(za[...], wp[...])
-    ha_out[...] = ha
+    q = (mm(xn[:, D1:], wq[...]) + one_lane((TILE, W1))).astype(bf16)
+    heads = [slice(LANE * h, LANE * (h + 1)) for h in range(H1)]
+    scores = [mm_nt(q[:, at], k_out[:, at]) for at in heads]
+    for h, at in enumerate(heads):
+        o, qx = head_forward(q[:, at], scores[h], v_out[:, at])
+        ozq[:, 2 * W1 + LANE * h : 2 * W1 + LANE * (h + 1)] = qx
+        ozq[:, at] = o.astype(bf16)
+        ozq[:, W1 + LANE * h : W1 + LANE * (h + 1)] = (o + q[:, at].astype(f32)).astype(bf16)
+    ha = xn[:, :D1].astype(f32) + mm(ozq[:, W1 : 2 * W1], wp[...])
+    hm[:, :D1] = ha
     unit, _ = norm_stats(ha)
     nb = (unit * gain_m[...]).astype(bf16)
-    nb_out[...] = nb
     part = F1 // 3
     mid = ha
+    ahead = mm(nb, wfc[:, :part])
     for j in range(3):
         at = slice(part * j, part * (j + 1))
-        act, slope = gelu_both(mm(nb, wfc[:, at]))
+        inner = ahead
+        if j < 2:
+            ahead = mm(nb, wfc[:, part * (j + 1) : part * (j + 2)])
+        act, slope = gelu_both(inner)
         act = act.astype(bf16)
-        ub_out[:, at] = act
-        gp_out[:, at] = slope.astype(bf16)
+        ubgp[:, at] = act
+        ubgp[:, F1 + part * j : F1 + part * (j + 1)] = slope.astype(bf16)
         mid = mid + mm(act, wout[at, :])
-    mid_out[...] = mid
+    hm[:, D1:] = mid
     unit, _ = norm_stats(mid)
     xs[pl.ds(pl.multiple_of(step * TILE, TILE), TILE), :] = (unit * gain_c[...]).astype(bf16).astype(f32)
 
@@ -297,22 +301,17 @@
         mem[...] = mm(tmean_matrix(), pooled).astype(bf16)
 
 
-def block1(kv, near, far, kext, na, xp, w, wp, gain_m, wfc, wout, gain_c):
-    ins = [whole(kv), whole(near), whole(far), whole(kext), rows_tiled(na), rows_tiled(xp)]
+def block1(kv, near, far, kext, xn, w, wp, gain_m, wfc, wout, gain_c):
+    ins = [whole(kv), whole(near), whole(far), whole(kext), rows_tiled(xn)]
     ins += [cols_fixed(w, W1, j) for j in range(3)]
     ins += [whole(wp), whole(gain_m), whole(wfc), whole(wout), whole(gain_c)]
     outs = [
         whole(shape_of((KR, D1), bf16)),
         whole(shape_of((KR, W1), bf16)),
         whole(shape_of((KR, W1), bf16)),
-        rows_tiled(shape_of((QT, W1), bf16)),
-        rows_tiled(shape_of((QT, W1), bf16)),
-        rows_tiled(shape_of((QT, W1), bf16)),
-        rows_tiled(shape_of((QT, D1), f32)),
-        rows_tiled(shape_of((QT, D1), bf16)),
-        rows_tiled(shape_of((QT, F1), bf16)),
-        rows_tiled(shape_of((QT, F1), bf16)),
-        rows_tiled(shape_of((QT, D1), f32)),
+        rows_tiled(shape_of((QT, 3 * W1), bf16)),
+        rows_tiled(shape_of((QT, 2 * D1), f32)),
+        rows_tiled(shape_of((QT, 2 * F1), bf16)),
         whole(shape_of((PR, D1), bf16)),
         whole(shape_of((MR, D1), bf16)),
     ]
@@ -337,9 +336,10 @@
 
     keys_ext(kall[...], wk[...], wv[...], kext[...], 2, k_out, v_out)
     q = (mm(pc[...], wq[...]) + one_lane((PR, PAIR))).astype(bf16)
-    for h in range(2):
-        at = slice(LANE * h, LANE * (h + 1))
-        o, qx = head_forward(q[:, at], k_out[:, at], v_out[:, at])
+    heads = [slice(LANE * h, LANE * (h + 1)) for h in range(2)]
+    scores = [mm_nt(q[:, at], k_out[:, at]) for at in heads]
+    for h, at in enumerate(heads):
+        o, qx = head_forward(q[:, at], scores[h], v_out[:, at])
         qe[:, at] = qx
         o_out[:, at] = o.astype(bf16)
         zc[:, at] = (o + q[:, at].astype(f32)).astype(bf16)
@@ -547,11 +547,9 @@
 
 
 def mlp1_back_kernel(carry, *refs):
-    n_in = 14 + (3 if carry else 0)
-    dpc, rn, rf, gain_c, gain_m, mid, ha, nb, ub, gp, za, o, wout, wfc = refs[:14]
-    n_in += 1
-    wp = refs[14]
-    before = refs[15:n_in]
+    n_in = 11 + (3 if carry else 0)
+    dpc, rn, rf, gain_c, gain_m, hm, ubgp, oz, wout, wfc, wp = refs[:11]
+    before = refs[11:n_in]
     gha, gze, gg_c, gg_m, gw_out, gw_fc, gw_p, ds = refs[n_in:]
     step = pl.program_id(0)
 
@@ -566,37 +564,38 @@
         for i, ref in enumerate((gw_out, gw_fc, gw_p)):
             ref[...] = before[i][...] if carry else jnp.zeros_like(ref)
 
-    unit, inv = norm_stats(mid[...])
+    unit, inv = norm_stats(hm[:, D1:])
     dnc = ds[pl.ds(pl.multiple_of(step * TILE, TILE), TILE), :]
     gmid, dg = norm_back(dnc, unit, inv, gain_c[...])
     gg_c[...] += dg
     gm = gmid.astype(bf16)
     gmt = gm.T
-    nbt = nb[...].T
+    unit_b, inv_b = norm_stats(hm[:, :D1])
+    nbt = (unit_b * gain_m[...]).astype(bf16).T
     part = F1 // 3
     dn = jnp.zeros((TILE, D1), f32)
     for j in range(3):
         at = slice(part * j, part * (j + 1))
-        gi = (gp[:, at].astype(f32) * mm_nt(gm, wout[at, :])).astype(bf16)
-        gw_out[:, at] += mm(gmt, ub[:, at])
+        slope = ubgp[:, F1 + part * j : F1 + part * (j + 1)].astype(f32)
+        gi = (slope * mm_nt(gm, wout[at, :])).astype(bf16)
+        gw_out[:, at] += mm(gmt, ubgp[:, at])
         gw_fc[:, at] += mm(nbt, gi)
         dn = dn + mm_nt(gi, wfc[:, at])
-    unit, inv = norm_stats(ha[...])
-    dx, dg = norm_back(dn, unit, inv, gain_m[...])
+    dx, dg = norm_back(dn, unit_b, inv_b, gain_m[...])
     gg_m[...] += dg
     g = gmid + dx
     gha[...] = g
     gh = g.astype(bf16)
-    gw_p[...] += mm_tn(za[...], gh)
+    gw_p[...] += mm_tn(oz[:, W1:], gh)
     gz = mm_nt(gh, wp[...]).astype(bf16)
     for h in range(H1):
         at = slice(LANE * h, LANE * (h + 1))
-        gze[:, at] = grad_ext(gz[:, at], o[:, at])
-
-
-def mlp1_back(dpc, rn, rf, gain_c, gain_m, mid, ha, nb, ub, gp, za, o, wout, wfc, wp, before):
+        gze[:, at] = grad_ext(gz[:, at], oz[:, at])
+
+
+def mlp1_back(dpc, rn, rf, gain_c, gain_m, hm, ubgp, ozq, wout, wfc, wp, before):
     ins = [whole(a) for a in (dpc, rn, rf, gain_c, gain_m)]
-    ins += [rows_tiled(a) for a in (mid, ha, nb, ub, gp, za, o)]
+    ins += [rows_tiled(hm), rows_tiled(ubgp), (ozq, pl.BlockSpec((TILE, 2 * W1), lambda i: (i, 0)))]
     ins += [whole(wout), whole(wfc), whole(wp)]
     grads = [whole(shape_of((D1, F1), f32)), whole(shape_of((D1, F1), f32)), whole(shape_of((W1, D1), f32))]
     if before is not None:
@@ -624,7 +623,7 @@
 
 def att1_back_kernel(carry, *refs):
     n_in = 9 + (3 if carry else 0)
-    qe, gze, k, v, na, kall, wq, wk, wv = refs[:9]
+    qe, gze, k, v, xn, kall, wq, wk, wv = refs[:9]
     before = refs[9:n_in]
     dnear, dfar, down, dna, gq_w, gk_w, gv_w, dkv, nat = refs[n_in:]
     step = pl.program_id(0)
@@ -636,7 +635,7 @@
     def _():
         dkv[...] = jnp.zeros_like(dkv)
         dna[...] = jnp.zeros_like(dna)
-        nat[...] = na[...].T
+        nat[...] = xn[...].T
 
     gq, dk, dv = [[] for _ in QUERY_TILES], [], []
     for h in range(2):
@@ -665,10 +664,10 @@
         dfar[...] = dkv[PR + MR : KR, :].astype(bf16)
 
 
-def att1_back(qe, gze, k, v, na, kall, w, before):
+def att1_back(ozq, gze, k, v, xn, kall, w, before):
     pairs = H1 // 2
-    ins = [cols_tiled(a, PAIR) for a in (qe, gze, k, v)]
-    ins += [whole(na), whole(kall)]
+    ins = [cols_tiled(ozq, PAIR, 2 * pairs)] + [cols_tiled(a, PAIR) for a in (gze, k, v)]
+    ins += [cols_fixed(xn, D1, 1), whole(kall)]
     ins += [cols_tiled(w, PAIR, j * pairs) for j in range(3)]
     grads = [cols_tiled(shape_of((D1, W1), f32), PAIR) for _ in range(3)]
     if before is not None:
@@ -691,49 +690,6 @@
     )
 
 
-def last_kernel(dna, down, rn, rf, xp, gha, gain, gx, gg, gs, ds):
-    got = (rn[...].astype(f32) + rf[...].astype(f32)).astype(bf16)
-    d = 0.25 * (down[...] + mm_tn(tmean_matrix(), got))
-    for s in range(4):
-        ds[PT * s : PT * (s + 1), :] = d[0:PT]
-    total = jnp.zeros((1, D1), f32)
-    for i in range(STEPS):
-        at = slice(TILE * i, TILE * (i + 1))
-        unit, inv = norm_stats(xp[at, :].astype(f32))
-        dx, dg = norm_back(dna[at, :] + ds[at, :], unit, inv, gain[...])
-        total = total + dg
-        gs[at, :] = gha[at, :] + dx
-    gg[...] = total
-    for i in range(STEPS):
-        lo = min(CELL * i // 8 * 8, PT - 112)
-        window = jnp.concatenate([gs[PT * s + lo : PT * s + lo + 112, :] for s in range(4)], axis=0).astype(bf16)
-        shape = (TILE, 4 * 112)
-        t = rows_of(shape) + TILE * i
-        f = t // (HT * WD)
-        rest = t - f * (HT * WD)
-        r = rest // WD
-        c = rest - r * WD
-        r2 = r // 2
-        c2 = c // 2
-        s = 2 * (r - 2 * r2) + (c - 2 * c2)
-        p = f * CELL + r2 * 7 + c2
-        pick = jnp.where(s * 112 + p - lo == lanes(shape), 1.0, 0.0).astype(bf16)
-        gx[TILE * i : TILE * (i + 1), :] = mm(pick, window).astype(bf16)
-
-
-def last(dna, down, rn, rf, xp, gha, gain):
-    outs = [shape_of((QT, D1), bf16), shape_of((1, D1), f32)]
-    return call(
-        last_kernel,
-        (1,),
-        [whole(a) for a in (dna, down, rn, rf, xp, gha, gain)],
-        [whole(o) for o in outs],
-        [VMEM((QT, D1), f32), VMEM((QT, D1), f32)],
-        flops=2 * QT * 448 * D1,
-        name="last_norm_back",
-    )
-
-
 def shift(value, steps):
     count = lax.axis_size("clip")
     first_, last_ = (max(0, -steps), min(count, count - steps))
@@ -749,10 +705,30 @@
     return jnp.concatenate([grad[:, LANE * h : LANE * h + HD] for h in range(grad.shape[1] // LANE)], axis=1)
 
 
+def fold(v):
+    rows, cols = v.shape
+    if rows != 24:
+        return v
+    rest = jnp.concatenate([v[16:, : cols // 2], v[16:, cols // 2 :]], axis=0)
+    return jnp.concatenate([v[:16], rest], axis=1)
+
+
+def unfold(v, rows):
+    if rows != 24:
+        return v
+    cols = v.shape[1] * 2 // 3
+    rest = jnp.concatenate([v[:8, cols:], v[8:, cols:]], axis=1)
+    return jnp.concatenate([v[:, :cols], rest], axis=0)
+
+
+def folded(rows, cols):
+    return (16, cols * 3 // 2) if rows == 24 else (rows, cols)
+
+
 def pack2_kernel(micro, gq, gk, gv, gp, gs, keep_a, send_a, keep_b, send_b, qkv):
     for j, g in enumerate((gq, gk, gv)):
         qkv[:, D2 * j : D2 * (j + 1)] = strip(g[...])
-    clips, rows, _ = keep_a.shape
+    clips, rows = keep_a.shape[0], D1 // (2 * keep_a.shape[0])
     first_ = micro[0] == 0
 
     def proj(share, a):
@@ -769,13 +745,13 @@
             (keep_a, send_a, lambda n: qkv[rows * n : rows * (n + 1), :]),
             (keep_b, send_b, lambda n: jnp.concatenate([proj(n, 0), proj(n, 1), gs[rows * n : rows * (n + 1), :]], axis=1)),
         ):
-            k, t = pick_share(micro[0], piece(2 * i), piece(2 * i + 1))
+            k, t = pick_share(micro[0], fold(piece(2 * i)), fold(piece(2 * i + 1)))
             keep[i] = k
             send[i] = t
 
 
 def pack2(micro, clips, grads):
-    share = shape_of((clips, D1 // (2 * clips), 3 * D2), bf16)
+    share = shape_of((clips,) + folded(D1 // (2 * clips), 3 * D2), bf16)
     return call(
         pack2_kernel,
         (1,),
@@ -792,7 +768,7 @@
     for h in range(H1):
         qkv[HD * h : HD * (h + 1), 3 * D1 :] = gp[LANE * h : LANE * h + HD, :]
     out[...] = gout[...].T
-    clips, rows, _ = keep_a.shape
+    clips, rows = keep_a.shape[0], D1 // (2 * keep_a.shape[0])
     half = 2 * D1
 
     def piece_a(n):
@@ -806,13 +782,13 @@
 
     for i in range(clips):
         for keep, send, piece in ((keep_a, send_a, piece_a), (keep_b, send_b, piece_b)):
-            k, t = pick_share(micro[0], piece(2 * i), piece(2 * i + 1))
+            k, t = pick_share(micro[0], fold(piece(2 * i)), fold(piece(2 * i + 1)))
             keep[i] = k
             send[i] = t
 
 
 def pack1(micro, clips, grads):
-    share = shape_of((clips, D1 // (2 * clips), 6 * D1), bf16)
+    share = shape_of((clips,) + folded(D1 // (2 * clips), 6 * D1), bf16)
     return call(
         pack1_kernel,
         (1,),
@@ -827,35 +803,18 @@
     return a.astype(f32) + b.astype(f32)
 
 
-def over_micro(parts):
-    keep_a, send_a, keep_b, send_b = parts
-    return (keep_a, swap(send_a, "micro"), keep_b, swap(send_b, "micro"))
-
-
-def over_group(parts):
-    keep_a, got_a, keep_b, got_b = parts
-    first_ = lax.axis_index("group") == 0
-    a, b = add_up(keep_a, got_a), add_up(keep_b, got_b)
-    keep = jnp.where(first_, a, b).astype(bf16)
-    send = jnp.where(first_, b, a).astype(bf16)
-    return (keep, swap(send, "group"))
-
-
-def over_clip(parts, bit):
+def over_clip(parts, bit, bits_left):
     total = add_up(*parts).astype(bf16)
-    bits = lax.axis_size("clip").bit_length() - 1
-    v = total.reshape((2 ** (bits - bit - 1), 2) + total.shape[1:])
+    low = sum(1 for b in bits_left if b < bit)
+    left = len(bits_left)
+    v = total.reshape((2 ** (left - 1 - low), 2, 2**low) + total.shape[1:])
     mine = (lax.axis_index("clip") >> bit) & 1
-    keep = lax.dynamic_index_in_dim(v, mine, 1, keepdims=False)
-    send = lax.dynamic_index_in_dim(v, 1 - mine, 1, keepdims=False)
-    return (keep, swap(send, "clip", bit))
-
-
-def settle(parts):
-    total = add_up(*parts).astype(bf16)[0]
-    other = swap(total, "group")
-    first_ = lax.axis_index("group") == 0
-    return (jnp.where(first_, total, other).astype(f32), jnp.where(first_, other, total).astype(f32))
+
+    def part(which):
+        w = lax.dynamic_index_in_dim(v, which, 1, keepdims=False)
+        return w.reshape((2 ** (left - 1),) + total.shape[1:])
+
+    return (part(mine), swap(part(1 - mine), "clip", bit))
 
 
 def stack_blocks(v, count):
@@ -866,6 +825,223 @@
     flat, tree = jax.tree.flatten((held, others))
     held, others = jax.tree.unflatten(tree, lax.optimization_barrier(flat))
     return (held, *others)
+
+
+STREAMS = 4
+
+
+def bit_order(bits, stream):
+    order = list(range(bits))
+    if stream % 2 == 1 and bits > 1:
+        order[0], order[1] = 1, 0
+    return order
+
+
+def finish_kernel(clips, *refs):
+    videos = 2
+    sends, keeps = refs[:STREAMS], refs[STREAMS : 2 * STREAMS]
+    pos = 2 * STREAMS
+    big_keep, big_got = refs[pos : pos + 2], refs[pos + 2 : pos + 4]
+    gg_m, gg_c, gg_d, gain = refs[pos + 4 : pos + 8]
+    pos += 8
+    ins = [refs[pos + 6 * b : pos + 6 * (b + 1)] for b in range(videos)]
+    pos += 6 * videos
+    gx, gains = refs[pos : pos + 2]
+    done = refs[pos + 2 : pos + 2 + STREAMS]
+    big_done = refs[pos + 2 + STREAMS : pos + 4 + STREAMS]
+    pos += 4 + STREAMS
+    ds, gs, got0, big_sum, big_other, g_all, g_four = refs[pos : pos + 7]
+    pos += 7
+    bits = clips.bit_length() - 1
+    stage = [refs[pos + 3 * i : pos + 3 * (i + 1)] for i in range(bits)]
+    pos += 3 * bits
+    last_sum, last_got, sem_s, sem_r, gsem_s, gsem_r, fsem_s, fsem_r = refs[pos:]
+
+    g, c, m = (lax.axis_index(a) for a in ("group", "clip", "micro"))
+    barrier = pltpu.get_barrier_semaphore()
+    others = [{"clip": lax.rem(c + d, clips)} for d in range(1, clips)]
+    others += [{"micro": 1 - m}, {"group": 1 - g}, {"group": 1 - g, "micro": 1 - m}]
+    for other in others:
+        pl.semaphore_signal(barrier, inc=1, device_id=other, device_id_type=pl.DeviceIdType.MESH)
+    pl.semaphore_wait(barrier, len(others))
+
+    def remote(src, dst, number, other):
+        return pltpu.make_async_remote_copy(
+            src_ref=src,
+            dst_ref=dst,
+            send_sem=sem_s.at[number],
+            recv_sem=sem_r.at[number],
+            device_id=other,
+            device_id_type=pl.DeviceIdType.MESH,
+        )
+
+    copies = {}
+    for i in range(STREAMS):
+        copies[i] = remote(sends[i], got0.at[i], i, {"micro": 1 - m})
+        copies[i].start()
+    for i in range(2):
+        big_sum[i] = add_up(big_keep[i][0], big_got[i][0]).astype(bf16)
+        n = STREAMS * (bits + 2) + i
+        copies[n] = remote(big_sum.at[i], big_other.at[i], n, {"group": 1 - g})
+        copies[n].start()
+
+    def step_clip(number):
+        for i in range(STREAMS):
+            n = i + STREAMS * number
+            copies[n].wait()
+            order = bit_order(bits, i)
+            if number == 0:
+                keep, got = keeps[i], got0.at[i]
+            else:
+                keep, got = stage[number - 1][0].at[i], stage[number - 1][2].at[i]
+            if number == bits:
+                last_sum[i] = add_up(keep[0], got[0]).astype(bf16)
+                copies[n + STREAMS] = remote(last_sum.at[i], last_got.at[i], n + STREAMS, {"group": 1 - g})
+            else:
+                bit = order[number]
+                low = sum(1 for b in order[number + 1 :] if b < bit)
+                mine = lax.rem(lax.div(c, 2**bit), 2)
+                kp, sd, gt = stage[number]
+                for t in range(2 ** (bits - number - 1)):
+                    base = ((t >> low) << (low + 1)) + (t & (2**low - 1))
+                    away = base + (1 - mine) * 2**low
+                    home = base + mine * 2**low
+                    sd[i, t] = add_up(keep[away], got[away]).astype(bf16)
+                    kp[i, t] = add_up(keep[home], got[home]).astype(bf16)
+                partner = c + (1 - 2 * mine) * 2**bit
+                copies[n + STREAMS] = remote(sd.at[i], gt.at[i], n + STREAMS, {"clip": partner})
+            copies[n + STREAMS].start()
+
+    def norm_part(b):
+        dna, down, rn, rf, xn, gha = ins[b]
+        got = add_up(rn[...], rf[...]).astype(bf16)
+        d = 0.25 * (down[...] + mm_tn(tmean_matrix(), got))
+        for s in range(4):
+            ds[PT * s : PT * (s + 1), :] = d[0:PT]
+        total = jnp.zeros((1, D1), f32)
+        for i in range(PIECES):
+            at = slice(PIECE * i, PIECE * (i + 1))
+            unit, inv = norm_stats(xn[at, :].astype(f32))
+            dx, dg = norm_back(dna[at, :] + ds[at, :], unit, inv, gain[...])
+            total = total + dg
+            gs[at, :] = gha[at, :] + dx
+        return total
+
+    def order_part(b):
+        for i in range(PIECES):
+            lo = min(CELL * i // 8 * 8, PT - 112)
+            window = jnp.concatenate([gs[PT * s + lo : PT * s + lo + 112, :] for s in range(4)], axis=0).astype(bf16)
+            shape = (PIECE, 4 * 112)
+            t = rows_of(shape) + PIECE * i
+            f = t // (HT * WD)
+            rest = t - f * (HT * WD)
+            r = rest // WD
+            col = rest - r * WD
+            r2 = r // 2
+            c2 = col // 2
+            s = 2 * (r - 2 * r2) + (col - 2 * c2)
+            p = f * CELL + r2 * 7 + c2
+            pick = jnp.where(s * 112 + p - lo == lanes(shape), 1.0, 0.0).astype(bf16)
+            gx[b, PIECE * i : PIECE * (i + 1), :] = mm(pick, window).astype(bf16)
+
+    gg = norm_part(0)
+    step_clip(0)
+    order_part(0)
+    gg = gg + norm_part(1)
+    mine_all = g_all.at[c]
+    mine_all[...] = jnp.concatenate(
+        [gg, gg_m[...], gg_c[...], gg_d[:, :D1], gg_d[:, D1:], jnp.zeros((3, D1), f32)], axis=0
+    )
+    gcopies = []
+    for d in range(1, clips):
+        gcopies.append(
+            pltpu.make_async_remote_copy(
+                src_ref=g_all.at[c],
+                dst_ref=g_all.at[c],
+                send_sem=gsem_s.at[d - 1],
+                recv_sem=gsem_r.at[d - 1],
+                device_id={"clip": lax.rem(c + d, clips)},
+                device_id_type=pl.DeviceIdType.MESH,
+            )
+        )
+        gcopies[-1].start()
+    if bits > 0:
+        step_clip(1)
+    order_part(1)
+    for copy in gcopies:
+        copy.wait()
+    total = g_all[0]
+    for i in range(1, clips):
+        total = total + g_all[i]
+    place = 2 * g + m
+    g_four[place] = total
+    fcopies = []
+    for i, other in enumerate(others[-3:]):
+        fcopies.append(
+            pltpu.make_async_remote_copy(
+                src_ref=g_four.at[place],
+                dst_ref=g_four.at[place],
+                send_sem=fsem_s.at[i],
+                recv_sem=fsem_r.at[i],
+                device_id=other,
+                device_id_type=pl.DeviceIdType.MESH,
+            )
+        )
+        fcopies[-1].start()
+    for number in range(2, bits + 1):
+        step_clip(number)
+    for copy in fcopies:
+        copy.wait()
+    gains[...] = (g_four[0] + g_four[1]) + (g_four[2] + g_four[3])
+    first_ = g == 0
+    for i in range(2):
+        copies[STREAMS * (bits + 2) + i].wait()
+        big_done[i][...] = add_up(big_sum[i], big_other[i])
+    for i in range(STREAMS):
+        copies[i + STREAMS * (bits + 1)].wait()
+        done[i][...] = add_up(last_sum[i], last_got[i])
+
+
+def finish(clips, sends, keeps, big, gg_m, gg_c, gg_d, gain, videos):
+    bits = clips.bit_length() - 1
+    part = sends[0].shape[1:]
+    big_part = big[0][0].shape[1:]
+    hbm = pl.BlockSpec(memory_space=pl.ANY)
+    ins = [(a, hbm) for a in sends] + [whole(a) for a in keeps]
+    ins += [whole(b[0]) for b in big] + [whole(b[1]) for b in big]
+    ins += [whole(a) for a in (gg_m, gg_c, gg_d, gain)]
+    for dna, down, rn, rf, xn, gha in videos:
+        ins += [whole(a) for a in (dna, down, rn, rf)] + [cols_fixed(xn, D1, 0), whole(gha)]
+    outs = [whole(shape_of((2, QT, D1), bf16)), whole(shape_of((8, D1), f32))]
+    outs += [whole(shape_of(part, f32))] * STREAMS + [whole(shape_of(big_part, f32))] * 2
+    scratch = [
+        VMEM((QT, D1), f32),
+        VMEM((QT, D1), f32),
+        VMEM((STREAMS, clips) + part, bf16),
+        VMEM((2,) + big_part, bf16),
+        VMEM((2,) + big_part, bf16),
+        VMEM((clips, 8, D1), f32),
+        VMEM((4, 8, D1), f32),
+    ]
+    for i in range(bits):
+        scratch += [VMEM((STREAMS, 2 ** (bits - 1 - i)) + part, bf16)] * 3
+    count = STREAMS * (bits + 2) + 2
+    dma = pltpu.SemaphoreType.DMA
+    scratch += [VMEM((STREAMS,) + part, bf16)] * 2
+    scratch += [dma((count,))] * 2 + [dma((clips - 1,))] * 2 + [dma((3,))] * 2
+    arrays = [a for a, _ in ins]
+    return pl.pallas_call(
+        partial(finish_kernel, clips),
+        grid=(1,),
+        in_specs=[sp for _, sp in ins],
+        out_specs=[sp for _, sp in outs],
+        out_shape=[o for o, _ in outs],
+        scratch_shapes=scratch,
+        compiler_params=pltpu.CompilerParams(
+            vmem_limit_bytes=58 * 1024 * 1024, collective_id=1, has_side_effects=True
+        ),
+        name="finish",
+    )(*arrays)
 
 
 def body(inputs, offsets, cotangent, gain_attn1, w_qkv1, w_proj1, gain_mlp1, w_fc1, w_out1,
@@ -883,40 +1059,43 @@
     kext = kext.astype(f32)
 
     w1p, p1p, w2p, p2p = pad_weights(w_qkv1, w_proj1, w_qkv2, w_proj2)
-    xp, na, kva, mema = zip(*[first(inputs, b, g_a1) for b in videos])
+    xn, kva, mema = zip(*[first(inputs, b, g_a1) for b in videos])
     a = [
-        block1(kva[b], shift(mema[b], 1), shift(mema[b], 2), kext, na[b], xp[b], w1p, p1p, g_m1, w_fc1, w_out1, g_a2)
+        block1(kva[b], shift(mema[b], 1), shift(mema[b], 2), kext, xn[b], w1p, p1p, g_m1, w_fc1, w_out1, g_a2)
         for b in videos
     ]
-    ka, Ka, Va, qea, oa, za, ha, nb, ub, gp, mid, pc, memc = zip(*a)
+    ka, Ka, Va, ozq, hm, ubgp, pc, memc = zip(*a)
     c = [block2(pc[b], shift(memc[b], 1), shift(memc[b], 2), kext, w2p, w_skip, p2p) for b in videos]
     kc, Kc, Vc, qec, oc, zc, hc = zip(*c)
     micro, clips = lax.axis_index("micro"), lax.axis_size("clip")
     bits = clips.bit_length() - 1
     output, gh, keep_fc, send_fc, keep_out, send_out, gg_mlp2 = mlp2(micro, clips, hc[0], hc[1], cotangent, g_m2, w_fc2, w_out2)
-    big = over_micro((keep_fc, send_fc, keep_out, send_out))
+    big = [(keep_fc, swap(send_fc, "micro")), (keep_out, swap(send_out, "micro"))]
+    orders = [bit_order(bits, i) for i in range(2)]
+
+    def big_step(parts, number):
+        return [over_clip(p, o[number], o[number:]) for p, o in zip(parts, orders)]
 
     before, dn2, df2, dpc = None, [], [], []
     for b in videos:
         if b == 1:
             big, gh = tied(big, gh)
-            big = over_group(big)
+            big = big_step(big, 0)
         near, far, d, *before = att2_back(
             b, gh, p2p, qec[b], oc[b], Kc[b], Vc[b], zc[b], pc[b], kc[b], w_skip, w2p, before
         )
         dn2.append(shift(near, -1))
         df2.append(shift(far, -2))
         dpc.append(d)
-    middle = over_micro(pack2(micro, clips, before))
+    grads2 = pack2(micro, clips, before)
     before, gha, gze, gg_c, gg_m = None, [], [], 0.0, 0.0
     for b in videos:
         d = dpc[b]
         if b == 1:
-            big, middle, d = tied(big, middle, d)
-            big = over_clip(big, 0)
-            middle = over_group(middle)
+            big, d = tied(big, d)
+            big = big_step(big, 1)
         g, z, gc, gm, *before = mlp1_back(
-            d, dn2[b], df2[b], g_a2, g_m1, mid[b], ha[b], nb[b], ub[b], gp[b], za[b], oa[b], w_out1, w_fc1, p1p, before
+            d, dn2[b], df2[b], g_a2, g_m1, hm[b], ubgp[b], ozq[b], w_out1, w_fc1, p1p, before
         )
         gha.append(g)
         gze.append(z)
@@ -927,37 +1106,22 @@
     for b in videos:
         z = gze[b]
         if b == 0:
-            big, middle, z = tied(big, middle, z)
-            big = over_clip(big, 1)
-            middle = over_clip(middle, 0)
-        else:
-            big, middle, z = tied(big, middle, z)
-            for bit in range(2, bits):
-                big = over_clip(big, bit)
-            middle = over_clip(middle, 1)
-        near, far, d, dn, *before = att1_back(qea[b], z, Ka[b], Va[b], na[b], ka[b], w1p, before)
+            big, z = tied(big, z)
+            for number in range(2, bits):
+                big = big_step(big, number)
+        near, far, d, dn, *before = att1_back(ozq[b], z, Ka[b], Va[b], xn[b], ka[b], w1p, before)
         dn1.append(shift(near, -1))
         df1.append(shift(far, -2))
         down.append(d)
         dna.append(dn)
-    small = over_micro(pack1(micro, clips, list(before) + [gp1, gw_fc1, gw_out1t]))
-    ends = [last(dna[b], down[b], dn1[b], df1[b], xp[b], gha[b], g_a1) for b in videos]
-    gx = jnp.stack([e[0] for e in ends])
-    gg_a = ends[0][1] + ends[1][1]
-    gains = jnp.concatenate([gg_a, gg_m, gg_c, gg_mlp2], axis=1)
-    gains = gains + swap(gains, "micro")
-    gains = gains + swap(gains, "group")
-    for bit in range(bits):
-        gains = gains + swap(gains, "clip", bit)
-    for bit in range(2, bits):
-        middle = over_clip(middle, bit)
-    small = over_group(small)
-    for bit in range(bits):
-        small = over_clip(small, bit)
-    gw_fc2, gw_out2 = settle(big)
-    gw_qkv2, rest2 = settle(middle)
-    left, right = settle(small)
-    r = rest2.shape[0]
+    grads1 = pack1(micro, clips, list(before) + [gp1, gw_fc1, gw_out1t])
+    keeps = [grads2[0], grads2[2], grads1[0], grads1[2]]
+    sends = [grads2[1], grads2[3], grads1[1], grads1[3]]
+    ends = [(dna[b], down[b], dn1[b], df1[b], xn[b], gha[b]) for b in videos]
+    gx, gains, *sums = finish(clips, sends, keeps, big, gg_m, gg_c, gg_mlp2, g_a1, ends)
+    rows = D1 // (2 * clips)
+    gw_qkv2, rest2, left, right = (unfold(v, rows) for v in sums[:STREAMS])
+    gw_fc2, gw_out2 = sums[STREAMS:]
     shares = (
         jnp.concatenate([left[:, F1:], right[:, F1 : F1 + D1]], axis=1),
         right[:, F1 + D1 :],
@@ -969,8 +1133,8 @@
         gw_fc2,
         stack_blocks(gw_out2, 4),
     )
-    gains = jnp.split(gains.reshape(-1), [D1, 2 * D1, 3 * D1])
-    return (output, gx.reshape(inputs.shape)) + tuple(gains) + tuple(v.reshape(-1) for v in shares)
+    gains = (gains[0], gains[1], gains[2], gains[3:5].reshape(-1))
+    return (output, gx.reshape(inputs.shape)) + gains + tuple(v.reshape(-1) for v in shares)
 
 
 def solution(mesh):

time: 513 us -> 484 us (0.943)
  waiting for transfers between devices: 52.9 us -> 17.2 us
  Pallas kernels: 340 us -> 374 us
  starting transfers between devices: 76.4 us -> 44.1 us
  local copies, waits for them, and re-layouts: 17.1 us -> 31.3 us
  other arithmetic: 18.9 us -> 7.67 us
    pallas_call x0 -> x1, Pallas kernels: none -> 71.7 us  [finish(): pl.pallas_call(partial(finish_kernel, clips), grid=(1,), in_specs=[sp for...]
    ppermute x26 -> x8, waiting for transfers between devices: 52.9 us -> 0.8 us  [swap(): return lax.ppermute(value, axis, [(i, i ^ 1 << bit) for i in range(n)])]
    pallas_call x18 -> x16, Pallas kernels: 340 us -> 302 us  [call(): pl.pallas_call(kernel, grid=grid, in_specs=[s for _, s in ins], out_specs...]
    ppermute x26 -> x8, starting transfers between devices: 40.7 us -> 9.05 us  [swap(): return lax.ppermute(value, axis, [(i, i ^ 1 << bit) for i in range(n)])]
    ppermute x16, waiting for transfers between devices: 0.04 us -> 16.4 us  [shift(): lax.ppermute(value, 'clip', [(s, s + steps) for s in range(first_, last_)])]
    convert_element_type x6 -> x0, other arithmetic: 10.8 us -> none  [the longest x3 10.7 us: over_group(): send = jnp.where(first_, b, a).astype(bf16)]
    slice x2 -> x10, local copies, waits for them, and re-layouts: 0.02 us -> 8.99 us  [the longest x4 3.68 us: unfold(): return jnp.concatenate([v[:, :cols], rest], axis=0)]
  transfers between devices with their start and end apart: 42 -> 24, of which waited for: 13 -> 6; matrix products, arithmetic and copies ran while one was open for 4% -> 2% of each run, Pallas kernels for 55% -> 51%
where the time goes in v3:
time: 484 us; the launch traced here: 476 us
  Pallas kernels  374 us (77%)
  starting transfers between devices  44.1 us (9%)
  local copies, waits for them, and re-layouts  31.3 us (6%)
  waiting for transfers between devices  17.2 us (4%)
  other arithmetic  7.67 us (2%)
    pallas_call x16, Pallas kernels, call(): pl.pallas_call(kernel, grid=grid, in_specs=[s for _, s in ins], out_specs...  302 us
    pallas_call x1, Pallas kernels, finish(): pl.pallas_call(partial(finish_kernel, clips), grid=(1,), in_specs=[sp for...  71.7 us
    ppermute x16, starting transfers between devices, shift(): lax.ppermute(value, 'clip', [(s, s + steps) for s in range(first_, last_)])  35 us
    ppermute x16, waiting for transfers between devices, shift(): lax.ppermute(value, 'clip', [(s, s + steps) for s in range(first_, last_)])  16.4 us
  transfers between devices with their start and end apart: 24, of which 6 were waited for; matrix products, arithmetic and copies ran while one was open for 2% of the time, Pallas kernels for 51%

profile of v3, /device:TPU:0, one launch (start us, length us, event | category | flops | bytes accessed | tf_op | source)
XLA Modules:
  0.0 476.2 jit_solution(12408633137195918040)
XLA Ops:
  0.6 1.2 reshape.215.gain.refs_15_
  1.9 6.0 %first_norm.3 = (bf16[1568,768]{1,0:T(8,128)(2,1)}, bf16[400,384]{1,0:T(8,128)(2,1)}, bf16[208,384]{1,0:T(8,128)(2,1)}) custom-call(bf16[1,2,1,1568,384]{4,3,2,1,0:T(8,128)(2,1)} %x.3, f32[1,384]{1,0:T(1,128)} %reshape.215.gain.refs_15_), custom_call_target="tpu_custom_call" | custom-call | flops 500957184 | bytes 5285376 | tf_op jit(solution)/shard_map/first_norm/pallas_call | solution.py:120
  7.9 4.8 %collective-permute-start.4 = (bf16[208,384]{1,0:T(8,128)(2,1)}, bf16[208,384]{1,0:T(8,128)(2,1)S(1)}, u32[]{:S(2)}, u32[]{:S(2)}) collective-permute-start(bf16[208,384]{1,0:T(8,128)(2,1)} %get-tuple-element.148), channel_id=1, source_target_pairs={{0,2},{2,4},{4,6},{6,8},{8,10},{10,12},{12,14},{1,3},{3,5},{5,7},{... | collective-permute-start | bytes 479240 | tf_op jit(solution)/shard_map/ppermute | solution.py:696
  12.7 3.5 collective-permute-start.5
  16.2 5.9 %first_norm.2 = (bf16[1568,768]{1,0:T(8,128)(2,1)}, bf16[400,384]{1,0:T(8,128)(2,1)}, bf16[208,384]{1,0:T(8,128)(2,1)}) custom-call(bf16[1,2,1,1568,384]{4,3,2,1,0:T(8,128)(2,1)} %x.3, f32[1,384]{1,0:T(1,128)} %reshape.215.gain.refs_15_), custom_call_target="tpu_custom_call" | custom-call | flops 500957184 | bytes 5285376 | tf_op jit(solution)/shard_map/first_norm/pallas_call | solution.py:120
  22.1 3.4 collective-permute-start
  25.6 3.5 collective-permute-start.1
  31.5 5.8 %pad_heads.1 = (bf16[384,1536]{1,0:T(8,128)(2,1)}, bf16[512,384]{1,0:T(8,128)(2,1)}, bf16[384,3072]{1,0:T(8,128)(2,1)}, bf16[1024,768]{1,0:T(8,128)(2,1)}) custom-call(bf16[384,1152]{1,0:T(8,128)(2,1)} %wa.1, bf16[384,384]{1,0:T(8,128)(2,1)} %pa.1, bf16[384,2304]{1,0:T(8,128)(2,1)} %wc.1, bf16[768,768]{1,0:T(8,128)(2,1)} %pc.1), custom_call_target="tpu_custom_call" | custom-call | bytes 9633792 | tf_op jit(solution)/shard_map/pad_heads/pallas_call | solution.py:120
  37.3 0.9 broadcast_select_fusion.kext
  38.9 31.3 %block1_forward.3 = (bf16[816,384]{1,0:T(8,128)(2,1)}, bf16[816,512]{1,0:T(8,128)(2,1)}, bf16[816,512]{1,0:T(8,128)(2,1)}, bf16[1568,1536]{1,0:T(8,128)(2,1)}, f...) custom-call(bf16[400,384]{1,0:T(8,128)(2,1)} %get-tuple-element.147.kv, ...), custom_call_target="tpu_custom_call" | custom-call | flops 10173284352 | bytes 31779840 | tf_op jit(solution)/shard_map/block1_forward/pallas_call | solution.py:120
  70.2 3.4 collective-permute-start.6
  73.6 1.9 collective-permute-start.7
  76.3 31.5 %block1_forward.2 = (bf16[816,384]{1,0:T(8,128)(2,1)}, bf16[816,512]{1,0:T(8,128)(2,1)}, bf16[816,512]{1,0:T(8,128)(2,1)}, bf16[1568,1536]{1,0:T(8,128)(2,1)}, f...) custom-call(bf16[400,384]{1,0:T(8,128)(2,1)} %get-tuple-element.137.kv, ...), custom_call_target="tpu_custom_call" | custom-call | flops 10173284352 | bytes 31779840 | tf_op jit(solution)/shard_map/block1_forward/pallas_call | solution.py:120
  107.8 1.9 collective-permute-start.2
  109.7 1.9 collective-permute-start.3
  112.3 13.1 %block2_attention.3 = (bf16[816,384]{1,0:T(8,128)(2,1)}, bf16[816,1024]{1,0:T(8,128)(2,1)}, bf16[816,1024]{1,0:T(8,128)(2,1)}, bf16[400,1024]{1,0:T(8,128)(2,1)}...) custom-call(bf16[400,384]{1,0:T(8,128)(2,1)} %get-tuple-element.150.pc.refs_7_, ...), custom_call_target="tpu_custom_call" | custom-call | flops 5136973824 | bytes 17940480 | tf_op jit(solution)/shard_map/block2_attention/pallas_call | solution.py:120
  126.2 13.2 %block2_attention.2 = (bf16[816,384]{1,0:T(8,128)(2,1)}, bf16[816,1024]{1,0:T(8,128)(2,1)}, bf16[816,1024]{1,0:T(8,128)(2,1)}, bf16[400,1024]{1,0:T(8,128)(2,1)}...) custom-call(bf16[400,384]{1,0:T(8,128)(2,1)} %get-tuple-element.142.pc.refs_7_, ...), custom_call_target="tpu_custom_call" | custom-call | flops 5136973824 | bytes 17940480 | tf_op jit(solution)/shard_map/block2_attention/pallas_call | solution.py:120
  139.4 39.8 %block2_mlp.1 = (bf16[1,2,1,392,768]{4,3,2,1,0:T(8,128)(2,1)}, bf16[2,400,768]{2,1,0:T(8,128)(2,1)}, bf16[8,48,3072]{2,1,0:T(8,128)(2,1)}, bf16[8,48,3072]{2,1,0...) custom-call(s32[1]{0:T(128)} %bitcast.micro, ...), custom_call_target="tpu_custom_call" | custom-call | flops 22649241600 | bytes 24975364 | tf_op jit(solution)/shard_map/block2_mlp/pallas_call | solution.py:120
  180.3 22.5 %block2_attention_back.2 = (bf16[208,384]{1,0:T(8,128)(2,1)}, bf16[208,384]{1,0:T(8,128)(2,1)}, f32[400,384]{1,0:T(8,128)}, f32[384,1024]{1,0:T(8,128)}, f32[384...) custom-call(bf16[2,400,768]{2,1,0:T(8,128)(2,1)} %get-tuple-element.159.refs_0_, ...), custom_call_target="tpu_custom_call" | custom-call | flops 13026459648 | bytes 27189248 | tf_op jit(solution)/shard_map/block2_attention_back/pallas_call | solution.py:120
  202.9 1.3 collective-permute-start.14
  204.2 1.3 collective-permute-start.15
  205.5 5.6 %collective-permute-done.14.refs_1_ = bf16[208,384]{1,0:T(8,128)(2,1)S(1)} collective-permute-done((bf16[208,384]{1,0:T(8,128)(2,1)}, bf16[208,384]{1,0:T(8,128)(2,1)S(1)}, u32[]{:S(2)}, u32[]{:S(2)}) %collective-permute-start.14) | collective-permute-done | bytes 159776 | tf_op jit(solution)/shard_map/ppermute | solution.py:696
  211.1 3.7 collective-permute-done.15.refs_2_
  215.4 23.4 %block1_mlp_back.2 = (f32[1568,384]{1,0:T(8,128)}, bf16[1568,512]{1,0:T(8,128)(2,1)}, f32[1,384]{1,0:T(1,128)}, f32[1,384]{1,0:T(1,128)}, f32[384,1536]{1,0:T(8,...) custom-call(f32[400,384]{1,0:T(8,128)} %get-tuple-element.195.refs_0_, bf16[208,384]{1,0:T(8,128)(2,1)} %copy-done.20, ...), custom_call_target="tpu_custom_call" | custom-call | flops 8631877632 | bytes 32479232 | tf_op jit(solution)/shard_map/block1_mlp_back/pallas_call | solution.py:120
  238.9 4.4 add_convert_fusion
  243.7 1.2 dynamic-slice_bitcast_fusion
  244.9 23.7 %block2_attention_back.3 = (bf16[208,384]{1,0:T(8,128)(2,1)}, bf16[208,384]{1,0:T(8,128)(2,1)}, f32[400,384]{1,0:T(8,128)}, f32[384,1024]{1,0:T(8,128)}, f32[384...) custom-call(bf16[2,400,768]{2,1,0:T(8,128)(2,1)} %get-tuple-element.159.refs_0_, ...), custom_call_target="tpu_custom_call" | custom-call | flops 13026459648 | bytes 36233216 | tf_op jit(solution)/shard_map/block2_attention_back/pallas_call | solution.py:120
  268.6 1.3 collective-permute-start.12
  269.9 1.3 collective-permute-start.13
  271.2 0.8 collective-permute-done.10
  272.5 1.9 collective-permute-start.17
  275.0 2.7 collective-permute-start.16
  277.8 4.8 %collective-permute-done.13.refs_2_ = bf16[208,384]{1,0:T(8,128)(2,1)S(1)} collective-permute-done((bf16[208,384]{1,0:T(8,128)(2,1)}, bf16[208,384]{1,0:T(8,128)(2,1)S(1)}, u32[]{:S(2)}, u32[]{:S(2)}) %collective-permute-start.13) | collective-permute-done | bytes 159776 | tf_op jit(solution)/shard_map/ppermute | solution.py:696
  283.3 25.2 %block1_mlp_back.3 = (f32[1568,384]{1,0:T(8,128)}, bf16[1568,512]{1,0:T(8,128)(2,1)}, f32[1,384]{1,0:T(1,128)}, f32[1,384]{1,0:T(1,128)}, f32[384,1536]{1,0:T(8,...) custom-call(f32[400,384]{1,0:T(8,128)} %get-tuple-element.190.refs_0_, bf16[208,384]{1,0:T(8,128)(2,1)} %copy-done.23, ...), custom_call_target="tpu_custom_call" | custom-call | flops 8631877632 | bytes 37984256 | tf_op jit(solution)/shard_map/block1_mlp_back/pallas_call | solution.py:120
  308.7 0.8 constant_dynamic-slice_fusion
  309.4 1.8 collective-permute-start.19
  311.2 23.8 %block1_attention_back.2 = (bf16[208,384]{1,0:T(8,128)(2,1)}, bf16[208,384]{1,0:T(8,128)(2,1)}, f32[400,384]{1,0:T(8,128)}, f32[1568,384]{1,0:T(8,128)}, f32[384...) custom-call(bf16[1568,1536]{1,0:T(8,128)(2,1)} %get-tuple-element.200.refs_7_.refs_0_, ...), custom_call_target="tpu_custom_call" | custom-call | flops 15618539520 | bytes 20369408 | tf_op jit(solution)/shard_map/block1_attention_back/pallas_call | solution.py:120
  335.1 24.5 %block1_attention_back.3 = (bf16[208,384]{1,0:T(8,128)(2,1)}, bf16[208,384]{1,0:T(8,128)(2,1)}, f32[400,384]{1,0:T(8,128)}, f32[1568,384]{1,0:T(8,128)}, f32[384...) custom-call(bf16[1568,1536]{1,0:T(8,128)(2,1)} %get-tuple-element.184.refs_7_.refs_0_, ...), custom_call_target="tpu_custom_call" | custom-call | flops 15618539520 | bytes 22728704 | tf_op jit(solution)/shard_map/block1_attention_back/pallas_call | solution.py:120
  359.7 1.4 collective-permute-start.22
  361.2 0.8 constant_dynamic-slice_fusion.1
  362.0 1.7 collective-permute-start.18
  363.7 1.3 collective-permute-start.23
  365.0 1.3 collective-permute-start.20
  366.3 2.2 collective-permute-done.22.refs_24_
  368.5 1.5 collective-permute-start.21
  370.0 6.2 %pack_block2_grads.1 = (bf16[8,16,3456]{2,1,0:T(8,128)(2,1)}, bf16[8,16,3456]{2,1,0:T(8,128)(2,1)}, bf16[8,16,3456]{2,1,0:T(8,128)(2,1)}, bf16[8,16,3456]{2,1,0:T(8,128)(2,1)}) custom-call(s32[1]{0:T(128)} %bitcast.micro, f32[384,1024]{1,0:T(8,128)} %get-tuple-element.177.gq, f32[384,1024]{1,0:T(8,128)} %get-tuple-element.178.gk, ...), custom_call_target="tpu_custom_call" | custom-call | bytes 12582916 | tf_op jit(solution)/shard_map/pack_block2_grads/pallas_call | solution.py:120
  377.4 6.0 %pack_block1_grads.1 = (bf16[8,16,3456]{2,1,0:T(8,128)(2,1)}, bf16[8,16,3456]{2,1,0:T(8,128)(2,1)}, bf16[8,16,3456]{2,1,0:T(8,128)(2,1)}, bf16[8,16,3456]{2,1,0:T(8,128)(2,1)}) custom-call(s32[1]{0:T(128)} %bitcast.micro, f32[384,512]{1,0:T(8,128)} %get-tuple-element.220.gq, f32[384,512]{1,0:T(8,128)} %get-tuple-element.221.gk, ...), custom_call_target="tpu_custom_call" | custom-call | bytes 11403268 | tf_op jit(solution)/shard_map/pack_block1_grads/pallas_call | solution.py:120
  384.3 71.7 %finish.1 = (bf16[2,1568,384]{2,1,0:T(8,128)(2,1)}, f32[8,384]{1,0:T(8,128)}, f32[16,3456]{1,0:T(8,128)}, f32[16,3456]{1,0:T(8,128)}, f32[16,3456]{1,0:T(8,128)}...) custom-call(bf16[8,16,3456]{2,1,0:T(8,128)(2,1)} %get-tuple-element.182.refs_0_, ...), custom_call_target="tpu_custom_call" | custom-call | tf_op jit(solution)/shard_map/finish/pallas_call | solution.py:1033
  456.1 0.9 slice.88
  457.0 0.8 fusion.18
  457.8 0.9 slice.85
  458.7 0.8 fusion.19
  459.5 0.9 slice.79
  460.5 0.8 fusion.21
  461.2 0.9 slice.75
  462.2 0.8 fusion.22
  463.0 0.7 slice.74
  463.7 1.4 slice_reduce_fusion
  465.1 1.2 fusion.16
  466.3 0.9 reshape.241
  467.2 0.7 reshape.238
  468.6 0.7 reshape.237
  472.0 2.0 copy.33
  474.6 1.4 copy.36
  (117 shorter events, 15.0 us)
Async XLA Ops:
  1.9 27.8 %copy-start.10 = (f32[384]{0:T(512)S(1)}, f32[384]{0:T(512)}, u32[]{:S(2)}) copy-start(f32[384]{0:T(512)} %param.22) | copy-start | bytes 4612
  1.9 28.4 %copy-start.11 = (f32[384]{0:T(512)S(1)}, f32[384]{0:T(512)}, u32[]{:S(2)}) copy-start(f32[384]{0:T(512)} %param.25) | copy-start | bytes 4612
  1.9 29.0 %copy-start.9 = (f32[768]{0:T(1024)S(1)}, f32[768]{0:T(1024)}, u32[]{:S(2)}) copy-start(f32[768]{0:T(1024)} %param.29) | copy-start | bytes 9220
  7.9 30.4 %collective-permute-start.4 = (bf16[208,384]{1,0:T(8,128)(2,1)}, bf16[208,384]{1,0:T(8,128)(2,1)S(1)}, u32[]{:S(2)}, u32[]{:S(2)}) collective-permute-start(bf16[208,384]{1,0:T(8,128)(2,1)} %get-tuple-element.148), channel_id=1, source_target_pairs={{0,2},{2,4},{4,6},{6,8},{8,10},{10,12},{12,14},{1,3},{3,5},{5,7},{... | collective-permute-start | bytes 479240 | tf_op jit(solution)/shard_map/ppermute | solution.py:696
  12.7 25.5 %collective-permute-start.5 = (bf16[208,384]{1,0:T(8,128)(2,1)}, bf16[208,384]{1,0:T(8,128)(2,1)S(1)}, u32[]{:S(2)}, u32[]{:S(2)}) collective-permute-start(bf16[208,384]{1,0:T(8,128)(2,1)} %get-tuple-element.148), channel_id=1, source_target_pairs={{0,4},{2,6},{4,8},{6,10},{8,12},{10,14},{1,5},{3,7},{5,9},{7,11},{... | collective-permute-start | bytes 479240 | tf_op jit(solution)/shard_map/ppermute | solution.py:696
  22.1 53.5 %collective-permute-start = (bf16[208,384]{1,0:T(8,128)(2,1)}, bf16[208,384]{1,0:T(8,128)(2,1)S(1)}, u32[]{:S(2)}, u32[]{:S(2)}) collective-permute-start(bf16[208,384]{1,0:T(8,128)(2,1)} %get-tuple-element.138), channel_id=1, source_target_pairs={{0,2},{2,4},{4,6},{6,8},{8,10},{10,12},{12,14},{1,3},{3,5},{5,7},{... | collective-permute-start | bytes 479240 | tf_op jit(solution)/shard_map/ppermute | solution.py:696
  25.6 50.0 %collective-permute-start.1 = (bf16[208,384]{1,0:T(8,128)(2,1)}, bf16[208,384]{1,0:T(8,128)(2,1)S(1)}, u32[]{:S(2)}, u32[]{:S(2)}) collective-permute-start(bf16[208,384]{1,0:T(8,128)(2,1)} %get-tuple-element.138), channel_id=1, source_target_pairs={{0,4},{2,6},{4,8},{6,10},{8,12},{10,14},{1,5},{3,7},{5,9},{7,11},{... | collective-permute-start | bytes 479240 | tf_op jit(solution)/shard_map/ppermute | solution.py:696
  38.2 0.7 copy-start.24
  38.2 0.7 copy-start.26
  70.2 41.4 %collective-permute-start.6 = (bf16[208,384]{1,0:T(8,128)(2,1)}, bf16[208,384]{1,0:T(8,128)(2,1)S(1)}, u32[]{:S(2)}, u32[]{:S(2)}) collective-permute-start(bf16[208,384]{1,0:T(8,128)(2,1)} %get-tuple-element.151), channel_id=1, source_target_pairs={{0,2},{2,4},{4,6},{6,8},{8,10},{10,12},{12,14},{1,3},{3,5},{5,7},{... | collective-permute-start | bytes 479240 | tf_op jit(solution)/shard_map/ppermute | solution.py:696
  73.6 38.0 %collective-permute-start.7 = (bf16[208,384]{1,0:T(8,128)(2,1)}, bf16[208,384]{1,0:T(8,128)(2,1)S(1)}, u32[]{:S(2)}, u32[]{:S(2)}) collective-permute-start(bf16[208,384]{1,0:T(8,128)(2,1)} %get-tuple-element.151), channel_id=1, source_target_pairs={{0,4},{2,6},{4,8},{6,10},{8,12},{10,14},{1,5},{3,7},{5,9},{7,11},{... | collective-permute-start | bytes 479240 | tf_op jit(solution)/shard_map/ppermute | solution.py:696
  75.6 0.7 copy-start.18
  75.6 0.7 copy-start.19
  107.8 17.7 %collective-permute-start.2 = (bf16[208,384]{1,0:T(8,128)(2,1)}, bf16[208,384]{1,0:T(8,128)(2,1)S(1)}, u32[]{:S(2)}, u32[]{:S(2)}) collective-permute-start(bf16[208,384]{1,0:T(8,128)(2,1)} %get-tuple-element.143), channel_id=1, source_target_pairs={{0,2},{2,4},{4,6},{6,8},{8,10},{10,12},{12,14},{1,3},{3,5},{5,7},{... | collective-permute-start | bytes 479240 | tf_op jit(solution)/shard_map/ppermute | solution.py:696
  109.7 15.8 %collective-permute-start.3 = (bf16[208,384]{1,0:T(8,128)(2,1)}, bf16[208,384]{1,0:T(8,128)(2,1)S(1)}, u32[]{:S(2)}, u32[]{:S(2)}) collective-permute-start(bf16[208,384]{1,0:T(8,128)(2,1)} %get-tuple-element.143), channel_id=1, source_target_pairs={{0,4},{2,6},{4,8},{6,10},{8,12},{10,14},{1,5},{3,7},{5,9},{7,11},{... | collective-permute-start | bytes 479240 | tf_op jit(solution)/shard_map/ppermute | solution.py:696
  111.6 0.7 copy-start.27
  111.6 0.7 copy-start.28
  125.5 0.7 copy-start.29
  125.5 0.7 copy-start.30
  179.2 59.7 %collective-permute-start.8 = (bf16[8,48,3072]{2,1,0:T(8,128)(2,1)}, bf16[8,48,3072]{2,1,0:T(8,128)(2,1)}, u32[]{:S(2)}, u32[]{:S(2)}) collective-permute-start(bf16[8,48,3072]{2,1,0:T(8,128)(2,1)} %get-tuple-element.155), channel_id=1, source_target_pairs={{0,1},{1,0},{2,3},{3,2},{4,5},{5,4},{6,7},{7,6},{8,9},{9,8},{10,11... | collective-permute-start | bytes 7077896 | tf_op jit(solution)/shard_map/ppermute | solution.py:701
  179.2 59.6 %collective-permute-start.9 = (bf16[8,48,3072]{2,1,0:T(8,128)(2,1)}, bf16[8,48,3072]{2,1,0:T(8,128)(2,1)}, u32[]{:S(2)}, u32[]{:S(2)}) collective-permute-start(bf16[8,48,3072]{2,1,0:T(8,128)(2,1)} %get-tuple-element.157), channel_id=1, source_target_pairs={{0,1},{1,0},{2,3},{3,2},{4,5},{5,4},{6,7},{7,6},{8,9},{9,8},{10,11... | collective-permute-start | bytes 7077896 | tf_op jit(solution)/shard_map/ppermute | solution.py:701
  202.9 8.2 %collective-permute-start.14 = (bf16[208,384]{1,0:T(8,128)(2,1)}, bf16[208,384]{1,0:T(8,128)(2,1)S(1)}, u32[]{:S(2)}, u32[]{:S(2)}) collective-permute-start(bf16[208,384]{1,0:T(8,128)(2,1)} %get-tuple-element.196), channel_id=1, source_target_pairs={{2,0},{4,2},{6,4},{8,6},{10,8},{12,10},{14,12},{3,1},{5,3},{7,5},{... | collective-permute-start | bytes 479240 | tf_op jit(solution)/shard_map/ppermute | solution.py:696
  204.2 10.6 %collective-permute-start.15 = (bf16[208,384]{1,0:T(8,128)(2,1)}, bf16[208,384]{1,0:T(8,128)(2,1)S(1)}, u32[]{:S(2)}, u32[]{:S(2)}) collective-permute-start(bf16[208,384]{1,0:T(8,128)(2,1)} %get-tuple-element.197), channel_id=1, source_target_pairs={{4,0},{6,2},{8,4},{10,6},{12,8},{14,10},{5,1},{7,3},{9,5},{11,7},{... | collective-permute-start | bytes 479240 | tf_op jit(solution)/shard_map/ppermute | solution.py:696
  211.1 3.7 copy-start.20
  214.8 0.7 copy-start.22
  215.4 23.5 %copy-start.1 = (bf16[8,48,3072]{2,1,0:T(8,128)(2,1)S(1)}, bf16[8,48,3072]{2,1,0:T(8,128)(2,1)}, u32[]{:S(2)}) copy-start(bf16[8,48,3072]{2,1,0:T(8,128)(2,1)} %get-tuple-element.185) | copy-start | bytes 7077892
  215.4 23.5 %copy-start.2 = (bf16[8,48,3072]{2,1,0:T(8,128)(2,1)S(1)}, bf16[8,48,3072]{2,1,0:T(8,128)(2,1)}, u32[]{:S(2)}) copy-start(bf16[8,48,3072]{2,1,0:T(8,128)(2,1)} %get-tuple-element.187) | copy-start | bytes 7077892
  243.4 27.8 %collective-permute-start.11 = (bf16[4,48,3072]{2,1,0:T(8,128)(2,1)S(1)}, bf16[4,48,3072]{2,1,0:T(8,128)(2,1)S(1)}, u32[]{:S(2)}, u32[]{:S(2)}) collective-permute-start(bf16[4,48,3072]{2,1,0:T(8,128)(2,1)S(1)} %bitcast.32), channel_id=1, source_target_pairs={{0,4},{2,6},{4,0},{6,2},{8,12},{10,14},{12,8},{14,10},{1,5},{3,7},... | collective-permute-start | bytes 3538952 | tf_op jit(solution)/shard_map/ppermute | solution.py:701
  244.9 27.1 %collective-permute-start.10 = (bf16[4,48,3072]{2,1,0:T(8,128)(2,1)}, bf16[4,48,3072]{2,1,0:T(8,128)(2,1)S(1)}, u32[]{:S(2)}, u32[]{:S(2)}) collective-permute-start(bf16[4,48,3072]{2,1,0:T(8,128)(2,1)} %get-tuple-element.294), channel_id=1, source_target_pairs={{0,2},{2,0},{4,6},{6,4},{8,10},{10,8},{12,14},{14,12},{1,3},{3,1},... | collective-permute-start | bytes 3538952 | tf_op jit(solution)/shard_map/ppermute | solution.py:701
  268.6 9.2 %collective-permute-start.12 = (bf16[208,384]{1,0:T(8,128)(2,1)}, bf16[208,384]{1,0:T(8,128)(2,1)S(1)}, u32[]{:S(2)}, u32[]{:S(2)}) collective-permute-start(bf16[208,384]{1,0:T(8,128)(2,1)} %get-tuple-element.191), channel_id=1, source_target_pairs={{2,0},{4,2},{6,4},{8,6},{10,8},{12,10},{14,12},{3,1},{5,3},{7,5},{... | collective-permute-start | bytes 479240 | tf_op jit(solution)/shard_map/ppermute | solution.py:696
  269.9 12.7 %collective-permute-start.13 = (bf16[208,384]{1,0:T(8,128)(2,1)}, bf16[208,384]{1,0:T(8,128)(2,1)S(1)}, u32[]{:S(2)}, u32[]{:S(2)}) collective-permute-start(bf16[208,384]{1,0:T(8,128)(2,1)} %get-tuple-element.192), channel_id=1, source_target_pairs={{4,0},{6,2},{8,4},{10,6},{12,8},{14,10},{5,1},{7,3},{9,5},{11,7},{... | collective-permute-start | bytes 479240 | tf_op jit(solution)/shard_map/ppermute | solution.py:696
  272.5 36.0 %collective-permute-start.17 = (bf16[2,48,3072]{2,1,0:T(8,128)(2,1)S(1)}, bf16[2,48,3072]{2,1,0:T(8,128)(2,1)S(1)}, u32[]{:S(2)}, u32[]{:S(2)}) collective-permute-start(bf16[2,48,3072]{2,1,0:T(8,128)(2,1)S(1)} %get-tuple-element.296), channel_id=1, source_target_pairs={{0,2},{2,0},{4,6},{6,4},{8,10},{10,8},{12,14},{14,12},{1,3},{3,1},... | collective-permute-start | bytes 1769480 | tf_op jit(solution)/shard_map/ppermute | solution.py:701
  275.0 33.5 %collective-permute-start.16 = (bf16[2,48,3072]{2,1,0:T(8,128)(2,1)S(1)}, bf16[2,48,3072]{2,1,0:T(8,128)(2,1)S(1)}, u32[]{:S(2)}, u32[]{:S(2)}) collective-permute-start(bf16[2,48,3072]{2,1,0:T(8,128)(2,1)S(1)} %get-tuple-element.298), channel_id=1, source_target_pairs={{0,4},{2,6},{4,0},{6,2},{8,12},{10,14},{12,8},{14,10},{1,5},{3,7},... | collective-permute-start | bytes 1769480 | tf_op jit(solution)/shard_map/ppermute | solution.py:701
  277.8 4.8 %copy-start.23 = (bf16[208,384]{1,0:T(8,128)(2,1)}, bf16[208,384]{1,0:T(8,128)(2,1)S(1)}, u32[]{:S(2)}) copy-start(bf16[208,384]{1,0:T(8,128)(2,1)S(1)} %collective-permute-done.12.refs_1_) | copy-start | bytes 479236
  282.6 0.7 copy-start.25
  309.4 74.0 %collective-permute-start.19 = (bf16[1,48,3072]{2,1,0:T(8,128)(2,1)S(1)}, bf16[1,48,3072]{2,1,0:T(8,128)(2,1)S(1)}, u32[]{:S(2)}, u32[]{:S(2)}) collective-permute-start(bf16[1,48,3072]{2,1,0:T(8,128)(2,1)S(1)} %get-tuple-element.304), channel_id=1, source_target_pairs={{0,8},{2,10},{4,12},{6,14},{8,0},{10,2},{12,4},{14,6},{1,9},{3,11}... | collective-permute-start | bytes 884744 | tf_op jit(solution)/shard_map/ppermute | solution.py:701
  359.6 4.1 copy-start.21
  359.6 5.4 %copy-start.17 = (bf16[208,384]{1,0:T(8,128)(2,1)S(1)}, bf16[208,384]{1,0:T(8,128)(2,1)}, u32[]{:S(2)}) copy-start(bf16[208,384]{1,0:T(8,128)(2,1)} %get-tuple-element.243) | copy-start | bytes 479236
  359.6 8.9 %copy-start.16 = (bf16[208,384]{1,0:T(8,128)(2,1)S(1)}, bf16[208,384]{1,0:T(8,128)(2,1)}, u32[]{:S(2)}) copy-start(bf16[208,384]{1,0:T(8,128)(2,1)} %get-tuple-element.244) | copy-start | bytes 479236
  359.7 8.8 %collective-permute-start.22 = (bf16[208,384]{1,0:T(8,128)(2,1)}, bf16[208,384]{1,0:T(8,128)(2,1)S(1)}, u32[]{:S(2)}, u32[]{:S(2)}) collective-permute-start(bf16[208,384]{1,0:T(8,128)(2,1)} %get-tuple-element.248), channel_id=1, source_target_pairs={{2,0},{4,2},{6,4},{8,6},{10,8},{12,10},{14,12},{3,1},{5,3},{7,5},{... | collective-permute-start | bytes 479240 | tf_op jit(solution)/shard_map/ppermute | solution.py:696
  362.0 21.4 %collective-permute-start.18 = (bf16[1,48,3072]{2,1,0:T(8,128)(2,1)S(1)}, bf16[1,48,3072]{2,1,0:T(8,128)(2,1)S(1)}, u32[]{:S(2)}, u32[]{:S(2)}) collective-permute-start(bf16[1,48,3072]{2,1,0:T(8,128)(2,1)S(1)} %get-tuple-element.306), channel_id=1, source_target_pairs={{0,8},{2,10},{4,12},{6,14},{8,0},{10,2},{12,4},{14,6},{1,9},{3,11}... | collective-permute-start | bytes 884744 | tf_op jit(solution)/shard_map/ppermute | solution.py:701
  363.7 19.6 %collective-permute-start.23 = (bf16[208,384]{1,0:T(8,128)(2,1)S(1)}, bf16[208,384]{1,0:T(8,128)(2,1)S(1)}, u32[]{:S(2)}, u32[]{:S(2)}) collective-permute-start(bf16[208,384]{1,0:T(8,128)(2,1)S(1)} %copy-done.21), channel_id=1, source_target_pairs={{4,0},{6,2},{8,4},{10,6},{12,8},{14,10},{5,1},{7,3},{9,5},{11,7},{... | collective-permute-start | bytes 479240 | tf_op jit(solution)/shard_map/ppermute | solution.py:696
  365.0 18.3 %collective-permute-start.20 = (bf16[208,384]{1,0:T(8,128)(2,1)S(1)}, bf16[208,384]{1,0:T(8,128)(2,1)S(1)}, u32[]{:S(2)}, u32[]{:S(2)}) collective-permute-start(bf16[208,384]{1,0:T(8,128)(2,1)S(1)} %copy-done.17), channel_id=1, source_target_pairs={{2,0},{4,2},{6,4},{8,6},{10,8},{12,10},{14,12},{3,1},{5,3},{7,5},{... | collective-permute-start | bytes 479240 | tf_op jit(solution)/shard_map/ppermute | solution.py:696
  368.5 7.7 %copy-start.5 = (bf16[208,384]{1,0:T(8,128)(2,1)}, bf16[208,384]{1,0:T(8,128)(2,1)S(1)}, u32[]{:S(2)}) copy-start(bf16[208,384]{1,0:T(8,128)(2,1)S(1)} %collective-permute-done.22.refs_24_) | copy-start | bytes 479236
  368.5 14.9 %collective-permute-start.21 = (bf16[208,384]{1,0:T(8,128)(2,1)S(1)}, bf16[208,384]{1,0:T(8,128)(2,1)S(1)}, u32[]{:S(2)}, u32[]{:S(2)}) collective-permute-start(bf16[208,384]{1,0:T(8,128)(2,1)S(1)} %copy-done.16), channel_id=1, source_target_pairs={{4,0},{6,2},{8,4},{10,6},{12,8},{14,10},{5,1},{7,3},{9,5},{11,7},{... | collective-permute-start | bytes 479240 | tf_op jit(solution)/shard_map/ppermute | solution.py:696
  370.0 6.3 %copy-start.13 = (f32[1,384]{1,0:T(1,128)S(1)}, f32[1,384]{1,0:T(1,128)}, u32[]{:S(2)}) copy-start(f32[1,384]{1,0:T(1,128)} %get-tuple-element.238) | copy-start | bytes 4612
  370.0 6.3 %copy-start.15 = (f32[1,384]{1,0:T(1,128)S(1)}, f32[1,384]{1,0:T(1,128)}, u32[]{:S(2)}) copy-start(f32[1,384]{1,0:T(1,128)} %get-tuple-element.239) | copy-start | bytes 4612
  370.0 6.8 %copy-start.12 = (f32[1,384]{1,0:T(1,128)S(1)}, f32[1,384]{1,0:T(1,128)}, u32[]{:S(2)}) copy-start(f32[1,384]{1,0:T(1,128)} %get-tuple-element.236) | copy-start | bytes 4612
  370.0 6.8 %copy-start.14 = (f32[1,384]{1,0:T(1,128)S(1)}, f32[1,384]{1,0:T(1,128)}, u32[]{:S(2)}) copy-start(f32[1,384]{1,0:T(1,128)} %get-tuple-element.237) | copy-start | bytes 4612
  383.4 0.7 copy-start.6
  383.4 0.7 copy-start.7
  383.4 0.7 copy-start.8
  383.4 0.8 copy-start.3
  383.4 0.9 copy-start.4
  468.5 6.0 %copy-start = (bf16[2,1568,384]{2,1,0:T(8,128)(2,1)S(1)}, bf16[2,1568,384]{2,1,0:T(8,128)(2,1)}, u32[]{:S(2)}) copy-start(bf16[2,1568,384]{2,1,0:T(8,128)(2,1)} %get-tuple-element.251) | copy-start | bytes 7225348

commit v4 on v3

v4 whole, which is shorter than its diff:
```python
from functools import partial

import jax
import jax.numpy as jnp
from jax import lax
from jax.experimental import pallas as pl
from jax.experimental.pallas import tpu as pltpu
from jax.sharding import PartitionSpec as P

D1 = 384
D2 = 768
F1 = 1536
F2 = 3072
QT = 1568
PT = 392
MT = 196
HD = 96
FR = 8
HT = 14
WD = 14
H1 = 4
H2 = 8
CELL = (HT // 2) * (WD // 2)
LANE = 128
PR = 400
MR = 208
KR = PR + 2 * MR
TILE = 784
STEPS = QT // TILE
PIECE = 224
PIECES = QT // PIECE
W1 = H1 * LANE
W2 = H2 * LANE
epsilon = 1e-06
f32 = jnp.float32
bf16 = jnp.bfloat16
SCALE = HD ** (-0.5)
RATE = SCALE * 1.4426950408889634
VMEM_LIMIT = 60 * 1024 * 1024
VMEM = pltpu.VMEM


def mm(a, b):
    return lax.dot_general(a, b, (((1,), (0,)), ((), ())), preferred_element_type=f32)


def mm_nt(a, b):
    return lax.dot_general(a, b, (((1,), (1,)), ((), ())), preferred_element_type=f32)


def mm_tn(a, b):
    return lax.dot_general(a, b, (((0,), (0,)), ((), ())), preferred_element_type=f32)


def lanes(shape):
    return lax.broadcasted_iota(jnp.int32, shape, len(shape) - 1)


def rows_of(shape):
    return lax.broadcasted_iota(jnp.int32, shape, len(shape) - 2)


def norm_stats(values):
    center = values - jnp.mean(values, axis=-1, keepdims=True)
    inv = lax.rsqrt(jnp.mean(center * center, axis=-1, keepdims=True) + epsilon)
    return (center * inv, inv)


def norm_back(grad, unit, inv, gain):
    du = grad * gain
    dg = jnp.sum(grad * unit, axis=0, keepdims=True)
    dx = inv * (
        du - jnp.mean(du, axis=-1, keepdims=True) - unit * jnp.mean(du * unit, axis=-1, keepdims=True)
    )
    return (dx, dg)


def gelu_both(x):
    z = jnp.abs(x)
    t = 1.0 / (1.0 + 0.23164188 * z)
    e = jnp.exp2(x * x * -0.7213475204444817)
    poly = t * (0.127414796 + t * (-0.142248368 + t * (0.7107068705 + t * (-0.7265760135 + t * 0.5307027145))))
    tail = poly * e
    phi = jnp.where(x >= 0.0, 1.0 - tail, tail)
    return (x * phi, phi + (x * 0.3989422804014327) * e)


def split3(v):
    hi = v.astype(bf16).astype(f32)
    mid = (v - hi).astype(bf16).astype(f32)
    return (hi, mid, v - hi - mid)


def put3(base, v):
    hi, mid, low = split3(v)
    lane = lanes(base.shape)
    return jnp.where(
        lane < HD, base, jnp.where(lane == HD, hi, jnp.where(lane == HD + 1, mid, jnp.where(lane == HD + 2, low, base)))
    )


def tmean_matrix():
    rows = rows_of((MR, PR))
    cols = lanes((MR, PR))
    hit = rows < 0
    for pair in range(FR // 2):
        inside = (rows >= pair * CELL) & (rows < (pair + 1) * CELL)
        shift_by = cols - rows - pair * CELL
        hit = hit | (inside & ((shift_by == 0) | (shift_by == CELL)))
    return jnp.where(hit, 0.5, 0.0).astype(bf16)


def pool_rows(ref):
    total = ref[0:PT, :] + ref[PT : 2 * PT, :] + ref[2 * PT : 3 * PT, :] + ref[3 * PT : 4 * PT, :]
    return jnp.concatenate([0.25 * total, jnp.zeros((PR - PT, total.shape[1]), f32)], axis=0).astype(bf16)


MESH = pl.DeviceIdType.MESH
HBM = pl.BlockSpec(memory_space=pl.ANY)


def add_up(a, b):
    return a.astype(f32) + b.astype(f32)


class Shift:
    def __init__(self, source, steps, begin, end, inner=False):
        self.source = source
        self.ins = [] if isinstance(source, int) else [(source, HBM)]
        shape = (MR, D1)
        self.outs = [] if inner else [whole(shape_of(shape, bf16))]
        self.scratch = [VMEM(shape, bf16)]
        self.peers = [("shift", steps), ("shift", -steps)]
        self.steps, self.inner = steps, inner
        self.sems = 1
        self.events = {begin: [self.start], end: [self.finish]}

    def copy(self, refs, sems, args):
        src = args[self.source] if isinstance(self.source, int) else refs[0]
        return pltpu.make_async_remote_copy(
            src_ref=src, dst_ref=refs[-1], send_sem=sems[0].at[0], recv_sem=sems[1].at[0],
            device_id={"clip": lax.axis_index("clip") + self.steps}, device_id_type=MESH,
        )

    def start(self, refs, sems, args):
        pl.when(exists(self.steps))(lambda: self.copy(refs, sems, args).start())

    def finish(self, refs, sems, args):
        land = refs[-1]
        pl.when(exists(self.steps))(lambda: self.copy(refs, sems, args).wait_send())
        pl.when(exists(-self.steps))(lambda: self.copy(refs, sems, args).wait_recv())

        @pl.when(jnp.logical_not(exists(-self.steps)))
        def _():
            land[...] = jnp.zeros_like(land)

        if not self.inner:
            refs[-2][...] = land[...]


class Chain:
    def __init__(self, parts, order, plan, last):
        keep, other = parts
        self.order, self.plan = order, plan
        first_ = plan[0][0]
        tail = keep.shape[1:]
        self.ins = [(keep, HBM), (other, HBM)]
        self.scratch = [VMEM(keep.shape, bf16), VMEM(other.shape, bf16)]
        count = keep.shape[0]
        for number, _ in plan:
            if number >= 0:
                count //= 2
                self.scratch += [VMEM((count,) + tail, bf16)] * 2
                if number != plan[-1][0]:
                    self.scratch.append(VMEM((count,) + tail, bf16))
        self.only_swap = plan[-1][0] < 0
        final = (shape_of((count,) + tail, bf16), HBM)
        self.outs = [final] if self.only_swap else [whole(final[0]), final]
        self.peers = [("micro", 0) if n < 0 else ("bit", order[n]) for n, _ in plan]
        self.sems = len(plan) + 2
        self.events = {(0, 0): [self.load]}
        for i, (_, step) in enumerate(plan):
            self.events.setdefault((step, 0), []).append(partial(self.advance, i))
        self.events.setdefault((last, 1), []).append(self.finish)
        self.first = first_

    def slots(self, refs):
        keep, other = refs[:2]
        outs = refs[2 : 2 + len(self.outs)]
        held = refs[2 + len(self.outs) :]
        pos, slots = 2, []
        for i, (number, _) in enumerate(self.plan):
            final = i == len(self.plan) - 1
            if number < 0:
                slots.append((held[0], other, outs[-1] if final else held[1]))
                continue
            kept, away = held[pos], held[pos + 1]
            pos += 2
            if final:
                slots.append((kept, away, outs[-1]))
            else:
                slots.append((kept, away, held[pos]))
                pos += 1
        return slots

    def load(self, refs, sems, args):
        n = len(self.plan)
        held = refs[2 + len(self.outs) :]
        if not self.only_swap:
            pltpu.make_async_copy(refs[0], held[0], sems[0].at[n]).start()
        if self.first >= 0:
            pltpu.make_async_copy(refs[1], held[1], sems[0].at[n + 1]).start()

    def loaded(self, refs, sems, other):
        n = len(self.plan)
        held = refs[2 + len(self.outs) :]
        pltpu.make_async_copy(refs[0], held[0], sems[0].at[n]).wait()
        if other:
            pltpu.make_async_copy(refs[1], held[1], sems[0].at[n + 1]).wait()

    def copy(self, i, refs, sems):
        number = self.plan[i][0]
        _, away, land = self.slots(refs)[i]
        to = {"micro": 1 - lax.axis_index("micro")} if number < 0 else {"clip": flipped(self.order[number])}
        return pltpu.make_async_remote_copy(
            src_ref=away, dst_ref=land, send_sem=sems[0].at[i], recv_sem=sems[1].at[i],
            device_id=to, device_id_type=MESH,
        )

    def advance(self, i, refs, sems, args):
        number = self.plan[i][0]
        slots = self.slots(refs)
        if i > 0:
            self.copy(i - 1, refs, sems).wait()
        if number >= 0:
            if i == 0:
                self.loaded(refs, sems, True)
                held = refs[2 + len(self.outs) :]
                keep, got = held[0], held[1]
            else:
                if self.plan[i - 1][0] < 0:
                    self.loaded(refs, sems, False)
                keep, got = slots[i - 1][0], slots[i - 1][2]
            kept, away, _ = slots[i]
            bit = self.order[number]
            low = sum(1 for b in self.order[number + 1 :] if b < bit)
            split_shares(keep, got, kept, away, bit, low, kept.shape[0])
        self.copy(i, refs, sems).start()

    def finish(self, refs, sems, args):
        self.copy(len(self.plan) - 1, refs, sems).wait()
        if not self.only_swap:
            refs[2][...] = self.slots(refs)[-1][0][...]


def side(bit):
    return lax.rem(lax.div(lax.axis_index("clip"), 2**bit), 2)


def flipped(bit):
    return lax.axis_index("clip") + (1 - 2 * side(bit)) * 2**bit


def exists(steps):
    other = lax.axis_index("clip") + steps
    return jnp.logical_and(other >= 0, other < lax.axis_size("clip"))


def split_shares(keep, got, kept, send, bit, low, half):
    mine = side(bit)
    for t in range(half):
        base = ((t >> low) << (low + 1)) + (t & (2**low - 1))
        away = base + (1 - mine) * 2**low
        home = base + mine * 2**low
        send[t] = keep[away] + got[away]
        kept[t] = keep[home] + got[home]


def greet(peers):
    barrier = pltpu.get_barrier_semaphore()
    count = jnp.int32(0)
    for kind, arg in sorted(set(peers)):
        if kind == "shift":
            there = exists(arg)
            to = {"clip": lax.axis_index("clip") + arg}

            @pl.when(there)
            def _():
                pl.semaphore_signal(barrier, inc=1, device_id=to, device_id_type=MESH)

            count = count + there.astype(jnp.int32)
        else:
            to = {"micro": 1 - lax.axis_index("micro")} if kind == "micro" else {"clip": flipped(arg)}
            pl.semaphore_signal(barrier, inc=1, device_id=to, device_id_type=MESH)
            count = count + 1
    pl.semaphore_wait(barrier, count)


def call(kernel, grid, ins, outs, scratch=(), flops=0, name=None, jobs=(), tag=None):
    ins, outs, scratch = list(ins), list(outs), list(scratch)
    n_in, n_out, n_scratch = len(ins), len(outs), len(scratch)
    places = []
    for job in jobs:
        places.append((len(ins), len(outs), len(scratch)))
        ins += job.ins
        outs += job.outs
        scratch += job.scratch + [pltpu.SemaphoreType.DMA((job.sems,))] * 2

    def body_(*refs):
        i, o = len(ins), len(ins) + len(outs)
        args = refs[:n_in] + refs[i : i + n_out] + refs[o : o + n_scratch]
        if not jobs:
            kernel(*args)
            return
        step = pl.program_id(0)
        sets, lands = [], []
        for job, (pi, po, ps) in zip(jobs, places):
            mine = refs[pi : pi + len(job.ins)] + refs[i + po : i + po + len(job.outs)]
            mine += refs[o + ps : o + ps + len(job.scratch)]
            sems = refs[o + ps + len(job.scratch) : o + ps + len(job.scratch) + 2]
            sets.append((job, mine, sems))
            if getattr(job, "inner", False):
                lands.append(mine[-1])
        moments = sorted({when for job in jobs for when in job.events})

        def run(moment):
            for job, mine, sems in sets:
                for event in job.events.get(moment, ()):
                    event(mine, sems, args)

        @pl.when(step == 0)
        def _():
            greet([p for job in jobs for p in job.peers])

        for moment in moments:
            if moment[1] == 0:
                pl.when(step == moment[0])(partial(run, moment))
        kernel(*args, *lands)
        for moment in moments:
            if moment[1] == 1:
                pl.when(step == moment[0])(partial(run, moment))

    arrays = [a for a, _ in ins]
    moved = sum(a.size * a.dtype.itemsize for a in arrays) + sum(t.size * t.dtype.itemsize for t, _ in outs)
    got = pl.pallas_call(
        body_,
        grid=grid,
        in_specs=[t for _, t in ins],
        out_specs=[t for _, t in outs],
        out_shape=[t for t, _ in outs],
        scratch_shapes=scratch,
        compiler_params=pltpu.CompilerParams(
            vmem_limit_bytes=VMEM_LIMIT,
            dimension_semantics=("arbitrary",) * len(grid),
            **(dict(collective_id=tag, has_side_effects=True) if jobs else {}),
        ),
        cost_estimate=pl.CostEstimate(flops=int(flops), bytes_accessed=int(moved), transcendentals=0),
        name=name,
    )(*arrays)
    results = [got[po : po + len(job.outs)] for job, (_, po, _) in zip(jobs, places)]
    return (got[:n_out], results) if jobs else got


def whole(array):
    return (array, pl.BlockSpec(array.shape, lambda i: (0,) * array.ndim))


def per_video(array, n):
    return (array, pl.BlockSpec((None,) + array.shape[1:], lambda i: (i // n, 0, 0)))


def video_rows(array, n, tile, cols=None, at=0):
    return (array, pl.BlockSpec((None, tile, cols or array.shape[2]), lambda i: (i // n, i % n, at)))


def video_cols(array, n, tile, at=0):
    return (array, pl.BlockSpec((None, array.shape[1], tile), lambda i: (i // n, 0, i % n + at)))


def turn_cols(array, n, tile, at=0):
    return (array, pl.BlockSpec((array.shape[0], tile), lambda i: (0, i % n + at)))


def turn_rows(array, n, tile):
    return (array, pl.BlockSpec((tile, array.shape[1]), lambda i: (i % n, 0)))


def rows_tiled(array, tile=TILE):
    return (array, pl.BlockSpec((tile, array.shape[1]), lambda i: (i, 0)))


def cols_tiled(array, tile, first=0):
    return (array, pl.BlockSpec((array.shape[0], tile), lambda i: (0, i + first)))


def shape_of(shape, dtype):
    return jax.ShapeDtypeStruct(shape, dtype)


def pad_kernel(wa, pa, wc, pc, wa_out, pa_out, wc_out, pc_out):
    for src, dst in ((wa, wa_out), (wc, wc_out)):
        blank = jnp.zeros((src.shape[0], LANE - HD), bf16)
        for j in range(src.shape[1] // HD):
            dst[:, LANE * j : LANE * (j + 1)] = jnp.concatenate([src[:, HD * j : HD * (j + 1)], blank], axis=1)
    for src, dst in ((pa, pa_out), (pc, pc_out)):
        blank = jnp.zeros((LANE - HD, src.shape[1]), bf16)
        for j in range(src.shape[0] // HD):
            dst[LANE * j : LANE * j + HD, :] = src[HD * j : HD * (j + 1), :]
            dst[LANE * j + HD : LANE * (j + 1), :] = blank


def source_of(rows_shape, start):
    r = rows_of(rows_shape)
    s = r // 56
    p = r - s * 56 + start
    f = p // CELL
    rest = p - f * CELL
    r2 = rest // 7
    c2 = rest - r2 * 7
    a = s // 2
    return f * (HT * WD) + r2 * (2 * WD) + a * WD + c2 * 2 + (s - 2 * a)


def first_kernel(x, gain, xn, kv, mem, xs):
    for i in range(7):
        lo = 196 * i // 16 * 16
        hi = min(QT, (196 * i + 392 + 15) // 16 * 16)
        shape = (PIECE, hi - lo)
        pick = jnp.where(source_of(shape, 56 * i) == lanes(shape) + lo, 1.0, 0.0).astype(bf16)
        out = mm(pick, x[0, 0, 0, lo:hi, :])
        for s in range(4):
            xs[PT * s + 56 * i : PT * s + 56 * (i + 1), :] = out[56 * s : 56 * (s + 1)]
    for i in range(PIECES):
        at = slice(PIECE * i, PIECE * (i + 1))
        v = xs[at, :]
        unit, _ = norm_stats(v)
        n = (unit * gain[...]).astype(bf16)
        xn[at, :D1] = v.astype(bf16)
        xn[at, D1:] = n
        xs[at, :] = n.astype(f32)
    pooled = pool_rows(xs)
    kv[...] = pooled
    mem[...] = mm(tmean_matrix(), pooled).astype(bf16)


def front_kernel(x, gains, wa, pa, wc, pc, xn, kv, mem, wa_out, pa_out, wc_out, pc_out, xs, mem0):
    step = pl.program_id(0)
    first_kernel(x, gains.at[0:1, :], xn, kv, mem, xs)

    @pl.when(step == 0)
    def _():
        mem0[...] = mem[...]

    @pl.when(step == 1)
    def _():
        pad_kernel(wa, pa, wc, pc, wa_out, pa_out, wc_out, pc_out)


def front(inputs, gains, w_qkv1, w_proj1, w_qkv2, w_proj2):
    ins = [(inputs, pl.BlockSpec((1, 1, 1, QT, D1), lambda i: (0, i, 0, 0, 0))), whole(gains)]
    ins += [whole(w) for w in (w_qkv1, w_proj1, w_qkv2, w_proj2)]
    outs = [per_video(shape_of((2,) + t, bf16), 1) for t in ((QT, 2 * D1), (PR, D1), (MR, D1))]
    outs += [whole(shape_of(t, bf16)) for t in ((D1, 3 * W1), (W1, D1), (D1, 3 * W2), (W2, D2))]
    jobs = [Shift(14, 1, (0, 1), (1, 1)), Shift(14, 2, (0, 1), (1, 1))]
    return call(
        front_kernel, (2,), ins, outs, [VMEM((QT, D1), f32), VMEM((MR, D1), bf16)],
        flops=4 * QT * 416 * D1, name="first_norm", jobs=jobs, tag=1,
    )


def keys_ext(kall, wk, wv, kext, heads, k_out, v_out):
    k = mm(kall, wk)
    v = mm(kall, wv)
    lane = lanes((KR, LANE))
    ones = jnp.where((lane >= HD) & (lane < HD + 3), 1.0, 0.0)
    for h in range(heads):
        at = slice(LANE * h, LANE * (h + 1))
        k_out[:, at] = (k[:, at] + kext).astype(bf16)
        v_out[:, at] = (v[:, at] + ones).astype(bf16)


def head_forward(q, s, v):
    top = jnp.max(s, axis=-1, keepdims=True)
    e = jnp.exp2((s - top) * RATE).astype(bf16)
    mixed = mm(e, v)
    total = mixed[:, HD : HD + 1]
    lse = top + jnp.log(total) * (1.0 / SCALE)
    return (mixed * (1.0 / total), put3(q.astype(f32), -lse).astype(bf16))


def one_lane(shape):
    return jnp.where(lanes(shape) % LANE == HD + 3, 1.0, 0.0)


def remember(kall, step, near0, far0, near1, far1):
    @pl.when(step == 0)
    def _():
        kall[PR : PR + MR, :] = near0[...]
        kall[PR + MR : KR, :] = far0[...]

    @pl.when(step > 0)
    def _():
        kall[PR : PR + MR, :] = near1[...]
        kall[PR + MR : KR, :] = far1[...]


def block1_kernel(
    kv, near0, far0, kext, xn, wq, wk, wv, wp, gains, wfc, wout,
    kall, k_out, v_out, ozq, hm, ubgp, pc, mem, xs, mem0, near1, far1,
):
    step = pl.program_id(0)
    video, turn = step // STEPS, step % STEPS

    @pl.when(turn == 0)
    def _():
        kall[0:PR, :] = kv[...]
        remember(kall, step, near0, far0, near1, far1)
        keys_ext(kall[...], wk[...], wv[...], kext[...], H1, k_out, v_out)

    q = (mm(xn[:, D1:], wq[...]) + one_lane((TILE, W1))).astype(bf16)
    heads = [slice(LANE * h, LANE * (h + 1)) for h in range(H1)]
    scores = [mm_nt(q[:, at], k_out[:, at]) for at in heads]
    for h, at in enumerate(heads):
        o, qx = head_forward(q[:, at], scores[h], v_out[:, at])
        ozq[:, 2 * W1 + LANE * h : 2 * W1 + LANE * (h + 1)] = qx
        ozq[:, at] = o.astype(bf16)
        ozq[:, W1 + LANE * h : W1 + LANE * (h + 1)] = (o + q[:, at].astype(f32)).astype(bf16)
    ha = xn[:, :D1].astype(f32) + mm(ozq[:, W1 : 2 * W1], wp[...])
    hm[:, :D1] = ha
    unit, _ = norm_stats(ha)
    nb = (unit * gains[1:2, :]).astype(bf16)
    part = F1 // 3
    mid = ha
    ahead = mm(nb, wfc[:, :part])
    for j in range(3):
        at = slice(part * j, part * (j + 1))
        inner = ahead
        if j < 2:
            ahead = mm(nb, wfc[:, part * (j + 1) : part * (j + 2)])
        act, slope = gelu_both(inner)
        act = act.astype(bf16)
        ubgp[:, at] = act
        ubgp[:, F1 + part * j : F1 + part * (j + 1)] = slope.astype(bf16)
        mid = mid + mm(act, wout[at, :])
    hm[:, D1:] = mid
    unit, _ = norm_stats(mid)
    xs[pl.ds(pl.multiple_of(turn * TILE, TILE), TILE), :] = (unit * gains[2:3, :]).astype(bf16).astype(f32)

    @pl.when(turn == STEPS - 1)
    def _():
        pooled = pool_rows(xs)
        pc[...] = pooled
        m = mm(tmean_matrix(), pooled).astype(bf16)
        mem[...] = m

        @pl.when(video == 0)
        def _():
            mem0[...] = m


def block1(kv, got0, mem1, kext, xn, w, wp, gains, wfc, wout):
    n = STEPS
    ins = [per_video(kv, n), whole(got0[0]), whole(got0[1]), whole(kext), video_rows(xn, n, TILE)]
    ins += [cols_fixed(w, W1, j) for j in range(3)]
    ins += [whole(wp), whole(gains), whole(wfc), whole(wout)]
    outs = [per_video(shape_of((2, KR, c), bf16), n) for c in (D1, W1, W1)]
    outs += [video_rows(shape_of((2, QT, c), t), n, TILE) for c, t in ((3 * W1, bf16), (2 * D1, f32), (2 * F1, bf16))]
    outs += [per_video(shape_of((2, r, D1), bf16), n) for r in (PR, MR)]
    flops = 4 * QT * (D1 * W1 * 2 + 2 * D1 * F1 + 4 * KR * W1)
    jobs = [Shift(mem1, k, (0, 0), (n, 0), True) for k in (1, 2)]
    jobs += [Shift(21, k, (n - 1, 1), (2 * n - 1, 1)) for k in (1, 2)]
    scratch = [VMEM((QT, D1), f32), VMEM((MR, D1), bf16)]
    return call(block1_kernel, (2 * n,), ins, outs, scratch, flops=flops, name="block1_forward", jobs=jobs, tag=2)


def cols_fixed(array, tile, at):
    return (array, pl.BlockSpec((array.shape[0], tile), lambda i: (0, at)))


PAIR = 2 * LANE


def block2_kernel(pc, near0, far0, kext, wq, wk, wv, wskip, wp, kall, k_out, v_out, qe, o_out, zc, hc, near1, far1):
    step = pl.program_id(0)

    @pl.when(step % (H2 // 2) == 0)
    def _():
        kall[0:PR, :] = pc[...]
        remember(kall, step, near0, far0, near1, far1)
        hc[...] = mm(pc[...], wskip[...])

    keys_ext(kall[...], wk[...], wv[...], kext[...], 2, k_out, v_out)
    q = (mm(pc[...], wq[...]) + one_lane((PR, PAIR))).astype(bf16)
    heads = [slice(LANE * h, LANE * (h + 1)) for h in range(2)]
    scores = [mm_nt(q[:, at], k_out[:, at]) for at in heads]
    for h, at in enumerate(heads):
        o, qx = head_forward(q[:, at], scores[h], v_out[:, at])
        qe[:, at] = qx
        o_out[:, at] = o.astype(bf16)
        zc[:, at] = (o + q[:, at].astype(f32)).astype(bf16)
    hc[...] += mm(zc[...], wp[...])


def block2(pc, got0, mem1, kext, w, wskip, wp):
    n = H2 // 2
    ins = [per_video(pc, n), whole(got0[0]), whole(got0[1]), whole(kext)]
    ins += [turn_cols(w, n, PAIR, j * n) for j in range(3)]
    ins += [whole(wskip), turn_rows(wp, n, PAIR)]
    outs = [per_video(shape_of((2, KR, D1), bf16), n)]
    outs += [video_cols(shape_of((2, r, W2), bf16), n, PAIR) for r in (KR, KR, PR, PR, PR)]
    outs += [per_video(shape_of((2, PR, D2), f32), n)]
    flops = 4 * (PR * D1 * (W2 + D2) + 2 * KR * D1 * W2 + PR * W2 * D2 + 4 * PR * KR * W2)
    jobs = [Shift(mem1, k, (0, 0), (n, 0), True) for k in (1, 2)]
    return call(block2_kernel, (2 * n,), ins, outs, flops=flops, name="block2_attention", jobs=jobs, tag=3)


PART = 768


def pick_share(micro, even, odd):
    first_ = micro == 0
    return (jnp.where(first_, even, odd).astype(bf16), jnp.where(first_, odd, even).astype(bf16))


def mlp2_kernel(micro, hc, cot, gain, wfc, wout, out, gh, keep_fc, send_fc, keep_out, send_out, gg, hs, nd, ndt, gm, acc, dn):
    step = pl.program_id(0)

    @pl.when(step == 0)
    def _():
        blank = jnp.zeros((PR - PT, D2), f32)
        for b in range(2):
            at = slice(PR * b, PR * (b + 1))
            v = hc[b]
            hs[at, :] = v
            unit, _ = norm_stats(v)
            nd[at, :] = (unit * gain[...]).astype(bf16)
            g = cot[0, b, 0].astype(f32)
            gm[at, :] = jnp.concatenate([g, blank], axis=0).astype(bf16)
        ndt[...] = nd[...].T

    act, slope = gelu_both(mm(nd[...], wfc[...]))
    act = act.astype(bf16)
    gi = (slope * mm_nt(gm[...], wout[...])).astype(bf16)
    m = micro[0]
    gw = mm_tn(act, gm[...])
    rows = keep_fc.shape[1]
    for i in range(keep_out.shape[0]):
        keep, send = pick_share(m, gw[8 * rows * i : 8 * rows * i + 4 * rows], gw[8 * rows * i + 4 * rows : 8 * rows * (i + 1)])
        for a in range(4):
            keep_out[i, :, D2 * a : D2 * (a + 1)] = keep[rows * a : rows * (a + 1)]
            send_out[i, :, D2 * a : D2 * (a + 1)] = send[rows * a : rows * (a + 1)]
    gw = mm(ndt[...], gi)
    for i in range(keep_fc.shape[0]):
        keep, send = pick_share(m, gw[2 * rows * i : 2 * rows * i + rows], gw[2 * rows * i + rows : 2 * rows * (i + 1)])
        keep_fc[i] = keep
        send_fc[i] = send
    o = mm(act, wout[...])
    d = mm_nt(gi, wfc[...])

    @pl.when(step == 0)
    def _():
        acc[...] = o
        dn[...] = d

    @pl.when(step > 0)
    def _():
        acc[...] += o
        dn[...] += d

    @pl.when(step == F2 // PART - 1)
    def _():
        v = hs[...]
        y = v + acc[...]
        unit, inv = norm_stats(v)
        dx, dg = norm_back(dn[...], unit, inv, gain[...])
        gg[...] = dg
        g = (gm[...].astype(f32) + dx).astype(bf16)
        for b in range(2):
            out[0, b, 0] = y[PR * b : PR * b + PT].astype(bf16)
            gh[b] = g[PR * b : PR * (b + 1)]


def scalar(value):
    return (value.astype(jnp.int32).reshape(1), pl.BlockSpec(memory_space=pltpu.SMEM))


def mlp2(micro, clips, hc, cot, gain, wfc, wout):
    rows = D2 // (2 * clips)
    steps = F2 // PART
    ins = [scalar(micro), whole(hc), whole(cot), whole(gain), cols_tiled(wfc, PART), rows_tiled(wout, PART)]
    share = shape_of((clips, rows, F2), bf16)
    fc_spec = (share, pl.BlockSpec((clips, rows, PART), lambda i: (0, 0, i)))
    out_spec = (share, pl.BlockSpec((clips // steps, rows, F2), lambda i: (i, 0, 0)))
    outs = [
        whole(shape_of(cot.shape, bf16)),
        whole(shape_of((2, PR, D2), bf16)),
        fc_spec,
        fc_spec,
        out_spec,
        out_spec,
        whole(shape_of((1, D2), f32)),
    ]
    n = 2 * PR
    scratch = [
        VMEM((n, D2), f32),
        VMEM((n, D2), bf16),
        VMEM((D2, n), bf16),
        VMEM((n, D2), bf16),
        VMEM((n, D2), f32),
        VMEM((n, D2), f32),
    ]
    return call(mlp2_kernel, (steps,), ins, outs, scratch, flops=12 * n * D2 * F2, name="block2_mlp")


def head_backward(q, g, k, v, tiles):
    kt = k.T
    dk = jnp.zeros((KR, LANE), f32)
    dv = jnp.zeros((KR, LANE), f32)
    dqs = []
    for at in tiles:
        p = jnp.exp2(mm_nt(k, q[at]) * RATE)
        ds = (p * mm_nt(v, g[at])).astype(bf16)
        dv = dv + mm(p.astype(bf16), g[at])
        dk = dk + mm(ds, q[at])
        dqs.append((mm(kt, ds) * SCALE).T)
    return (dqs, dk * SCALE, dv)


def grad_ext(gz, o):
    delta = jnp.sum(jnp.where(lanes(gz.shape) < HD, gz.astype(f32) * o.astype(f32), 0.0), axis=-1, keepdims=True)
    return put3(gz.astype(f32), -delta).astype(bf16)


def add_columns(ref, step, value, again):
    at = pl.ds(pl.multiple_of(step * PAIR, PAIR), PAIR)

    @pl.when(again)
    def _():
        ref[:, at] += value

    @pl.when(jnp.logical_not(again))
    def _():
        ref[:, at] = value


def att2_back_kernel(
    micro, gh, wp, qe, o, k, v, zc, pc, kall, wskip, wq, wk, wv,
    dnear, dfar, dpc, keep_a, send_a, keep_b, send_b,
    gq_w, gk_w, gv_w, gp_w, gs_w, dkv, qkv, dnear0, dfar0,
):
    step = pl.program_id(0)
    turn = step % (H2 // 2)
    again = step >= H2 // 2

    @pl.when(turn == 0)
    def _():
        dpc[...] = mm_nt(gh[...], wskip[...])
        skip = mm_tn(pc[...], gh[...])
        gs_w[...] = jnp.where(again, gs_w[...], 0.0) + skip
        dkv[...] = jnp.zeros_like(dkv)

    gz = mm_nt(gh[...], wp[...]).astype(bf16)
    gp = mm_tn(zc[...], gh[...])
    at_rows = pl.ds(pl.multiple_of(turn * PAIR, PAIR), PAIR)

    @pl.when(again)
    def _():
        gp_w[at_rows, :] += gp

    @pl.when(jnp.logical_not(again))
    def _():
        gp_w[at_rows, :] = gp

    heads = [slice(LANE * h, LANE * (h + 1)) for h in range(2)]
    gq, dk, dv = [], [], []
    for at in heads:
        g = grad_ext(gz[:, at], o[:, at])
        dqs, dkh, dvh = head_backward(qe[:, at], g, k[:, at], v[:, at], [slice(0, PR)])
        gq.append((gz[:, at].astype(f32) + dqs[0]).astype(bf16))
        dk.append(dkh.astype(bf16))
        dv.append(dvh.astype(bf16))
    gq = jnp.concatenate(gq, axis=1)
    dk = jnp.concatenate(dk, axis=1)
    dv = jnp.concatenate(dv, axis=1)
    dpc[...] += mm_nt(gq, wq[...])
    dkv[...] += mm_nt(dk, wk[...]) + mm_nt(dv, wv[...])
    add_columns(gq_w, turn, mm_tn(pc[...], gq), again)
    add_columns(gk_w, turn, mm_tn(kall[...], dk), again)
    add_columns(gv_w, turn, mm_tn(kall[...], dv), again)

    @pl.when(turn == H2 // 2 - 1)
    def _():
        dpc[...] += dkv[0:PR, :]

    @pl.when(step == H2 // 2 - 1)
    def _():
        dnear0[...] = dkv[PR : PR + MR, :].astype(bf16)
        dfar0[...] = dkv[PR + MR : KR, :].astype(bf16)

    @pl.when(step == H2 - 1)
    def _():
        dnear[...] = dkv[PR : PR + MR, :].astype(bf16)
        dfar[...] = dkv[PR + MR : KR, :].astype(bf16)
        pack2(micro, gq_w, gk_w, gv_w, gp_w, gs_w, keep_a, send_a, keep_b, send_b, qkv)


def att2_back(gh, wp, qe, o, k, v, zc, pc, kall, wskip, w, micro, clips, jobs):
    n = H2 // 2
    ins = [scalar(micro), per_video(gh, n), turn_rows(wp, n, PAIR)]
    ins += [video_cols(a, n, PAIR) for a in (qe, o, k, v, zc)]
    ins += [per_video(pc, n), per_video(kall, n), whole(wskip)]
    ins += [turn_cols(w, n, PAIR, j * n) for j in range(3)]
    outs = [whole(shape_of((MR, D1), bf16))] * 2 + [per_video(shape_of((2, PR, D1), f32), n)]
    outs += [whole(shape_of((clips,) + folded(D1 // (2 * clips), 3 * D2), bf16))] * 4
    scratch = [VMEM((D1, W2), f32)] * 3 + [VMEM((W2, D2), f32), VMEM((D1, D2), f32)]
    scratch += [VMEM((KR, D1), f32), VMEM((D1, 3 * D2), f32)] + [VMEM((MR, D1), bf16)] * 2
    flops = 4 * (10 * PR * KR * W2 + 4 * PR * D1 * W2 + 4 * KR * D1 * W2 + 4 * PR * W2 * D2)
    jobs = [Shift(28, -1, (n - 1, 1), (2 * n - 1, 1)), Shift(29, -2, (n - 1, 1), (2 * n - 1, 1))] + jobs
    return call(att2_back_kernel, (2 * n,), ins, outs, scratch, flops=flops, name="block2_attention_back", jobs=jobs, tag=4)


def mlp1_back_kernel(
    micro, dpc, rn0, rf0, gains, hm, ubgp, oz, wout, wfc, wp,
    gha, gze, gg_c, gg_m, gw_p, keep_a, send_a, keep_b, send_b,
    gw_out, gw_fc, ds, flip, rn1, rf1,
):
    step = pl.program_id(0)
    turn = step % PIECES

    @pl.when(step == 0)
    def _():
        for ref in (gg_c, gg_m, gw_out, gw_fc, gw_p):
            ref[...] = jnp.zeros_like(ref)

    def spread(rn, rf):
        got = add_up(rn[...], rf[...]).astype(bf16)
        d = 0.25 * (dpc[...] + mm_tn(tmean_matrix(), got))
        for s in range(4):
            ds[PT * s : PT * (s + 1), :] = d[0:PT]

    pl.when(step == 0)(lambda: spread(rn0, rf0))
    pl.when(step == PIECES)(lambda: spread(rn1, rf1))

    unit, inv = norm_stats(hm[:, D1:])
    dnc = ds[pl.ds(pl.multiple_of(turn * PIECE, PIECE), PIECE), :]
    gmid, dg = norm_back(dnc, unit, inv, gains[2:3, :])
    gg_c[...] += dg
    gm = gmid.astype(bf16)
    gmt = gm.T
    unit_b, inv_b = norm_stats(hm[:, :D1])
    nbt = (unit_b * gains[1:2, :]).astype(bf16).T
    part = F1 // 3
    dn = jnp.zeros((PIECE, D1), f32)
    ahead = mm_nt(gm, wout[:part, :])
    for j in range(3):
        at = slice(part * j, part * (j + 1))
        inner = ahead
        if j < 2:
            ahead = mm_nt(gm, wout[part * (j + 1) : part * (j + 2), :])
        slope = ubgp[:, F1 + part * j : F1 + part * (j + 1)].astype(f32)
        gi = (slope * inner).astype(bf16)
        gw_out[:, at] += mm(gmt, ubgp[:, at])
        gw_fc[:, at] += mm(nbt, gi)
        dn = dn + mm_nt(gi, wfc[:, at])
    dx, dg = norm_back(dn, unit_b, inv_b, gains[1:2, :])
    gg_m[...] += dg
    g = gmid + dx
    gha[...] = g
    gh = g.astype(bf16)
    gw_p[...] += mm_tn(oz[:, W1:], gh)
    gz = mm_nt(gh, wp[...]).astype(bf16)
    for h in range(H1):
        at = slice(LANE * h, LANE * (h + 1))
        gze[:, at] = grad_ext(gz[:, at], oz[:, at])

    @pl.when(step == 2 * PIECES - 1)
    def _():
        pack_mlp1(micro, gw_fc, gw_out, keep_a, send_a, keep_b, send_b, flip)


def mlp1_back(dpc, got0, near1, far1, gains, hm, ubgp, ozq, wout, wfc, wp, micro, clips, jobs):
    n = PIECES
    ins = [scalar(micro), per_video(dpc, n), whole(got0[0]), whole(got0[1]), whole(gains)]
    ins += [video_rows(hm, n, PIECE), video_rows(ubgp, n, PIECE), video_rows(ozq, n, PIECE, 2 * W1)]
    ins += [whole(wout), whole(wfc), whole(wp)]
    outs = [video_rows(shape_of((2, QT, D1), f32), n, PIECE), video_rows(shape_of((2, QT, W1), bf16), n, PIECE)]
    outs += [whole(shape_of((1, D1), f32))] * 2 + [whole(shape_of((W1, D1), f32))]
    outs += [whole(shape_of((clips,) + folded(D1 // (2 * clips), F1), bf16))] * 4
    scratch = [VMEM((D1, F1), f32)] * 2 + [VMEM((QT, D1), f32), VMEM((F1, D1), f32)]
    flops = 4 * QT * (4 * D1 * F1 + 2 * D1 * W1)
    jobs = [Shift(near1, -1, (0, 0), (n, 0), True), Shift(far1, -2, (0, 0), (n, 0), True)] + jobs
    return call(mlp1_back_kernel, (2 * n,), ins, outs, scratch, flops=flops, name="block1_mlp_back", jobs=jobs, tag=5)


QUERY_TILES = [slice(0, 512), slice(512, 1024), slice(1024, QT)]


def att1_back_kernel(
    micro, qe, gze, k, v, xn, kall, wq, wk, wv, gp,
    dnear, dfar, down, dna, keep_a, send_a, keep_b, send_b,
    gq_w, gk_w, gv_w, dkv, nat, qkv, dnear0, dfar0,
):
    step = pl.program_id(0)
    turn = step % (H1 // 2)
    again = step >= H1 // 2

    @pl.when(turn == 0)
    def _():
        dkv[...] = jnp.zeros_like(dkv)
        dna[...] = jnp.zeros_like(dna)
        nat[...] = xn[...].T

    gq, dk, dv = [[] for _ in QUERY_TILES], [], []
    for h in range(2):
        at = slice(LANE * h, LANE * (h + 1))
        g = gze[:, at]
        dqs, dkh, dvh = head_backward(qe[:, at], g, k[:, at], v[:, at], QUERY_TILES)
        for i, rows in enumerate(QUERY_TILES):
            gq[i].append((g[rows].astype(f32) + dqs[i]).astype(bf16))
        dk.append(dkh.astype(bf16))
        dv.append(dvh.astype(bf16))
    gq = jnp.concatenate([jnp.concatenate(t, axis=1) for t in gq], axis=0)
    lane = lanes((1, PAIR)) % LANE
    gq = jnp.where(lane < HD, gq, jnp.zeros_like(gq))
    dk = jnp.concatenate(dk, axis=1)
    dv = jnp.concatenate(dv, axis=1)
    dna[...] += mm_nt(gq, wq[...])
    dkv[...] += mm_nt(dk, wk[...]) + mm_nt(dv, wv[...])
    add_columns(gq_w, turn, mm(nat[...], gq), again)
    add_columns(gk_w, turn, mm_tn(kall[...], dk), again)
    add_columns(gv_w, turn, mm_tn(kall[...], dv), again)

    @pl.when(turn == H1 // 2 - 1)
    def _():
        down[...] = dkv[0:PR, :]

    @pl.when(step == H1 // 2 - 1)
    def _():
        dnear0[...] = dkv[PR : PR + MR, :].astype(bf16)
        dfar0[...] = dkv[PR + MR : KR, :].astype(bf16)

    @pl.when(step == H1 - 1)
    def _():
        dnear[...] = dkv[PR : PR + MR, :].astype(bf16)
        dfar[...] = dkv[PR + MR : KR, :].astype(bf16)
        pack_att1(micro, gq_w, gk_w, gv_w, gp, keep_a, send_a, keep_b, send_b, qkv)


def att1_back(ozq, gze, k, v, xn, kall, w, gp, micro, clips, jobs):
    n = H1 // 2
    ins = [scalar(micro), video_cols(ozq, n, PAIR, 2 * n)] + [video_cols(a, n, PAIR) for a in (gze, k, v)]
    ins += [(xn, pl.BlockSpec((None, QT, D1), lambda i: (i // n, 0, 1))), per_video(kall, n)]
    ins += [turn_cols(w, n, PAIR, j * n) for j in range(3)] + [whole(gp)]
    outs = [whole(shape_of((MR, D1), bf16))] * 2
    outs += [per_video(shape_of((2, PR, D1), f32), n), per_video(shape_of((2, QT, D1), f32), n)]
    outs += [whole(shape_of((clips,) + folded(D1 // (2 * clips), 2 * D1), bf16))] * 4
    scratch = [VMEM((D1, W1), f32)] * 3
    scratch += [VMEM((KR, D1), f32), VMEM((D1, QT), bf16), VMEM((D1, 4 * D1), f32)] + [VMEM((MR, D1), bf16)] * 2
    flops = 4 * (10 * QT * KR * W1 + 2 * QT * D1 * W1 + 4 * KR * D1 * W1)
    jobs = [Shift(25, -1, (n - 1, 1), (2 * n - 1, 1)), Shift(26, -2, (n - 1, 1), (2 * n - 1, 1))] + jobs
    return call(att1_back_kernel, (2 * n,), ins, outs, scratch, flops=flops, name="block1_attention_back", jobs=jobs, tag=6)


def strip(grad):
    return jnp.concatenate([grad[:, LANE * h : LANE * h + HD] for h in range(grad.shape[1] // LANE)], axis=1)


def fold(v):
    rows, cols = v.shape
    if rows != 24:
        return v
    rest = jnp.concatenate([v[16:, : cols // 2], v[16:, cols // 2 :]], axis=0)
    return jnp.concatenate([v[:16], rest], axis=1)


def unfold(v, rows):
    if rows != 24:
        return v
    cols = v.shape[1] * 2 // 3
    rest = jnp.concatenate([v[:8, cols:], v[8:, cols:]], axis=1)
    return jnp.concatenate([v[:, :cols], rest], axis=0)


def folded(rows, cols):
    return (16, cols * 3 // 2) if rows == 24 else (rows, cols)


def store_shares(micro, clips, pieces):
    for i in range(clips):
        for keep, send, piece in pieces:
            k, t = pick_share(micro, fold(piece(2 * i)), fold(piece(2 * i + 1)))
            keep[i] = k
            send[i] = t


def pack2(micro, gq, gk, gv, gp, gs, keep_a, send_a, keep_b, send_b, qkv):
    for j, g in enumerate((gq, gk, gv)):
        qkv[:, D2 * j : D2 * (j + 1)] = strip(g[...])
    clips, rows = keep_a.shape[0], D1 // (2 * keep_a.shape[0])

    def proj(share, a):
        lo = rows * (2 * share + a)
        h = lo // HD
        start = lo + (LANE - HD) * h
        if (lo + rows - 1) // HD == h:
            return gp[start : start + rows, :]
        cut = HD * (h + 1) - lo
        return jnp.concatenate([gp[start : start + cut, :], gp[LANE * (h + 1) : LANE * (h + 1) + rows - cut, :]], axis=0)

    def piece_a(n):
        return qkv[rows * n : rows * (n + 1), :]

    def piece_b(n):
        return jnp.concatenate([proj(n, 0), proj(n, 1), gs[rows * n : rows * (n + 1), :]], axis=1)

    store_shares(micro[0], clips, ((keep_a, send_a, piece_a), (keep_b, send_b, piece_b)))


def pack_mlp1(micro, gfc, gout, keep_a, send_a, keep_b, send_b, flip):
    flip[...] = gout[...].T
    clips, rows = keep_a.shape[0], D1 // (2 * keep_a.shape[0])

    def piece_a(n):
        return gfc[rows * n : rows * (n + 1), :]

    def piece_b(n):
        return jnp.concatenate([flip[rows * (4 * n + a) : rows * (4 * n + a + 1), :] for a in range(4)], axis=1)

    store_shares(micro[0], clips, ((keep_a, send_a, piece_a), (keep_b, send_b, piece_b)))


def pack_att1(micro, gq, gk, gv, gp, keep_a, send_a, keep_b, send_b, qkv):
    for j, g in enumerate((gq, gk, gv)):
        qkv[:, D1 * j : D1 * (j + 1)] = strip(g[...])
    for h in range(H1):
        qkv[HD * h : HD * (h + 1), 3 * D1 :] = gp[LANE * h : LANE * h + HD, :]
    clips, rows = keep_a.shape[0], D1 // (2 * keep_a.shape[0])
    half = 2 * D1

    def piece_a(n):
        return qkv[rows * n : rows * (n + 1), :half]

    def piece_b(n):
        return qkv[rows * n : rows * (n + 1), half:]

    store_shares(micro[0], clips, ((keep_a, send_a, piece_a), (keep_b, send_b, piece_b)))


def stack_blocks(v, count):
    return jnp.concatenate(jnp.split(v, count, axis=1), axis=0)


def bit_order(bits, stream):
    order = list(range(bits))
    if stream % 2 == 1 and bits > 1:
        order[0], order[1] = 1, 0
    return order


def finish_kernel(clips, starts, *refs):
    count = len(starts)
    keeps, gots = refs[:count], refs[count : 2 * count]
    pos = 2 * count
    gg_m, gg_c, gg_d, gain, dnear, dfar, dna, down, xn, gha, rn0, rf0 = refs[pos : pos + 12]
    pos += 12
    gx, gains = refs[pos : pos + 2]
    done = refs[pos + 2 : pos + 2 + count]
    pos += 2 + count
    ds, gs, rn1, rf1, g_all, g_four = refs[pos : pos + 6]
    pos += 6
    bits = clips.bit_length() - 1
    land, stage, ends = {}, {}, {}
    for i in range(count):
        if starts[i] < 0:
            land[i] = refs[pos]
            pos += 1
        for k in range(max(starts[i], 0), bits):
            stage[i, k] = refs[pos : pos + 3]
            pos += 3
        ends[i] = refs[pos : pos + 2]
        pos += 2
    sem_s, sem_r, gsem_s, gsem_r, fsem_s, fsem_r, msem_s, msem_r = refs[pos:]

    g, c, m = (lax.axis_index(a) for a in ("group", "clip", "micro"))
    barrier = pltpu.get_barrier_semaphore()
    others = [{"clip": lax.rem(c + d, clips)} for d in range(1, clips)]
    others += [{"micro": 1 - m}, {"group": 1 - g}, {"group": 1 - g, "micro": 1 - m}]
    for other in others:
        pl.semaphore_signal(barrier, inc=1, device_id=other, device_id_type=MESH)
    pl.semaphore_wait(barrier, len(others))

    shifts = [(dnear, rn1, -1), (dfar, rf1, -2)]

    def memory_copy(i):
        src, dst, steps = shifts[i]
        return pltpu.make_async_remote_copy(
            src_ref=src, dst_ref=dst, send_sem=msem_s.at[i], recv_sem=msem_r.at[i],
            device_id={"clip": c + steps}, device_id_type=MESH,
        )

    for i in range(2):
        pl.when(exists(shifts[i][2]))(lambda i=i: memory_copy(i).start())

    copies = {}

    def send(i, number, src, dst, other):
        n = i * (bits + 2) + number + 1
        copies[i, number] = pltpu.make_async_remote_copy(
            src_ref=src, dst_ref=dst, send_sem=sem_s.at[n], recv_sem=sem_r.at[n],
            device_id=other, device_id_type=MESH,
        )
        copies[i, number].start()

    def advance(i, number):
        if number < 0:
            send(i, number, gots[i], land[i], {"micro": 1 - m})
            return
        if (i, number - 1) in copies:
            copies[i, number - 1].wait()
        if number == starts[i]:
            keep, got = keeps[i], gots[i]
        elif number == 0:
            keep, got = keeps[i], land[i]
        else:
            keep, got = stage[i, number - 1][0], stage[i, number - 1][2]
        if number == bits:
            ends[i][0][...] = add_up(keep[0], got[0]).astype(bf16)
            send(i, number, ends[i][0], ends[i][1], {"group": 1 - g})
        else:
            order = bit_order(bits, i)
            bit = order[number]
            low = sum(1 for b in order[number + 1 :] if b < bit)
            kept, away, there = stage[i, number]
            split_shares(keep, got, kept, away, bit, low, 2 ** (bits - number - 1))
            send(i, number, away, there, {"clip": flipped(bit)})

    at_stage = list(starts)

    def advance_all():
        for i in range(count):
            if at_stage[i] <= bits:
                advance(i, at_stage[i])
                at_stage[i] += 1

    def norm_part(b, rn, rf):
        got = add_up(rn, rf).astype(bf16)
        d = 0.25 * (down[b] + mm_tn(tmean_matrix(), got))
        for s in range(4):
            ds[PT * s : PT * (s + 1), :] = d[0:PT]
        total = jnp.zeros((1, D1), f32)
        for i in range(PIECES):
            at = slice(PIECE * i, PIECE * (i + 1))
            unit, inv = norm_stats(xn[b, at, :].astype(f32))
            dx, dg = norm_back(dna[b, at, :] + ds[at, :], unit, inv, gain[0:1, :])
            total = total + dg
            gs[at, :] = gha[b, at, :] + dx
        return total

    def order_part(b):
        for i in range(PIECES):
            lo = min(CELL * i // 8 * 8, PT - 112)
            window = jnp.concatenate([gs[PT * s + lo : PT * s + lo + 112, :] for s in range(4)], axis=0).astype(bf16)
            shape = (PIECE, 4 * 112)
            t = rows_of(shape) + PIECE * i
            f = t // (HT * WD)
            rest = t - f * (HT * WD)
            r = rest // WD
            col = rest - r * WD
            r2 = r // 2
            c2 = col // 2
            s = 2 * (r - 2 * r2) + (col - 2 * c2)
            p = f * CELL + r2 * 7 + c2
            pick = jnp.where(s * 112 + p - lo == lanes(shape), 1.0, 0.0).astype(bf16)
            gx[b, PIECE * i : PIECE * (i + 1), :] = mm(pick, window).astype(bf16)

    advance_all()
    gg = norm_part(0, rn0[...], rf0[...])
    advance_all()
    order_part(0)
    advance_all()
    for i in range(2):
        _, dst, steps = shifts[i]
        pl.when(exists(steps))(lambda i=i: memory_copy(i).wait_send())

        @pl.when(exists(-steps))
        def _():
            memory_copy(i).wait_recv()

        @pl.when(jnp.logical_not(exists(-steps)))
        def _():
            dst[...] = jnp.zeros_like(dst)

    gg = gg + norm_part(1, rn1[...], rf1[...])
    advance_all()
    g_all[c] = jnp.concatenate(
        [gg, gg_m[...], gg_c[...], gg_d[:, :D1], gg_d[:, D1:], jnp.zeros((3, D1), f32)], axis=0
    )
    gcopies = []
    for d in range(1, clips):
        gcopies.append(
            pltpu.make_async_remote_copy(
                src_ref=g_all.at[c], dst_ref=g_all.at[c], send_sem=gsem_s.at[d - 1], recv_sem=gsem_r.at[d - 1],
                device_id={"clip": lax.rem(c + d, clips)}, device_id_type=MESH,
            )
        )
        gcopies[-1].start()
    order_part(1)
    advance_all()
    for copy in gcopies:
        copy.wait()
    total = g_all[0]
    for i in range(1, clips):
        total = total + g_all[i]
    place = 2 * g + m
    g_four[place] = total
    fcopies = []
    for i, other in enumerate(others[-3:]):
        fcopies.append(
            pltpu.make_async_remote_copy(
                src_ref=g_four.at[place], dst_ref=g_four.at[place], send_sem=fsem_s.at[i], recv_sem=fsem_r.at[i],
                device_id=other, device_id_type=MESH,
            )
        )
        fcopies[-1].start()
    for _ in range(bits + 2):
        advance_all()
    for copy in fcopies:
        copy.wait()
    gains[...] = (g_four[0] + g_four[1]) + (g_four[2] + g_four[3])
    for i in range(count):
        copies[i, bits].wait()
        done[i][...] = add_up(*(ref[...] for ref in ends[i]))


def finish(clips, streams, starts, gg_m, gg_c, gg_d, gain, dnear, dfar, dna, down, xn, gha, got0, tag):
    bits = clips.bit_length() - 1
    count = len(streams)
    ins = [whole(k) for k, _ in streams] + [(t, HBM) if n < 0 else whole(t) for (_, t), n in zip(streams, starts)]
    ins += [whole(a) for a in (gg_m, gg_c, gg_d, gain)] + [(dnear, HBM), (dfar, HBM)]
    ins += [whole(dna), whole(down), (xn, pl.BlockSpec((2, QT, D1), lambda i: (0, 0, 0))), whole(gha)]
    ins += [whole(a) for a in got0]
    parts = [k.shape[1:] for k, _ in streams]
    outs = [whole(shape_of((2, QT, D1), bf16)), whole(shape_of((8, D1), f32))]
    outs += [whole(shape_of(p, f32)) for p in parts]
    scratch = [VMEM((QT, D1), f32)] * 2 + [VMEM((MR, D1), bf16)] * 2
    scratch += [VMEM((clips, 8, D1), f32), VMEM((4, 8, D1), f32)]
    for p, n in zip(parts, starts):
        if n < 0:
            scratch.append(VMEM((clips,) + p, bf16))
        for k in range(max(n, 0), bits):
            scratch += [VMEM((2 ** (bits - 1 - k),) + p, bf16)] * 3
        scratch += [VMEM(p, bf16)] * 2
    dma = pltpu.SemaphoreType.DMA
    for n in (count * (bits + 2), clips - 1, 3, 2):
        scratch += [dma((n,))] * 2
    return pl.pallas_call(
        partial(finish_kernel, clips, starts),
        grid=(1,),
        in_specs=[t for _, t in ins],
        out_specs=[t for _, t in outs],
        out_shape=[t for t, _ in outs],
        scratch_shapes=scratch,
        compiler_params=pltpu.CompilerParams(
            vmem_limit_bytes=VMEM_LIMIT, collective_id=tag, has_side_effects=True
        ),
        name="finish",
    )(*[a for a, _ in ins])


def body(inputs, offsets, cotangent, gain_attn1, w_qkv1, w_proj1, gain_mlp1, w_fc1, w_out1,
         gain_attn2, w_qkv2, w_proj2, w_skip, gain_mlp2, w_fc2, w_out2):
    clip = lax.axis_index("clip")
    gains_in = jnp.stack([gain_attn1, gain_mlp1, gain_attn2])
    g_m2 = gain_mlp2.reshape(1, -1)
    row = jnp.arange(KR, dtype=jnp.int32)[:, None]
    place = jnp.where(row < PR + MR, row - PR, row - PR - MR)
    later = (place // CELL >= offsets[0]) & (place < MT)
    hops = jnp.where(row < PR + MR, 1, 2)
    valid = jnp.where(row < PR, row < PT, later & (clip >= hops))
    lane = jnp.arange(LANE, dtype=jnp.int32)[None, :]
    kext = jnp.where(lane == HD + 3, jnp.where(valid, 0.0, -1e30), jnp.where((lane >= HD) & (lane < HD + 3), 1.0, 0.0))
    kext = kext.astype(f32)

    micro, clips = lax.axis_index("micro"), lax.axis_size("clip")
    bits = clips.bit_length() - 1

    def flat(results):
        return [r[0] for r in results]

    (xn, kva, mem, w1p, p1p, w2p, p2p), got = front(inputs, gains_in, w_qkv1, w_proj1, w_qkv2, w_proj2)
    (ka, Ka, Va, ozq, hm, ubgp, pc, mem), got = block1(kva, flat(got), mem[1], kext, xn, w1p, p1p, gains_in, w_fc1, w_out1)
    (kc, Kc, Vc, qec, oc, zc, hc), _ = block2(pc, flat(got[2:]), mem[1], kext, w2p, w_skip, p2p)
    output, gh, keep_fc, send_fc, keep_out, send_out, gg_mlp2 = mlp2(micro, clips, hc, cotangent, g_m2, w_fc2, w_out2)

    orders = [bit_order(bits, i) for i in range(2)]

    def chains(parts, plan, last):
        return [Chain(p, o, plan, last) for p, o in zip(parts, orders)]

    n = H2 // 2
    jobs = chains([(keep_fc, send_fc), (keep_out, send_out)], [(-1, 0), (0, 3)], 2 * n - 1)
    (near1, far1, dpc, *packed), got = att2_back(gh, p2p, qec, oc, Kc, Vc, zc, pc, kc, w_skip, w2p, micro, clips, jobs)
    got0, big = flat(got[:2]), got[2:]
    att2 = [(packed[0], packed[1]), (packed[2], packed[3])]
    n = PIECES
    jobs = chains(big, [(1, 1), (2, 7)], 2 * n - 1) + chains(att2, [(-1, 0), (0, 4)], 2 * n - 1)
    (gha, gze, gg_c, gg_m, gp, *packed), got = mlp1_back(
        dpc, got0, near1, far1, gains_in, hm, ubgp, ozq, w_out1, w_fc1, p1p, micro, clips, jobs
    )
    big, att2 = got[2:4], got[4:]
    mlp1 = [(packed[0], packed[1]), (packed[2], packed[3])]
    n = H1 // 2
    jobs = chains(att2, [(1, 0), (2, 2)], 2 * n - 1) + chains(mlp1, [(-1, 0), (0, 1), (1, 2)], 2 * n - 1)
    (near1, far1, down, dna, *packed), got = att1_back(ozq, gze, Ka, Va, xn, ka, w1p, gp, micro, clips, jobs)
    got0, att2, mlp1 = flat(got[:2]), got[2:4], got[4:]
    att1 = [(packed[0], packed[1]), (packed[2], packed[3])]
    streams = [tuple(p) for p in att1 + mlp1 + att2 + big]
    starts = [-1, -1, 2, 2, 3, 3, 3, 3]
    gx, gains, *sums = finish(
        clips, streams, starts, gg_m, gg_c, gg_mlp2, gains_in, near1, far1, dna, down, xn, gha, got0, 7
    )
    rows = D1 // (2 * clips)
    left, right, gw_fc1, gw_out1, gw_qkv2, rest2 = (unfold(v, rows) for v in sums[:6])
    gw_fc2, gw_out2 = sums[6:]
    shares = (
        jnp.concatenate([left, right[:, :D1]], axis=1),
        right[:, D1:],
        gw_fc1,
        stack_blocks(gw_out1, 4),
        gw_qkv2,
        stack_blocks(rest2[:, : 2 * D2], 2),
        rest2[:, 2 * D2 :],
        gw_fc2,
        stack_blocks(gw_out2, 4),
    )
    gains = (gains[0], gains[1], gains[2], gains[3:5].reshape(-1))
    return (output, gx.reshape(inputs.shape)) + gains + tuple(v.reshape(-1) for v in shares)


def solution(mesh):
    tokens = P("group", "micro", "clip", None, None)
    share = P(("clip", "micro"))
    return jax.shard_map(
        body,
        mesh=mesh,
        in_specs=(tokens, P("group"), tokens) + (P(),) * 13,
        out_specs=(tokens, tokens) + (P(),) * 4 + (share,) * 9,
        check_vma=False,
    )
```

time: 484 us -> 379 us (0.78)
  starting transfers between devices: 44.1 us -> 0 us
  Pallas kernels: 374 us -> 349 us
  waiting for transfers between devices: 17.2 us -> 0 us
  local copies, waits for them, and re-layouts: 31.3 us -> 21.7 us
  other arithmetic: 7.67 us -> 1.7 us
    ppermute x24 -> x0, starting transfers between devices: 44.1 us -> none  [the longest x16 35 us: shift(): lax.ppermute(value, 'clip', [(s, s + steps) for s in range(first_, last_)])]
    pallas_call x17 -> x8, Pallas kernels: 374 us -> 349 us  [the longest x7 309 us: call(): pl.pallas_call(body_, grid=grid, in_specs=[t for _, t in ins], out_specs=...]
    ppermute x24 -> x0, waiting for transfers between devices: 17.2 us -> none  [the longest x16 16.4 us: shift(): lax.ppermute(value, 'clip', [(s, s + steps) for s in range(first_, last_)])]
    convert_element_type x5 -> x0, other arithmetic: 5.44 us -> none  [over_clip(): total = add_up(*parts).astype(bf16)]
  transfers between devices with their start and end apart: 24 -> 0, of which waited for: 6 -> 0; matrix products, arithmetic and copies ran while one was open for 2% -> 0% of each run, Pallas kernels for 51% -> 0%
where the time goes in v4:
time: 379 us; the launch traced here: 374 us
  Pallas kernels  349 us (92%)
  local copies, waits for them, and re-layouts  21.7 us (6%)
    pallas_call x7, Pallas kernels, call(): pl.pallas_call(body_, grid=grid, in_specs=[t for _, t in ins], out_specs=...  309 us
    pallas_call x1, Pallas kernels, finish(): pl.pallas_call(partial(finish_kernel, clips, starts), grid=(1,), in_specs...  39.6 us

profile of v4, /device:TPU:0, one launch (start us, length us, event | category | flops | bytes accessed | tf_op | source)
XLA Modules:
  0.0 374.0 jit_solution(13513765568412701044)
XLA Ops:
  1.3 0.7 stack.12
  2.0 0.7 stack.13
  2.7 0.7 stack.14
  3.4 0.6 pad_maximum_fusion.4.refs_1_.refs_9_.refs_4_.refs_19_
  4.0 1.3 reshape.145.refs_3_
  5.3 0.9 broadcast_select_fusion.refs_3_
  6.2 17.2 %first_norm.1 = (bf16[2,1568,768]{2,1,0:T(8,128)(2,1)}, bf16[2,400,384]{2,1,0:T(8,128)(2,1)}, bf16[2,208,384]{2,1,0:T(8,128)(2,1)}, bf16[384,1536]{1,0:T(8,128)(...) custom-call(bf16[1,2,1,1568,384]{4,3,2,1,0:T(8,128)(2,1)} %refs_0_.1, ...), custom_call_target="tpu_custom_call" | custom-call | flops 1001914368 | bytes 18117120 | tf_op jit(solution)/shard_map/first_norm/pallas_call | solution.py:345
  23.4 1.6 slice_bitcast_fusion.1.refs_12_.refs_13_
  25.0 59.5 %block1_forward.1 = (bf16[2,816,384]{2,1,0:T(8,128)(2,1)}, bf16[2,816,512]{2,1,0:T(8,128)(2,1)}, bf16[2,816,512]{2,1,0:T(8,128)(2,1)}, bf16[2,1568,1536]{2,1,0:T...) custom-call(bf16[2,400,384]{2,1,0:T(8,128)(2,1)} %get-tuple-element., ...), custom_call_target="tpu_custom_call" | custom-call | flops 20346568704 | bytes 57168384 | tf_op jit(solution)/shard_map/block1_forward/pallas_call | solution.py:345
  84.5 1.6 slice_bitcast_fusion.refs_9_.refs_10_
  86.1 26.3 %block2_attention.1 = (bf16[2,816,384]{2,1,0:T(8,128)(2,1)}, bf16[2,816,1024]{2,1,0:T(8,128)(2,1)}, bf16[2,816,1024]{2,1,0:T(8,128)(2,1)}, bf16[2,400,1024]{2,1,...) custom-call(bf16[2,400,384]{2,1,0:T(8,128)(2,1)} %get-tuple-element.113.refs_0, ...), custom_call_target="tpu_custom_call" | custom-call | flops 10273947648 | bytes 26222592 | tf_op jit(solution)/shard_map/block2_attention/pallas_call | solution.py:345
  112.4 39.8 %block2_mlp.1 = (bf16[1,2,1,392,768]{4,3,2,1,0:T(8,128)(2,1)}, bf16[2,400,768]{2,1,0:T(8,128)(2,1)}, bf16[8,48,3072]{2,1,0:T(8,128)(2,1)}, bf16[8,48,3072]{2,1,0...) custom-call(s32[1]{0:T(128)} %bitcast.refs_0_, ...), custom_call_target="tpu_custom_call" | custom-call | flops 22649241600 | bytes 24975364 | tf_op jit(solution)/shard_map/block2_mlp/pallas_call | solution.py:345
  152.2 58.1 %block2_attention_back.1 = (bf16[208,384]{1,0:T(8,128)(2,1)}, bf16[208,384]{1,0:T(8,128)(2,1)}, f32[2,400,384]{2,1,0:T(8,128)}, bf16[8,16,3456]{2,1,0:T(8,128)(2...) custom-call(s32[1]{0:T(128)} %bitcast.refs_0_, ...), custom_call_target="tpu_custom_call" | custom-call | flops 26052919296 | bytes 43499524 | tf_op jit(solution)/shard_map/block2_attention_back/pallas_call | solution.py:345
  210.2 55.4 %block1_mlp_back.1 = (f32[2,1568,384]{2,1,0:T(8,128)}, bf16[2,1568,512]{2,1,0:T(8,128)(2,1)}, f32[1,384]{1,0:T(1,128)}, f32[1,384]{1,0:T(1,128)}, f32[512,384]{1...) custom-call(s32[1]{0:T(128)} %bitcast.refs_0_, ...), custom_call_target="tpu_custom_call" | custom-call | flops 17263755264 | bytes 65543684 | tf_op jit(solution)/shard_map/block1_mlp_back/pallas_call | solution.py:345
  265.6 52.9 %block1_attention_back.1 = (bf16[208,384]{1,0:T(8,128)(2,1)}, bf16[208,384]{1,0:T(8,128)(2,1)}, f32[2,400,384]{2,1,0:T(8,128)}, f32[2,1568,384]{2,1,0:T(8,128)},...) custom-call(s32[1]{0:T(128)} %bitcast.refs_0_, ...), custom_call_target="tpu_custom_call" | custom-call | flops 31237079040 | bytes 39608324 | tf_op jit(solution)/shard_map/block1_attention_back/pallas_call | solution.py:345
  318.5 39.6 %finish.1 = (bf16[2,1568,384]{2,1,0:T(8,128)(2,1)}, f32[8,384]{1,0:T(8,128)}, f32[16,1152]{1,0:T(8,128)}, f32[16,1152]{1,0:T(8,128)}, f32[16,2304]{1,0:T(8,128)}...) custom-call(bf16[8,16,1152]{2,1,0:T(8,128)(2,1)} %get-tuple-element., ...), custom_call_target="tpu_custom_call" | custom-call | tf_op jit(solution)/shard_map/finish/pallas_call | solution.py:1256
  358.1 0.0 copy-start.5
  358.1 0.0 copy-start.4
  358.1 2.0 copy.32
  360.2 0.0 copy-start.3
  360.2 0.8 slice.89
  360.9 1.4 slice_reduce_fusion
  362.3 0.6 reshape.147
  362.9 0.8 slice.90
  363.7 0.8 fusion.23
  364.5 0.8 slice.93
  365.3 0.0 copy-start.2
  365.3 0.6 reshape.149
  366.0 0.7 reshape.148
  366.6 0.0 copy-done.5
  366.6 0.0 copy-done.4
  366.7 0.7 reshape.151
  367.4 0.7 reshape.150
  368.1 0.0 copy-done.3
  368.1 0.0 copy-start.1
  368.1 0.0 copy-done.2
  368.2 0.6 reshape.154
  368.9 0.7 reshape.152
  369.6 0.7 reshape.153
  370.2 0.0 copy-done.1
  370.2 0.0 copy-start
  370.3 0.9 reshape.156
  371.2 0.9 copy-done
  372.1 1.4 copy.35
  (22 shorter events, 0.3 us)
Async XLA Ops:
  358.1 8.5 %copy-start.5 = (f32[16,2304]{1,0:T(8,128)S(1)}, f32[16,2304]{1,0:T(8,128)}, u32[]{:S(2)}) copy-start(f32[16,2304]{1,0:T(8,128)} %get-tuple-element.191) | copy-start | bytes 442372
  358.1 8.5 %copy-start.4 = (f32[16,2304]{1,0:T(8,128)S(1)}, f32[16,2304]{1,0:T(8,128)}, u32[]{:S(2)}) copy-start(f32[16,2304]{1,0:T(8,128)} %get-tuple-element.192) | copy-start | bytes 442372
  360.2 7.9 %copy-start.3 = (f32[16,3456]{1,0:T(8,128)S(1)}, f32[16,3456]{1,0:T(8,128)}, u32[]{:S(2)}) copy-start(f32[16,3456]{1,0:T(8,128)} %get-tuple-element.193) | copy-start | bytes 663556
  365.3 2.8 copy-start.2
  368.1 2.2 copy-start.1
  370.2 1.9 copy-start

commit v5 on v4

--- a/solution.py
+++ b/solution.py
@@ -124,8 +124,8 @@
 
 
 class Shift:
-    def __init__(self, source, steps, begin, end, inner=False):
-        self.source = source
+    def __init__(self, source, steps, begin, end, inner=False, video=None):
+        self.source, self.video = source, video
         self.ins = [] if isinstance(source, int) else [(source, HBM)]
         shape = (MR, D1)
         self.outs = [] if inner else [whole(shape_of(shape, bf16))]
@@ -137,6 +137,8 @@
 
     def copy(self, refs, sems, args):
         src = args[self.source] if isinstance(self.source, int) else refs[0]
+        if self.video is not None:
+            src = src.at[self.video]
         return pltpu.make_async_remote_copy(
             src_ref=src, dst_ref=refs[-1], send_sem=sems[0].at[0], recv_sem=sems[1].at[0],
             device_id={"clip": lax.axis_index("clip") + self.steps}, device_id_type=MESH,
@@ -158,34 +160,48 @@
             refs[-2][...] = land[...]
 
 
+GROUP = 99
+
+
 class Chain:
     def __init__(self, parts, order, plan, last):
         keep, other = parts
         self.order, self.plan = order, plan
-        first_ = plan[0][0]
         tail = keep.shape[1:]
         self.ins = [(keep, HBM), (other, HBM)]
         self.scratch = [VMEM(keep.shape, bf16), VMEM(other.shape, bf16)]
         count = keep.shape[0]
         for number, _ in plan:
-            if number >= 0:
-                count //= 2
-                self.scratch += [VMEM((count,) + tail, bf16)] * 2
-                if number != plan[-1][0]:
-                    self.scratch.append(VMEM((count,) + tail, bf16))
+            if number < 0:
+                continue
+            if number == GROUP:
+                self.scratch += [VMEM((1,) + tail, bf16)] * 2
+                continue
+            count //= 2
+            self.scratch += [VMEM((count,) + tail, bf16)] * 2
+            if number != plan[-1][0]:
+                self.scratch.append(VMEM((count,) + tail, bf16))
         self.only_swap = plan[-1][0] < 0
+        self.ends = plan[-1][0] == GROUP
         final = (shape_of((count,) + tail, bf16), HBM)
         self.outs = [final] if self.only_swap else [whole(final[0]), final]
-        self.peers = [("micro", 0) if n < 0 else ("bit", order[n]) for n, _ in plan]
+        if self.ends:
+            self.outs = [whole(shape_of(tail, f32))]
+        self.peers = [self.peer(n) for n, _ in plan]
         self.sems = len(plan) + 2
         self.events = {(0, 0): [self.load]}
         for i, (_, step) in enumerate(plan):
             self.events.setdefault((step, 0), []).append(partial(self.advance, i))
         self.events.setdefault((last, 1), []).append(self.finish)
-        self.first = first_
+        self.first = plan[0][0]
+
+    def peer(self, number):
+        if number < 0:
+            return ("micro", 0)
+        return ("group", 0) if number == GROUP else ("bit", self.order[number])
 
     def slots(self, refs):
-        keep, other = refs[:2]
+        other = refs[1]
         outs = refs[2 : 2 + len(self.outs)]
         held = refs[2 + len(self.outs) :]
         pos, slots = 2, []
@@ -193,14 +209,14 @@
             final = i == len(self.plan) - 1
             if number < 0:
                 slots.append((held[0], other, outs[-1] if final else held[1]))
-                continue
-            kept, away = held[pos], held[pos + 1]
-            pos += 2
-            if final:
-                slots.append((kept, away, outs[-1]))
+            elif number == GROUP:
+                slots.append((held[pos], held[pos], held[pos + 1]))
+                pos += 2
+            elif final:
+                slots.append((held[pos], held[pos + 1], outs[-1]))
             else:
-                slots.append((kept, away, held[pos]))
-                pos += 1
+                slots.append(tuple(held[pos : pos + 3]))
+                pos += 3
         return slots
 
     def load(self, refs, sems, args):
@@ -221,7 +237,12 @@
     def copy(self, i, refs, sems):
         number = self.plan[i][0]
         _, away, land = self.slots(refs)[i]
-        to = {"micro": 1 - lax.axis_index("micro")} if number < 0 else {"clip": flipped(self.order[number])}
+        if number < 0:
+            to = {"micro": 1 - lax.axis_index("micro")}
+        elif number == GROUP:
+            to = {"group": 1 - lax.axis_index("group")}
+        else:
+            to = {"clip": flipped(self.order[number])}
         return pltpu.make_async_remote_copy(
             src_ref=away, dst_ref=land, send_sem=sems[0].at[i], recv_sem=sems[1].at[i],
             device_id=to, device_id_type=MESH,
@@ -235,22 +256,27 @@
         if number >= 0:
             if i == 0:
                 self.loaded(refs, sems, True)
-                held = refs[2 + len(self.outs) :]
-                keep, got = held[0], held[1]
+                keep, got = refs[2 + len(self.outs) :][:2]
             else:
                 if self.plan[i - 1][0] < 0:
                     self.loaded(refs, sems, False)
                 keep, got = slots[i - 1][0], slots[i - 1][2]
             kept, away, _ = slots[i]
-            bit = self.order[number]
-            low = sum(1 for b in self.order[number + 1 :] if b < bit)
-            split_shares(keep, got, kept, away, bit, low, kept.shape[0])
+            if number == GROUP:
+                kept[...] = keep[...] + got[...]
+            else:
+                bit = self.order[number]
+                low = sum(1 for b in self.order[number + 1 :] if b < bit)
+                split_shares(keep, got, kept, away, bit, low, kept.shape[0])
         self.copy(i, refs, sems).start()
 
     def finish(self, refs, sems, args):
         self.copy(len(self.plan) - 1, refs, sems).wait()
-        if not self.only_swap:
-            refs[2][...] = self.slots(refs)[-1][0][...]
+        kept, _, land = self.slots(refs)[-1]
+        if self.ends:
+            refs[2][...] = add_up(kept[0], land[0])
+        elif not self.only_swap:
+            refs[2][...] = kept[...]
 
 
 def side(bit):
@@ -290,7 +316,7 @@
 
             count = count + there.astype(jnp.int32)
         else:
-            to = {"micro": 1 - lax.axis_index("micro")} if kind == "micro" else {"clip": flipped(arg)}
+            to = {"clip": flipped(arg)} if kind == "bit" else {kind: 1 - lax.axis_index(kind)}
             pl.semaphore_signal(barrier, inc=1, device_id=to, device_id_type=MESH)
             count = count + 1
     pl.semaphore_wait(barrier, count)
@@ -443,8 +469,17 @@
     mem[...] = mm(tmean_matrix(), pooled).astype(bf16)
 
 
-def front_kernel(x, gains, wa, pa, wc, pc, xn, kv, mem, wa_out, pa_out, wc_out, pc_out, xs, mem0):
+def front_kernel(x, ga, gb, gc, gd, wa, pa, wc, pc, xn, kv, mem, gains, wa_out, pa_out, wc_out, pc_out, xs, mem0):
     step = pl.program_id(0)
+
+    @pl.when(step == 0)
+    def _():
+        gains[...] = jnp.concatenate(
+            [g[...].reshape(1, D1) for g in (ga, gb, gc)]
+            + [gd[0:D1].reshape(1, D1), gd[D1:].reshape(1, D1), jnp.zeros((3, D1), f32)],
+            axis=0,
+        )
+
     first_kernel(x, gains.at[0:1, :], xn, kv, mem, xs)
 
     @pl.when(step == 0)
@@ -457,11 +492,12 @@
 
 
 def front(inputs, gains, w_qkv1, w_proj1, w_qkv2, w_proj2):
-    ins = [(inputs, pl.BlockSpec((1, 1, 1, QT, D1), lambda i: (0, i, 0, 0, 0))), whole(gains)]
+    ins = [(inputs, pl.BlockSpec((1, 1, 1, QT, D1), lambda i: (0, i, 0, 0, 0)))] + [whole(g) for g in gains]
     ins += [whole(w) for w in (w_qkv1, w_proj1, w_qkv2, w_proj2)]
     outs = [per_video(shape_of((2,) + t, bf16), 1) for t in ((QT, 2 * D1), (PR, D1), (MR, D1))]
+    outs += [whole(shape_of((8, D1), f32))]
     outs += [whole(shape_of(t, bf16)) for t in ((D1, 3 * W1), (W1, D1), (D1, 3 * W2), (W2, D2))]
-    jobs = [Shift(14, 1, (0, 1), (1, 1)), Shift(14, 2, (0, 1), (1, 1))]
+    jobs = [Shift(18, 1, (0, 1), (1, 1)), Shift(18, 2, (0, 1), (1, 1))]
     return call(
         front_kernel, (2,), ins, outs, [VMEM((QT, D1), f32), VMEM((MR, D1), bf16)],
         flops=4 * QT * 416 * D1, name="first_norm", jobs=jobs, tag=1,
@@ -475,16 +511,16 @@
     ones = jnp.where((lane >= HD) & (lane < HD + 3), 1.0, 0.0)
     for h in range(heads):
         at = slice(LANE * h, LANE * (h + 1))
-        k_out[:, at] = (k[:, at] + kext).astype(bf16)
+        k_out[:, at] = (k[:, at] * RATE + kext).astype(bf16)
         v_out[:, at] = (v[:, at] + ones).astype(bf16)
 
 
 def head_forward(q, s, v):
     top = jnp.max(s, axis=-1, keepdims=True)
-    e = jnp.exp2((s - top) * RATE).astype(bf16)
+    e = jnp.exp2(s - top).astype(bf16)
     mixed = mm(e, v)
     total = mixed[:, HD : HD + 1]
-    lse = top + jnp.log(total) * (1.0 / SCALE)
+    lse = top + jnp.log(total) * 1.4426950408889634
     return (mixed * (1.0 / total), put3(q.astype(f32), -lse).astype(bf16))
 
 
@@ -558,7 +594,7 @@
             mem0[...] = m
 
 
-def block1(kv, got0, mem1, kext, xn, w, wp, gains, wfc, wout):
+def block1(kv, got0, mem, kext, xn, w, wp, gains, wfc, wout):
     n = STEPS
     ins = [per_video(kv, n), whole(got0[0]), whole(got0[1]), whole(kext), video_rows(xn, n, TILE)]
     ins += [cols_fixed(w, W1, j) for j in range(3)]
@@ -567,7 +603,7 @@
     outs += [video_rows(shape_of((2, QT, c), t), n, TILE) for c, t in ((3 * W1, bf16), (2 * D1, f32), (2 * F1, bf16))]
     outs += [per_video(shape_of((2, r, D1), bf16), n) for r in (PR, MR)]
     flops = 4 * QT * (D1 * W1 * 2 + 2 * D1 * F1 + 4 * KR * W1)
-    jobs = [Shift(mem1, k, (0, 0), (n, 0), True) for k in (1, 2)]
+    jobs = [Shift(mem, k, (0, 0), (n, 0), True, 1) for k in (1, 2)]
     jobs += [Shift(21, k, (n - 1, 1), (2 * n - 1, 1)) for k in (1, 2)]
     scratch = [VMEM((QT, D1), f32), VMEM((MR, D1), bf16)]
     return call(block1_kernel, (2 * n,), ins, outs, scratch, flops=flops, name="block1_forward", jobs=jobs, tag=2)
@@ -601,7 +637,7 @@
     hc[...] += mm(zc[...], wp[...])
 
 
-def block2(pc, got0, mem1, kext, w, wskip, wp):
+def block2(pc, got0, mem, kext, w, wskip, wp):
     n = H2 // 2
     ins = [per_video(pc, n), whole(got0[0]), whole(got0[1]), whole(kext)]
     ins += [turn_cols(w, n, PAIR, j * n) for j in range(3)]
@@ -610,7 +646,7 @@
     outs += [video_cols(shape_of((2, r, W2), bf16), n, PAIR) for r in (KR, KR, PR, PR, PR)]
     outs += [per_video(shape_of((2, PR, D2), f32), n)]
     flops = 4 * (PR * D1 * (W2 + D2) + 2 * KR * D1 * W2 + PR * W2 * D2 + 4 * PR * KR * W2)
-    jobs = [Shift(mem1, k, (0, 0), (n, 0), True) for k in (1, 2)]
+    jobs = [Shift(mem, k, (0, 0), (n, 0), True, 1) for k in (1, 2)]
     return call(block2_kernel, (2 * n,), ins, outs, flops=flops, name="block2_attention", jobs=jobs, tag=3)
 
 
@@ -620,6 +656,10 @@
 def pick_share(micro, even, odd):
     first_ = micro == 0
     return (jnp.where(first_, even, odd).astype(bf16), jnp.where(first_, odd, even).astype(bf16))
+
+
+def wide(gains):
+    return jnp.concatenate([gains[3:4, :], gains[4:5, :]], axis=1)
 
 
 def mlp2_kernel(micro, hc, cot, gain, wfc, wout, out, gh, keep_fc, send_fc, keep_out, send_out, gg, hs, nd, ndt, gm, acc, dn):
@@ -633,7 +673,7 @@
             v = hc[b]
             hs[at, :] = v
             unit, _ = norm_stats(v)
-            nd[at, :] = (unit * gain[...]).astype(bf16)
+            nd[at, :] = (unit * wide(gain)).astype(bf16)
             g = cot[0, b, 0].astype(f32)
             gm[at, :] = jnp.concatenate([g, blank], axis=0).astype(bf16)
         ndt[...] = nd[...].T
@@ -672,7 +712,7 @@
         v = hs[...]
         y = v + acc[...]
         unit, inv = norm_stats(v)
-        dx, dg = norm_back(dn[...], unit, inv, gain[...])
+        dx, dg = norm_back(dn[...], unit, inv, wide(gain))
         gg[...] = dg
         g = (gm[...].astype(f32) + dx).astype(bf16)
         for b in range(2):
@@ -712,18 +752,28 @@
     return call(mlp2_kernel, (steps,), ins, outs, scratch, flops=12 * n * D2 * F2, name="block2_mlp")
 
 
-def head_backward(q, g, k, v, tiles):
-    kt = k.T
-    dk = jnp.zeros((KR, LANE), f32)
-    dv = jnp.zeros((KR, LANE), f32)
-    dqs = []
-    for at in tiles:
-        p = jnp.exp2(mm_nt(k, q[at]) * RATE)
-        ds = (p * mm_nt(v, g[at])).astype(bf16)
-        dv = dv + mm(p.astype(bf16), g[at])
-        dk = dk + mm(ds, q[at])
-        dqs.append((mm(kt, ds) * SCALE).T)
-    return (dqs, dk * SCALE, dv)
+def heads_backward(heads, tiles):
+    items = [(h, at) for h in range(len(heads)) for at in tiles]
+
+    def products(item):
+        q, g, k, v = heads[item[0]]
+        return (mm_nt(k, q[item[1]]), mm_nt(v, g[item[1]]))
+
+    out = [([], [], []) for _ in heads]
+    kts = [k.T for _, _, k, _ in heads]
+    ahead = products(items[0])
+    for i, (h, at) in enumerate(items):
+        score, dp = ahead
+        if i + 1 < len(items):
+            ahead = products(items[i + 1])
+        q, g, _, _ = heads[h]
+        p = jnp.exp2(score)
+        ds = (p * dp).astype(bf16)
+        dqs, dks, dvs = out[h]
+        dvs.append(mm(p.astype(bf16), g[at]))
+        dks.append(mm(ds, q[at]))
+        dqs.append((mm(kts[h], ds) * (SCALE / RATE)).T)
+    return [(dqs, sum(dks[1:], dks[0]) * SCALE, sum(dvs[1:], dvs[0])) for dqs, dks, dvs in out]
 
 
 def grad_ext(gz, o):
@@ -731,91 +781,79 @@
     return put3(gz.astype(f32), -delta).astype(bf16)
 
 
-def add_columns(ref, step, value, again):
-    at = pl.ds(pl.multiple_of(step * PAIR, PAIR), PAIR)
-
+def put_columns(ref, turn, value):
+    ref[:, pl.ds(pl.multiple_of(turn * PAIR, PAIR), PAIR)] = value
+
+
+def add_to(ref, value, again):
     @pl.when(again)
     def _():
-        ref[:, at] += value
+        ref[...] += value
 
     @pl.when(jnp.logical_not(again))
     def _():
-        ref[:, at] = value
+        ref[...] = value
 
 
 def att2_back_kernel(
-    micro, gh, wp, qe, o, k, v, zc, pc, kall, wskip, wq, wk, wv,
+    micro, gh, wp, qe, o, k, v, zc, pc, kall, wskip, w,
     dnear, dfar, dpc, keep_a, send_a, keep_b, send_b,
-    gq_w, gk_w, gv_w, gp_w, gs_w, dkv, qkv, dnear0, dfar0,
+    gq_w, gk_w, gv_w, gp_w, gs_w, dnear0, dfar0, gqs, dks, dvs,
 ):
     step = pl.program_id(0)
     turn = step % (H2 // 2)
     again = step >= H2 // 2
-
-    @pl.when(turn == 0)
-    def _():
-        dpc[...] = mm_nt(gh[...], wskip[...])
-        skip = mm_tn(pc[...], gh[...])
-        gs_w[...] = jnp.where(again, gs_w[...], 0.0) + skip
-        dkv[...] = jnp.zeros_like(dkv)
-
     gz = mm_nt(gh[...], wp[...]).astype(bf16)
-    gp = mm_tn(zc[...], gh[...])
-    at_rows = pl.ds(pl.multiple_of(turn * PAIR, PAIR), PAIR)
-
-    @pl.when(again)
-    def _():
-        gp_w[at_rows, :] += gp
-
-    @pl.when(jnp.logical_not(again))
-    def _():
-        gp_w[at_rows, :] = gp
-
     heads = [slice(LANE * h, LANE * (h + 1)) for h in range(2)]
     gq, dk, dv = [], [], []
-    for at in heads:
-        g = grad_ext(gz[:, at], o[:, at])
-        dqs, dkh, dvh = head_backward(qe[:, at], g, k[:, at], v[:, at], [slice(0, PR)])
+    sets = [(qe[:, at], grad_ext(gz[:, at], o[:, at]), k[:, at], v[:, at]) for at in heads]
+    for at, (dqs, dkh, dvh) in zip(heads, heads_backward(sets, [slice(0, PR)])):
         gq.append((gz[:, at].astype(f32) + dqs[0]).astype(bf16))
         dk.append(dkh.astype(bf16))
         dv.append(dvh.astype(bf16))
-    gq = jnp.concatenate(gq, axis=1)
-    dk = jnp.concatenate(dk, axis=1)
-    dv = jnp.concatenate(dv, axis=1)
-    dpc[...] += mm_nt(gq, wq[...])
-    dkv[...] += mm_nt(dk, wk[...]) + mm_nt(dv, wv[...])
-    add_columns(gq_w, turn, mm_tn(pc[...], gq), again)
-    add_columns(gk_w, turn, mm_tn(kall[...], dk), again)
-    add_columns(gv_w, turn, mm_tn(kall[...], dv), again)
+    put_columns(gqs, turn, jnp.concatenate(gq, axis=1))
+    put_columns(dks, turn, jnp.concatenate(dk, axis=1))
+    put_columns(dvs, turn, jnp.concatenate(dv, axis=1))
 
     @pl.when(turn == H2 // 2 - 1)
     def _():
-        dpc[...] += dkv[0:PR, :]
-
-    @pl.when(step == H2 // 2 - 1)
-    def _():
-        dnear0[...] = dkv[PR : PR + MR, :].astype(bf16)
-        dfar0[...] = dkv[PR + MR : KR, :].astype(bf16)
-
-    @pl.when(step == H2 - 1)
-    def _():
-        dnear[...] = dkv[PR : PR + MR, :].astype(bf16)
-        dfar[...] = dkv[PR + MR : KR, :].astype(bf16)
-        pack2(micro, gq_w, gk_w, gv_w, gp_w, gs_w, keep_a, send_a, keep_b, send_b, qkv)
+        g = gh[...]
+        kallt = kall[...].T
+        pct = pc[...].T
+        add_to(gq_w, mm(pct, gqs[...]), again)
+        add_to(gk_w, mm(kallt, dks[...]), again)
+        add_to(gv_w, mm(kallt, dvs[...]), again)
+        add_to(gp_w, mm_tn(zc[...], g), again)
+        add_to(gs_w, mm(pct, g), again)
+        dkv = mm_nt(dks[...], w[:, W2 : 2 * W2]) + mm_nt(dvs[...], w[:, 2 * W2 :])
+        dpc[...] = mm_nt(g, wskip[...]) + mm_nt(gqs[...], w[:, :W2]) + dkv[0:PR]
+        near = dkv[PR : PR + MR].astype(bf16)
+        far = dkv[PR + MR : KR].astype(bf16)
+
+        @pl.when(jnp.logical_not(again))
+        def _():
+            dnear0[...] = near
+            dfar0[...] = far
+
+        @pl.when(again)
+        def _():
+            dnear[...] = near
+            dfar[...] = far
+            pack2(micro, gq_w, gk_w, gv_w, gp_w, gs_w, keep_a, send_a, keep_b, send_b)
 
 
 def att2_back(gh, wp, qe, o, k, v, zc, pc, kall, wskip, w, micro, clips, jobs):
     n = H2 // 2
     ins = [scalar(micro), per_video(gh, n), turn_rows(wp, n, PAIR)]
-    ins += [video_cols(a, n, PAIR) for a in (qe, o, k, v, zc)]
-    ins += [per_video(pc, n), per_video(kall, n), whole(wskip)]
-    ins += [turn_cols(w, n, PAIR, j * n) for j in range(3)]
+    ins += [video_cols(a, n, PAIR) for a in (qe, o, k, v)]
+    ins += [per_video(a, n) for a in (zc, pc, kall)] + [whole(wskip), whole(w)]
     outs = [whole(shape_of((MR, D1), bf16))] * 2 + [per_video(shape_of((2, PR, D1), f32), n)]
     outs += [whole(shape_of((clips,) + folded(D1 // (2 * clips), 3 * D2), bf16))] * 4
     scratch = [VMEM((D1, W2), f32)] * 3 + [VMEM((W2, D2), f32), VMEM((D1, D2), f32)]
-    scratch += [VMEM((KR, D1), f32), VMEM((D1, 3 * D2), f32)] + [VMEM((MR, D1), bf16)] * 2
+    scratch += [VMEM((MR, D1), bf16)] * 2
+    scratch += [VMEM((PR, W2), bf16), VMEM((KR, W2), bf16), VMEM((KR, W2), bf16)]
     flops = 4 * (10 * PR * KR * W2 + 4 * PR * D1 * W2 + 4 * KR * D1 * W2 + 4 * PR * W2 * D2)
-    jobs = [Shift(28, -1, (n - 1, 1), (2 * n - 1, 1)), Shift(29, -2, (n - 1, 1), (2 * n - 1, 1))] + jobs
+    jobs = [Shift(24, -1, (n - 1, 1), (2 * n - 1, 1)), Shift(25, -2, (n - 1, 1), (2 * n - 1, 1))] + jobs
     return call(att2_back_kernel, (2 * n,), ins, outs, scratch, flops=flops, name="block2_attention_back", jobs=jobs, tag=4)
 
 
@@ -896,68 +934,63 @@
 
 
 def att1_back_kernel(
-    micro, qe, gze, k, v, xn, kall, wq, wk, wv, gp,
+    micro, qe, gze, k, v, xn, kall, w, gp,
     dnear, dfar, down, dna, keep_a, send_a, keep_b, send_b,
-    gq_w, gk_w, gv_w, dkv, nat, qkv, dnear0, dfar0,
+    gq_w, gk_w, gv_w, qkv, dnear0, dfar0, gqs, dks, dvs,
 ):
     step = pl.program_id(0)
     turn = step % (H1 // 2)
     again = step >= H1 // 2
-
-    @pl.when(turn == 0)
-    def _():
-        dkv[...] = jnp.zeros_like(dkv)
-        dna[...] = jnp.zeros_like(dna)
-        nat[...] = xn[...].T
-
     gq, dk, dv = [[] for _ in QUERY_TILES], [], []
-    for h in range(2):
-        at = slice(LANE * h, LANE * (h + 1))
-        g = gze[:, at]
-        dqs, dkh, dvh = head_backward(qe[:, at], g, k[:, at], v[:, at], QUERY_TILES)
+    sets = [tuple(r[:, LANE * h : LANE * (h + 1)] for r in (qe, gze, k, v)) for h in range(2)]
+    for (_, g, _, _), (dqs, dkh, dvh) in zip(sets, heads_backward(sets, QUERY_TILES)):
         for i, rows in enumerate(QUERY_TILES):
             gq[i].append((g[rows].astype(f32) + dqs[i]).astype(bf16))
         dk.append(dkh.astype(bf16))
         dv.append(dvh.astype(bf16))
     gq = jnp.concatenate([jnp.concatenate(t, axis=1) for t in gq], axis=0)
     lane = lanes((1, PAIR)) % LANE
-    gq = jnp.where(lane < HD, gq, jnp.zeros_like(gq))
-    dk = jnp.concatenate(dk, axis=1)
-    dv = jnp.concatenate(dv, axis=1)
-    dna[...] += mm_nt(gq, wq[...])
-    dkv[...] += mm_nt(dk, wk[...]) + mm_nt(dv, wv[...])
-    add_columns(gq_w, turn, mm(nat[...], gq), again)
-    add_columns(gk_w, turn, mm_tn(kall[...], dk), again)
-    add_columns(gv_w, turn, mm_tn(kall[...], dv), again)
+    put_columns(gqs, turn, jnp.where(lane < HD, gq, jnp.zeros_like(gq)))
+    put_columns(dks, turn, jnp.concatenate(dk, axis=1))
+    put_columns(dvs, turn, jnp.concatenate(dv, axis=1))
 
     @pl.when(turn == H1 // 2 - 1)
     def _():
-        down[...] = dkv[0:PR, :]
-
-    @pl.when(step == H1 // 2 - 1)
-    def _():
-        dnear0[...] = dkv[PR : PR + MR, :].astype(bf16)
-        dfar0[...] = dkv[PR + MR : KR, :].astype(bf16)
-
-    @pl.when(step == H1 - 1)
-    def _():
-        dnear[...] = dkv[PR : PR + MR, :].astype(bf16)
-        dfar[...] = dkv[PR + MR : KR, :].astype(bf16)
-        pack_att1(micro, gq_w, gk_w, gv_w, gp, keep_a, send_a, keep_b, send_b, qkv)
+        kallt = kall[...].T
+        add_to(gq_w, mm(xn[...].T, gqs[...]), again)
+        add_to(gk_w, mm(kallt, dks[...]), again)
+        add_to(gv_w, mm(kallt, dvs[...]), again)
+        dkv = mm_nt(dks[...], w[:, W1 : 2 * W1]) + mm_nt(dvs[...], w[:, 2 * W1 :])
+        dna[...] = mm_nt(gqs[...], w[:, :W1])
+        down[...] = dkv[0:PR]
+        near = dkv[PR : PR + MR].astype(bf16)
+        far = dkv[PR + MR : KR].astype(bf16)
+
+        @pl.when(jnp.logical_not(again))
+        def _():
+            dnear0[...] = near
+            dfar0[...] = far
+
+        @pl.when(again)
+        def _():
+            dnear[...] = near
+            dfar[...] = far
+            pack_att1(micro, gq_w, gk_w, gv_w, gp, keep_a, send_a, keep_b, send_b, qkv)
 
 
 def att1_back(ozq, gze, k, v, xn, kall, w, gp, micro, clips, jobs):
     n = H1 // 2
     ins = [scalar(micro), video_cols(ozq, n, PAIR, 2 * n)] + [video_cols(a, n, PAIR) for a in (gze, k, v)]
     ins += [(xn, pl.BlockSpec((None, QT, D1), lambda i: (i // n, 0, 1))), per_video(kall, n)]
-    ins += [turn_cols(w, n, PAIR, j * n) for j in range(3)] + [whole(gp)]
+    ins += [whole(w), whole(gp)]
     outs = [whole(shape_of((MR, D1), bf16))] * 2
     outs += [per_video(shape_of((2, PR, D1), f32), n), per_video(shape_of((2, QT, D1), f32), n)]
     outs += [whole(shape_of((clips,) + folded(D1 // (2 * clips), 2 * D1), bf16))] * 4
     scratch = [VMEM((D1, W1), f32)] * 3
-    scratch += [VMEM((KR, D1), f32), VMEM((D1, QT), bf16), VMEM((D1, 4 * D1), f32)] + [VMEM((MR, D1), bf16)] * 2
+    scratch += [VMEM((D1, 4 * D1), f32)] + [VMEM((MR, D1), bf16)] * 2
+    scratch += [VMEM((QT, W1), bf16), VMEM((KR, W1), bf16), VMEM((KR, W1), bf16)]
     flops = 4 * (10 * QT * KR * W1 + 2 * QT * D1 * W1 + 4 * KR * D1 * W1)
-    jobs = [Shift(25, -1, (n - 1, 1), (2 * n - 1, 1)), Shift(26, -2, (n - 1, 1), (2 * n - 1, 1))] + jobs
+    jobs = [Shift(21, -1, (n - 1, 1), (2 * n - 1, 1)), Shift(22, -2, (n - 1, 1), (2 * n - 1, 1))] + jobs
     return call(att1_back_kernel, (2 * n,), ins, outs, scratch, flops=flops, name="block1_attention_back", jobs=jobs, tag=6)
 
 
@@ -993,9 +1026,7 @@
             send[i] = t
 
 
-def pack2(micro, gq, gk, gv, gp, gs, keep_a, send_a, keep_b, send_b, qkv):
-    for j, g in enumerate((gq, gk, gv)):
-        qkv[:, D2 * j : D2 * (j + 1)] = strip(g[...])
+def pack2(micro, gq, gk, gv, gp, gs, keep_a, send_a, keep_b, send_b):
     clips, rows = keep_a.shape[0], D1 // (2 * keep_a.shape[0])
 
     def proj(share, a):
@@ -1008,7 +1039,7 @@
         return jnp.concatenate([gp[start : start + cut, :], gp[LANE * (h + 1) : LANE * (h + 1) + rows - cut, :]], axis=0)
 
     def piece_a(n):
-        return qkv[rows * n : rows * (n + 1), :]
+        return jnp.concatenate([strip(t[rows * n : rows * (n + 1), :]) for t in (gq, gk, gv)], axis=1)
 
     def piece_b(n):
         return jnp.concatenate([proj(n, 0), proj(n, 1), gs[rows * n : rows * (n + 1), :]], axis=1)
@@ -1046,8 +1077,33 @@
     store_shares(micro[0], clips, ((keep_a, send_a, piece_a), (keep_b, send_b, piece_b)))
 
 
-def stack_blocks(v, count):
-    return jnp.concatenate(jnp.split(v, count, axis=1), axis=0)
+def flatten_into(out, v, row=0, column=0, columns=None):
+    rows, cols = v.shape
+    wide_ = (columns or cols) // LANE
+    for j in range(cols // LANE):
+        out[pl.ds(row * wide_ + column // LANE + j, rows, stride=wide_), :] = v[:, LANE * j : LANE * (j + 1)]
+
+
+def lay_out_kernel(rows, left, right, fc1, out1, qkv2, rest2, fc2, out2, *outs):
+    left, right, fc1, out1, qkv2, rest2 = (unfold(v[...], rows) for v in (left, right, fc1, out1, qkv2, rest2))
+    flatten_into(outs[0], left, 0, 0, 3 * D1)
+    flatten_into(outs[0], right[:, :D1], 0, 2 * D1, 3 * D1)
+    flatten_into(outs[1], right[:, D1:])
+    flatten_into(outs[2], fc1)
+    flatten_into(outs[4], qkv2)
+    for a in range(2):
+        flatten_into(outs[5], rest2[:, D2 * a : D2 * (a + 1)], rows * a)
+    flatten_into(outs[6], rest2[:, 2 * D2 :])
+    flatten_into(outs[7], fc2[...])
+    for a in range(4):
+        flatten_into(outs[3], out1[:, D1 * a : D1 * (a + 1)], rows * a)
+        flatten_into(outs[8], out2[:, D2 * a : D2 * (a + 1)], 2 * rows * a)
+
+
+def lay_out(clips, sums):
+    sizes = (3 * D1 * D1, D1 * D1, D1 * F1, D1 * F1, 3 * D1 * D2, D2 * D2, D1 * D2, D2 * F2, D2 * F2)
+    outs = [whole(shape_of((n // (2 * clips * LANE), LANE), f32)) for n in sizes]
+    return call(partial(lay_out_kernel, D1 // (2 * clips)), (1,), [whole(v) for v in sums], outs, name="lay_out")
 
 
 def bit_order(bits, stream):
@@ -1270,8 +1326,6 @@
 def body(inputs, offsets, cotangent, gain_attn1, w_qkv1, w_proj1, gain_mlp1, w_fc1, w_out1,
          gain_attn2, w_qkv2, w_proj2, w_skip, gain_mlp2, w_fc2, w_out2):
     clip = lax.axis_index("clip")
-    gains_in = jnp.stack([gain_attn1, gain_mlp1, gain_attn2])
-    g_m2 = gain_mlp2.reshape(1, -1)
     row = jnp.arange(KR, dtype=jnp.int32)[:, None]
     place = jnp.where(row < PR + MR, row - PR, row - PR - MR)
     later = (place // CELL >= offsets[0]) & (place < MT)
@@ -1287,10 +1341,11 @@
     def flat(results):
         return [r[0] for r in results]
 
-    (xn, kva, mem, w1p, p1p, w2p, p2p), got = front(inputs, gains_in, w_qkv1, w_proj1, w_qkv2, w_proj2)
-    (ka, Ka, Va, ozq, hm, ubgp, pc, mem), got = block1(kva, flat(got), mem[1], kext, xn, w1p, p1p, gains_in, w_fc1, w_out1)
-    (kc, Kc, Vc, qec, oc, zc, hc), _ = block2(pc, flat(got[2:]), mem[1], kext, w2p, w_skip, p2p)
-    output, gh, keep_fc, send_fc, keep_out, send_out, gg_mlp2 = mlp2(micro, clips, hc, cotangent, g_m2, w_fc2, w_out2)
+    gains_in = (gain_attn1, gain_mlp1, gain_attn2, gain_mlp2)
+    (xn, kva, mem, gains_in, w1p, p1p, w2p, p2p), got = front(inputs, gains_in, w_qkv1, w_proj1, w_qkv2, w_proj2)
+    (ka, Ka, Va, ozq, hm, ubgp, pc, mem), got = block1(kva, flat(got), mem, kext, xn, w1p, p1p, gains_in, w_fc1, w_out1)
+    (kc, Kc, Vc, qec, oc, zc, hc), _ = block2(pc, flat(got[2:]), mem, kext, w2p, w_skip, p2p)
+    output, gh, keep_fc, send_fc, keep_out, send_out, gg_mlp2 = mlp2(micro, clips, hc, cotangent, gains_in, w_fc2, w_out2)
 
     orders = [bit_order(bits, i) for i in range(2)]
 
@@ -1310,29 +1365,21 @@
     big, att2 = got[2:4], got[4:]
     mlp1 = [(packed[0], packed[1]), (packed[2], packed[3])]
     n = H1 // 2
-    jobs = chains(att2, [(1, 0), (2, 2)], 2 * n - 1) + chains(mlp1, [(-1, 0), (0, 1), (1, 2)], 2 * n - 1)
+    rest = [(k, 0) for k in range(3, bits)]
+    jobs = chains(big, rest + [(GROUP, 0)], 2 * n - 1)
+    rest = [(k, 2) for k in range(2, bits)]
+    jobs += chains(att2, [(1, 0)] + rest + [(GROUP, 3)], 2 * n - 1)
+    rest = [(k, 3) for k in range(2, bits)]
+    jobs += chains(mlp1, [(-1, 0), (0, 1), (1, 2)] + rest, 2 * n - 1)
     (near1, far1, down, dna, *packed), got = att1_back(ozq, gze, Ka, Va, xn, ka, w1p, gp, micro, clips, jobs)
-    got0, att2, mlp1 = flat(got[:2]), got[2:4], got[4:]
+    got0, big, att2, mlp1 = flat(got[:2]), flat(got[2:4]), flat(got[4:6]), got[6:]
     att1 = [(packed[0], packed[1]), (packed[2], packed[3])]
-    streams = [tuple(p) for p in att1 + mlp1 + att2 + big]
-    starts = [-1, -1, 2, 2, 3, 3, 3, 3]
+    streams = [tuple(p) for p in att1 + mlp1]
+    starts = [-1, -1, bits, bits]
     gx, gains, *sums = finish(
         clips, streams, starts, gg_m, gg_c, gg_mlp2, gains_in, near1, far1, dna, down, xn, gha, got0, 7
     )
-    rows = D1 // (2 * clips)
-    left, right, gw_fc1, gw_out1, gw_qkv2, rest2 = (unfold(v, rows) for v in sums[:6])
-    gw_fc2, gw_out2 = sums[6:]
-    shares = (
-        jnp.concatenate([left, right[:, :D1]], axis=1),
-        right[:, D1:],
-        gw_fc1,
-        stack_blocks(gw_out1, 4),
-        gw_qkv2,
-        stack_blocks(rest2[:, : 2 * D2], 2),
-        rest2[:, 2 * D2 :],
-        gw_fc2,
-        stack_blocks(gw_out2, 4),
-    )
+    shares = lay_out(clips, sums + att2 + big)
     gains = (gains[0], gains[1], gains[2], gains[3:5].reshape(-1))
     return (output, gx.reshape(inputs.shape)) + gains + tuple(v.reshape(-1) for v in shares)
 

time: 379 us -> 360 us (0.950)
  local copies, waits for them, and re-layouts: 21.7 us -> 6.07 us
    pallas_call x1, Pallas kernels: 39.6 us -> 30.3 us  [finish(): pl.pallas_call(partial(finish_kernel, clips, starts), grid=(1,), in_specs...]
    pallas_call x7 -> x8, Pallas kernels: 309 us -> 316 us  [call(): pl.pallas_call(body_, grid=grid, in_specs=[t for _, t in ins], out_specs=...]
    reshape x9 -> x0, local copies, waits for them, and re-layouts: 6.75 us -> none  [the longest x8 5.48 us: body(): v.reshape(-1)]
where the time goes in v5:
time: 360 us; the launch traced here: 356 us
  Pallas kernels  347 us (96%)
  local copies, waits for them, and re-layouts  6.07 us (2%)
    pallas_call x8, Pallas kernels, call(): pl.pallas_call(body_, grid=grid, in_specs=[t for _, t in ins], out_specs=...  316 us
    pallas_call x1, Pallas kernels, finish(): pl.pallas_call(partial(finish_kernel, clips, starts), grid=(1,), in_specs...  30.3 us

profile of v5, /device:TPU:0, one launch (start us, length us, event | category | flops | bytes accessed | tf_op | source)
XLA Modules:
  0.0 355.6 jit_solution(1186803304060206571)
XLA Ops:
  1.3 0.9 broadcast_select_fusion.refs_3_
  2.3 17.4 %first_norm.1 = (bf16[2,1568,768]{2,1,0:T(8,128)(2,1)}, bf16[2,400,384]{2,1,0:T(8,128)(2,1)}, bf16[2,208,384]{2,1,0:T(8,128)(2,1)}, f32[8,384]{1,0:T(8,128)}, bf...) custom-call(bf16[1,2,1,1568,384]{4,3,2,1,0:T(8,128)(2,1)} %refs_0_.1, ...), custom_call_target="tpu_custom_call" | custom-call | flops 1001914368 | bytes 18132480 | tf_op jit(solution)/shard_map/first_norm/pallas_call | solution.py:371
  19.6 59.3 %block1_forward.1 = (bf16[2,816,384]{2,1,0:T(8,128)(2,1)}, bf16[2,816,512]{2,1,0:T(8,128)(2,1)}, bf16[2,816,512]{2,1,0:T(8,128)(2,1)}, bf16[2,1568,1536]{2,1,0:T...) custom-call(bf16[2,400,384]{2,1,0:T(8,128)(2,1)} %get-tuple-element., ...), custom_call_target="tpu_custom_call" | custom-call | flops 20346568704 | bytes 57495552 | tf_op jit(solution)/shard_map/block1_forward/pallas_call | solution.py:371
  79.0 26.4 %block2_attention.1 = (bf16[2,816,384]{2,1,0:T(8,128)(2,1)}, bf16[2,816,1024]{2,1,0:T(8,128)(2,1)}, bf16[2,816,1024]{2,1,0:T(8,128)(2,1)}, bf16[2,400,1024]{2,1,...) custom-call(bf16[2,400,384]{2,1,0:T(8,128)(2,1)} %get-tuple-element.120.refs_0, ...), custom_call_target="tpu_custom_call" | custom-call | flops 10273947648 | bytes 26542080 | tf_op jit(solution)/shard_map/block2_attention/pallas_call | solution.py:371
  105.4 39.9 %block2_mlp.1 = (bf16[1,2,1,392,768]{4,3,2,1,0:T(8,128)(2,1)}, bf16[2,400,768]{2,1,0:T(8,128)(2,1)}, bf16[8,48,3072]{2,1,0:T(8,128)(2,1)}, bf16[8,48,3072]{2,1,0...) custom-call(s32[1]{0:T(128)} %bitcast.refs_0_, ...), custom_call_target="tpu_custom_call" | custom-call | flops 22649241600 | bytes 24984580 | tf_op jit(solution)/shard_map/block2_mlp/pallas_call | solution.py:371
  145.2 51.4 %block2_attention_back.1 = (bf16[208,384]{1,0:T(8,128)(2,1)}, bf16[208,384]{1,0:T(8,128)(2,1)}, f32[2,400,384]{2,1,0:T(8,128)}, bf16[8,16,3456]{2,1,0:T(8,128)(2...) custom-call(s32[1]{0:T(128)} %bitcast.refs_0_, ...), custom_call_target="tpu_custom_call" | custom-call | flops 26052919296 | bytes 38780932 | tf_op jit(solution)/shard_map/block2_attention_back/pallas_call | solution.py:371
  196.6 56.1 %block1_mlp_back.1 = (f32[2,1568,384]{2,1,0:T(8,128)}, bf16[2,1568,512]{2,1,0:T(8,128)(2,1)}, f32[1,384]{1,0:T(1,128)}, f32[1,384]{1,0:T(1,128)}, f32[512,384]{1...) custom-call(s32[1]{0:T(128)} %bitcast.refs_0_, ...), custom_call_target="tpu_custom_call" | custom-call | flops 17263755264 | bytes 65551364 | tf_op jit(solution)/shard_map/block1_mlp_back/pallas_call | solution.py:371
  252.7 63.0 %block1_attention_back.1 = (bf16[208,384]{1,0:T(8,128)(2,1)}, bf16[208,384]{1,0:T(8,128)(2,1)}, f32[2,400,384]{2,1,0:T(8,128)}, f32[2,1568,384]{2,1,0:T(8,128)},...) custom-call(s32[1]{0:T(128)} %bitcast.refs_0_, ...), custom_call_target="tpu_custom_call" | custom-call | flops 31237079040 | bytes 39313412 | tf_op jit(solution)/shard_map/block1_attention_back/pallas_call | solution.py:371
  315.7 30.3 %finish.1 = (bf16[2,1568,384]{2,1,0:T(8,128)(2,1)}, f32[8,384]{1,0:T(8,128)}, f32[16,1152]{1,0:T(8,128)}, f32[16,1152]{1,0:T(8,128)}, f32[16,2304]{1,0:T(8,128)}, /*index=5*/f32[16,2304]{1,0:T(8,128)}) custom-call(bf16[8,16,1152]{2,1,0:T(8,128)(2,1)} %get-tuple-element.172.refs_0_, bf16[8,16,1152]{2,1,0:T(8,128)(2,1)} %get-tuple-element.173.refs_1_, ...), custom_call_target="tpu_custom_call" | custom-call | tf_op jit(solution)/shard_map/finish/pallas_call | solution.py:1312
  346.1 0.7 slice.15
  346.8 1.4 slice_reduce_fusion
  348.2 0.6 reshape.143
  348.8 3.0 lay_out.1
  351.8 3.3 copy.34
  (3 shorter events, 0.0 us)

commit v6 on v5

--- a/solution.py
+++ b/solution.py
@@ -1084,7 +1084,12 @@
         out[pl.ds(row * wide_ + column // LANE + j, rows, stride=wide_), :] = v[:, LANE * j : LANE * (j + 1)]
 
 
-def lay_out_kernel(rows, left, right, fc1, out1, qkv2, rest2, fc2, out2, *outs):
+def lay_out_kernel(rows, left, right, fc1, out1, qkv2, rest2, fc2, out2, gains, gx, *outs):
+    for i in range(3):
+        outs[9 + i][...] = gains[i : i + 1, :].reshape(D1)
+    outs[12][0:D1] = gains[3:4, :].reshape(D1)
+    outs[12][D1:] = gains[4:5, :].reshape(D1)
+    outs[13][...] = gx[...]
     left, right, fc1, out1, qkv2, rest2 = (unfold(v[...], rows) for v in (left, right, fc1, out1, qkv2, rest2))
     flatten_into(outs[0], left, 0, 0, 3 * D1)
     flatten_into(outs[0], right[:, :D1], 0, 2 * D1, 3 * D1)
@@ -1100,10 +1105,11 @@
         flatten_into(outs[8], out2[:, D2 * a : D2 * (a + 1)], 2 * rows * a)
 
 
-def lay_out(clips, sums):
+def lay_out(clips, sums, gains, gx):
     sizes = (3 * D1 * D1, D1 * D1, D1 * F1, D1 * F1, 3 * D1 * D2, D2 * D2, D1 * D2, D2 * F2, D2 * F2)
     outs = [whole(shape_of((n // (2 * clips * LANE), LANE), f32)) for n in sizes]
-    return call(partial(lay_out_kernel, D1 // (2 * clips)), (1,), [whole(v) for v in sums], outs, name="lay_out")
+    outs += [whole(shape_of((n,), f32)) for n in (D1, D1, D1, D2)] + [whole(shape_of(gx.shape, bf16))]
+    return call(partial(lay_out_kernel, D1 // (2 * clips)), (1,), [whole(v) for v in sums + [gains, gx]], outs, name="lay_out")
 
 
 def bit_order(bits, stream):
@@ -1117,13 +1123,13 @@
     count = len(starts)
     keeps, gots = refs[:count], refs[count : 2 * count]
     pos = 2 * count
-    gg_m, gg_c, gg_d, gain, dnear, dfar, dna, down, xn, gha, rn0, rf0 = refs[pos : pos + 12]
+    gg_m, gg_c, gg_d, gain, dnear, dfar, dna_h, down, xn_h, gha_h, rn0, rf0 = refs[pos : pos + 12]
     pos += 12
     gx, gains = refs[pos : pos + 2]
     done = refs[pos + 2 : pos + 2 + count]
     pos += 2 + count
-    ds, gs, rn1, rf1, g_all, g_four = refs[pos : pos + 6]
-    pos += 6
+    dna, xn, gha, ds, gs, rn1, rf1, g_all, g_four = refs[pos : pos + 9]
+    pos += 9
     bits = clips.bit_length() - 1
     land, stage, ends = {}, {}, {}
     for i in range(count):
@@ -1135,7 +1141,15 @@
             pos += 3
         ends[i] = refs[pos : pos + 2]
         pos += 2
-    sem_s, sem_r, gsem_s, gsem_r, fsem_s, fsem_r, msem_s, msem_r = refs[pos:]
+    sem_s, sem_r, gsem_s, gsem_r, fsem_s, fsem_r, msem_s, msem_r, lsem = refs[pos:]
+
+    def loads(b):
+        pairs = ((dna_h.at[b], dna.at[b]), (xn_h.at[b, :, 0:D1], xn.at[b]), (gha_h.at[b], gha.at[b]))
+        return [pltpu.make_async_copy(src, dst, lsem.at[3 * b + i]) for i, (src, dst) in enumerate(pairs)]
+
+    for b in range(2):
+        for load in loads(b):
+            load.start()
 
     g, c, m = (lax.axis_index(a) for a in ("group", "clip", "micro"))
     barrier = pltpu.get_barrier_semaphore()
@@ -1199,6 +1213,8 @@
                 at_stage[i] += 1
 
     def norm_part(b, rn, rf):
+        for load in loads(b):
+            load.wait()
         got = add_up(rn, rf).astype(bf16)
         d = 0.25 * (down[b] + mm_tn(tmean_matrix(), got))
         for s in range(4):
@@ -1293,12 +1309,13 @@
     count = len(streams)
     ins = [whole(k) for k, _ in streams] + [(t, HBM) if n < 0 else whole(t) for (_, t), n in zip(streams, starts)]
     ins += [whole(a) for a in (gg_m, gg_c, gg_d, gain)] + [(dnear, HBM), (dfar, HBM)]
-    ins += [whole(dna), whole(down), (xn, pl.BlockSpec((2, QT, D1), lambda i: (0, 0, 0))), whole(gha)]
+    ins += [(dna, HBM), whole(down), (xn, HBM), (gha, HBM)]
     ins += [whole(a) for a in got0]
     parts = [k.shape[1:] for k, _ in streams]
     outs = [whole(shape_of((2, QT, D1), bf16)), whole(shape_of((8, D1), f32))]
     outs += [whole(shape_of(p, f32)) for p in parts]
-    scratch = [VMEM((QT, D1), f32)] * 2 + [VMEM((MR, D1), bf16)] * 2
+    scratch = [VMEM((2, QT, D1), f32), VMEM((2, QT, D1), bf16), VMEM((2, QT, D1), f32)]
+    scratch += [VMEM((QT, D1), f32)] * 2 + [VMEM((MR, D1), bf16)] * 2
     scratch += [VMEM((clips, 8, D1), f32), VMEM((4, 8, D1), f32)]
     for p, n in zip(parts, starts):
         if n < 0:
@@ -1309,6 +1326,7 @@
     dma = pltpu.SemaphoreType.DMA
     for n in (count * (bits + 2), clips - 1, 3, 2):
         scratch += [dma((n,))] * 2
+    scratch.append(dma((6,)))
     return pl.pallas_call(
         partial(finish_kernel, clips, starts),
         grid=(1,),
@@ -1367,8 +1385,8 @@
     n = H1 // 2
     rest = [(k, 0) for k in range(3, bits)]
     jobs = chains(big, rest + [(GROUP, 0)], 2 * n - 1)
-    rest = [(k, 2) for k in range(2, bits)]
-    jobs += chains(att2, [(1, 0)] + rest + [(GROUP, 3)], 2 * n - 1)
+    rest = [(k, 1) for k in range(2, bits)]
+    jobs += chains(att2, [(1, 0)] + rest + [(GROUP, 2)], 2 * n - 1)
     rest = [(k, 3) for k in range(2, bits)]
     jobs += chains(mlp1, [(-1, 0), (0, 1), (1, 2)] + rest, 2 * n - 1)
     (near1, far1, down, dna, *packed), got = att1_back(ozq, gze, Ka, Va, xn, ka, w1p, gp, micro, clips, jobs)
@@ -1379,9 +1397,8 @@
     gx, gains, *sums = finish(
         clips, streams, starts, gg_m, gg_c, gg_mlp2, gains_in, near1, far1, dna, down, xn, gha, got0, 7
     )
-    shares = lay_out(clips, sums + att2 + big)
-    gains = (gains[0], gains[1], gains[2], gains[3:5].reshape(-1))
-    return (output, gx.reshape(inputs.shape)) + gains + tuple(v.reshape(-1) for v in shares)
+    *shares, ga, gb, gc, gd, gx = lay_out(clips, sums + att2 + big, gains, gx)
+    return (output, gx.reshape(inputs.shape), ga, gb, gc, gd) + tuple(v.reshape(-1) for v in shares)
 
 
 def solution(mesh):

time: 360 us -> 343 us (0.953)
  Pallas kernels: 347 us -> 336 us
  local copies, waits for them, and re-layouts: 6.07 us -> 0 us
    pallas_call x8, Pallas kernels: 316 us -> 307 us  [call(): pl.pallas_call(body_, grid=grid, in_specs=[t for _, t in ins], out_specs=...]
where the time goes in v6:
time: 343 us; the launch traced here: 339 us
  Pallas kernels  336 us (98%)
    pallas_call x8, Pallas kernels, call(): pl.pallas_call(body_, grid=grid, in_specs=[t for _, t in ins], out_specs=...  307 us
    pallas_call x1, Pallas kernels, finish(): pl.pallas_call(partial(finish_kernel, clips, starts), grid=(1,), in_specs...  29 us

profile of v6, /device:TPU:0, one launch (start us, length us, event | category | flops | bytes accessed | tf_op | source)
XLA Modules:
  0.0 339.1 jit_solution(6000370184457038448)
XLA Ops:
  1.3 0.9 broadcast_select_fusion.refs_3_
  2.3 17.3 %first_norm.1 = (bf16[2,1568,768]{2,1,0:T(8,128)(2,1)}, bf16[2,400,384]{2,1,0:T(8,128)(2,1)}, bf16[2,208,384]{2,1,0:T(8,128)(2,1)}, f32[8,384]{1,0:T(8,128)}, bf...) custom-call(bf16[1,2,1,1568,384]{4,3,2,1,0:T(8,128)(2,1)} %refs_0_.1, ...), custom_call_target="tpu_custom_call" | custom-call | flops 1001914368 | bytes 18132480 | tf_op jit(solution)/shard_map/first_norm/pallas_call | solution.py:371
  19.6 59.3 %block1_forward.1 = (bf16[2,816,384]{2,1,0:T(8,128)(2,1)}, bf16[2,816,512]{2,1,0:T(8,128)(2,1)}, bf16[2,816,512]{2,1,0:T(8,128)(2,1)}, bf16[2,1568,1536]{2,1,0:T...) custom-call(bf16[2,400,384]{2,1,0:T(8,128)(2,1)} %get-tuple-element., ...), custom_call_target="tpu_custom_call" | custom-call | flops 20346568704 | bytes 57495552 | tf_op jit(solution)/shard_map/block1_forward/pallas_call | solution.py:371
  78.9 26.4 %block2_attention.1 = (bf16[2,816,384]{2,1,0:T(8,128)(2,1)}, bf16[2,816,1024]{2,1,0:T(8,128)(2,1)}, bf16[2,816,1024]{2,1,0:T(8,128)(2,1)}, bf16[2,400,1024]{2,1,...) custom-call(bf16[2,400,384]{2,1,0:T(8,128)(2,1)} %get-tuple-element.125.refs_0, ...), custom_call_target="tpu_custom_call" | custom-call | flops 10273947648 | bytes 26542080 | tf_op jit(solution)/shard_map/block2_attention/pallas_call | solution.py:371
  105.3 39.9 %block2_mlp.1 = (bf16[1,2,1,392,768]{4,3,2,1,0:T(8,128)(2,1)}, bf16[2,400,768]{2,1,0:T(8,128)(2,1)}, bf16[8,48,3072]{2,1,0:T(8,128)(2,1)}, bf16[8,48,3072]{2,1,0...) custom-call(s32[1]{0:T(128)} %bitcast.refs_0_, ...), custom_call_target="tpu_custom_call" | custom-call | flops 22649241600 | bytes 24984580 | tf_op jit(solution)/shard_map/block2_mlp/pallas_call | solution.py:371
  145.2 51.4 %block2_attention_back.1 = (bf16[208,384]{1,0:T(8,128)(2,1)}, bf16[208,384]{1,0:T(8,128)(2,1)}, f32[2,400,384]{2,1,0:T(8,128)}, bf16[8,16,3456]{2,1,0:T(8,128)(2...) custom-call(s32[1]{0:T(128)} %bitcast.refs_0_, ...), custom_call_target="tpu_custom_call" | custom-call | flops 26052919296 | bytes 38780932 | tf_op jit(solution)/shard_map/block2_attention_back/pallas_call | solution.py:371
  196.6 56.1 %block1_mlp_back.1 = (f32[2,1568,384]{2,1,0:T(8,128)}, bf16[2,1568,512]{2,1,0:T(8,128)(2,1)}, f32[1,384]{1,0:T(1,128)}, f32[1,384]{1,0:T(1,128)}, f32[512,384]{1...) custom-call(s32[1]{0:T(128)} %bitcast.refs_0_, ...), custom_call_target="tpu_custom_call" | custom-call | flops 17263755264 | bytes 65551364 | tf_op jit(solution)/shard_map/block1_mlp_back/pallas_call | solution.py:371
  252.7 52.0 %block1_attention_back.1 = (bf16[208,384]{1,0:T(8,128)(2,1)}, bf16[208,384]{1,0:T(8,128)(2,1)}, f32[2,400,384]{2,1,0:T(8,128)}, f32[2,1568,384]{2,1,0:T(8,128)},...) custom-call(s32[1]{0:T(128)} %bitcast.refs_0_, ...), custom_call_target="tpu_custom_call" | custom-call | flops 31237079040 | bytes 39313412 | tf_op jit(solution)/shard_map/block1_attention_back/pallas_call | solution.py:371
  304.7 29.0 %finish.1 = (bf16[2,1568,384]{2,1,0:T(8,128)(2,1)}, f32[8,384]{1,0:T(8,128)}, f32[16,1152]{1,0:T(8,128)}, f32[16,1152]{1,0:T(8,128)}, f32[16,2304]{1,0:T(8,128)}, /*index=5*/f32[16,2304]{1,0:T(8,128)}) custom-call(bf16[8,16,1152]{2,1,0:T(8,128)(2,1)} %get-tuple-element.177.refs_0_, bf16[8,16,1152]{2,1,0:T(8,128)(2,1)} %get-tuple-element.178.refs_1_, ...), custom_call_target="tpu_custom_call" | custom-call | tf_op jit(solution)/shard_map/finish/pallas_call | solution.py:1330
  333.7 4.9 %lay_out.1 = (f32[216,128]{1,0:T(8,128)}, f32[72,128]{1,0:T(8,128)}, f32[288,128]{1,0:T(8,128)}, f32[288,128]{1,0:T(8,128)}, f32[432,128]{1,0:T(8,128)}, /*index...) custom-call(f32[16,1152]{1,0:T(8,128)} %get-tuple-element.195.refs_0, ...), custom_call_target="tpu_custom_call" | custom-call | bytes 8965632 | tf_op jit(solution)/shard_map/lay_out/pallas_call | solution.py:371
  (3 shorter events, 0.0 us)
